TPU v7x, 128 devices: a whole 4x4x4 slice. The times are simulated.
128 devices in a mesh: seq: 4 (over x_hi, core), fsdp: 32 (over z, x_lo, y).
Axes of the slice: x: 4 (x_hi: 2, x_lo: 2; x = x_hi * 2 + x_lo), y: 4, z: 4, core: 2. Of those that a mesh axis runs over, the one named last changes fastest.
Arguments:
- tokens: bfloat16 [32, 1024, 768], P('fsdp', 'seq'), may hold values from -6 to 6
- image_ids: int32 [32, 1024], P('fsdp'), may hold values from 0 to 1, as said below
- cotangent: bfloat16 [32, 1024, 768], P('fsdp', 'seq'), may hold values from -6 to 6
- attn_norm_gain: bfloat16 [2, 768], P(None, 'fsdp'), may hold values from 0.25 to 1.75
- attn_norm_bias: bfloat16 [2, 768], P(None, 'fsdp'), may hold values from -1 to 1
- qkv_weight: bfloat16 [2, 768, 2304], P(None, 'fsdp'), may hold values from -0.21875 to 0.21875
- query_bias: bfloat16 [2, 768], P(None, 'fsdp'), may hold values from -1.5 to 1.5
- value_bias: bfloat16 [2, 768], P(None, 'fsdp'), may hold values from -0.25 to 0.25
- proj_weight: bfloat16 [2, 768, 768], P(None, 'fsdp'), may hold values from -1.75 to 1.75
- proj_bias: bfloat16 [2, 768], P(None, 'fsdp'), may hold values from -1 to 1
- mlp_norm_gain: bfloat16 [2, 768], P(None, 'fsdp'), may hold values from 0.25 to 1.75
- mlp_norm_bias: bfloat16 [2, 768], P(None, 'fsdp'), may hold values from -1 to 1
- fc_in_weight: bfloat16 [2, 768, 3072], P(None, 'fsdp'), may hold values from -0.21875 to 0.21875
- fc_in_bias: bfloat16 [2, 3072], P(None, 'fsdp'), may hold values from -2.5 to 2.5
- fc_out_weight: bfloat16 [2, 3072, 768], P(None, 'fsdp'), may hold values from -0.109375 to 0.109375
- fc_out_bias: bfloat16 [2, 768], P(None, 'fsdp'), may hold values from -1 to 1
Outputs:
- block_output: bfloat16 [32, 1024, 768], P('fsdp', 'seq')
- tokens_grad: float32 [32, 1024, 768], P('fsdp', 'seq')
- attn_norm_gain_grad: float32 [2, 768], P(None, 'fsdp')
- attn_norm_bias_grad: float32 [2, 768], P(None, 'fsdp')
- qkv_weight_grad: float32 [2, 768, 2304], P(None, 'fsdp')
- query_bias_grad: float32 [2, 768], P(None, 'fsdp')
- value_bias_grad: float32 [2, 768], P(None, 'fsdp')
- proj_weight_grad: float32 [2, 768, 768], P(None, 'fsdp')
- proj_bias_grad: float32 [2, 768], P(None, 'fsdp')
- mlp_norm_gain_grad: float32 [2, 768], P(None, 'fsdp')
- mlp_norm_bias_grad: float32 [2, 768], P(None, 'fsdp')
- fc_in_weight_grad: float32 [2, 768, 3072], P(None, 'fsdp')
- fc_in_bias_grad: float32 [2, 3072], P(None, 'fsdp')
- fc_out_weight_grad: float32 [2, 3072, 768], P(None, 'fsdp')
- fc_out_bias_grad: float32 [2, 768], P(None, 'fsdp')
Inputs may be any that keep to these rules, and one draw needn't show every extreme that they name: `image_ids`: each sequence holds one image: a run of 785 tokens with id 0 that starts at one of its first 240 positions; every other token of the sequence is padding with id 1. A token attends to the tokens of its own sequence that carry its id.
All inputs are finite; a program needn't handle non-finite values.
Results may differ from a plain program's by a relative error of at most 0.023.
Values may be sent and summed in bfloat16 or wider, within the bound.
No kernel may reach another device: no remote copies, remote signals or barrier semaphores. Data moves between devices by JAX's collectives and lax.ppermute only.
A program may use at most 256 MiB of HBM per device.

v0:
```python
import jax
import jax.numpy as jnp
from jax import lax
from jax.sharding import PartitionSpec as P

HD = 64


def shortened(x):
    return jax.tree.map(lambda a: a.astype(jnp.bfloat16) if a.dtype == jnp.float32 else a, x)


def layer_norm(values, gain_row, bias_row):
    centre = jnp.mean(values, -1, keepdims=True)
    centred = values - centre
    spread = jnp.mean(centred * centred, -1, keepdims=True)
    return centred * lax.rsqrt(spread + 1e-06) * gain_row + bias_row


def gelu_exact(values):
    return jax.nn.gelu(values, approximate=False)


def split_heads(block_data):
    return block_data.reshape(block_data.shape[0], block_data.shape[1] // HD, HD)


def attend_forward(packed):
    queries, key_rows, value_rows, labels = packed
    seq_length = queries.shape[0]
    score_scale = HD ** (-0.5)
    q_heads = split_heads(queries)
    k_heads = split_heads(key_rows)
    v_heads = split_heads(value_rows)
    block_rows = min(512, seq_length)
    outputs = []
    log_totals = []
    for begin_row in range(0, seq_length, block_rows):
        q_block = q_heads[begin_row : begin_row + block_rows]
        scores = (
            jnp.einsum("qge,kge->gqk", q_block, k_heads, preferred_element_type=jnp.float32)
            * score_scale
        )
        allowed = labels[begin_row : begin_row + block_rows, None] == labels[None, :]
        scores = jnp.where(allowed[None], scores, -1e30)
        row_peak = jnp.max(scores, -1, keepdims=True)
        expons = jnp.exp(scores - row_peak)
        row_total = jnp.sum(expons, -1, keepdims=True)
        probabilities = (expons / row_total).astype(jnp.bfloat16)
        attended = jnp.einsum(
            "gqk,kge->qge", probabilities, v_heads, preferred_element_type=jnp.float32
        )
        outputs.append(attended.astype(jnp.bfloat16))
        log_totals.append(row_peak[..., 0] + jnp.log(row_total[..., 0]))
    joined = jnp.concatenate(outputs, 0).reshape(seq_length, -1)
    return (joined, jnp.concatenate(log_totals, 1))


def attend_backward(packed):
    queries, key_rows, value_rows, labels, log_total, grad_out = packed
    seq_length = queries.shape[0]
    score_scale = HD ** (-0.5)
    q_heads = split_heads(queries)
    k_heads = split_heads(key_rows)
    v_heads = split_heads(value_rows)
    g_heads = split_heads(grad_out)
    block_rows = min(512, seq_length)
    grad_keys = jnp.zeros(k_heads.shape, jnp.float32)
    grad_values = jnp.zeros(v_heads.shape, jnp.float32)
    grad_queries = []
    for begin_row in range(0, seq_length, block_rows):
        q_block = q_heads[begin_row : begin_row + block_rows]
        g_block = g_heads[begin_row : begin_row + block_rows]
        scores = (
            jnp.einsum("qge,kge->gqk", q_block, k_heads, preferred_element_type=jnp.float32)
            * score_scale
        )
        allowed = labels[begin_row : begin_row + block_rows, None] == labels[None, :]
        scores = jnp.where(allowed[None], scores, -1e30)
        probabilities = jnp.exp(scores - log_total[:, begin_row : begin_row + block_rows, None])
        grad_values = grad_values + jnp.einsum(
            "gqk,qge->kge",
            probabilities.astype(jnp.bfloat16),
            g_block,
            preferred_element_type=jnp.float32,
        )
        grad_probs = jnp.einsum(
            "qge,kge->gqk", g_block, v_heads, preferred_element_type=jnp.float32
        )
        inner = jnp.sum(grad_probs * probabilities, -1, keepdims=True)
        grad_scores = (probabilities * (grad_probs - inner)).astype(jnp.bfloat16)
        grad_queries.append(
            jnp.einsum("gqk,kge->qge", grad_scores, k_heads, preferred_element_type=jnp.float32)
            * score_scale
        )
        grad_keys = (
            grad_keys
            + jnp.einsum("gqk,qge->kge", grad_scores, q_block, preferred_element_type=jnp.float32)
            * score_scale
        )
    query_part = jnp.concatenate(grad_queries, 0).reshape(seq_length, -1).astype(jnp.bfloat16)
    return (
        query_part,
        grad_keys.reshape(seq_length, -1).astype(jnp.bfloat16),
        grad_values.reshape(seq_length, -1).astype(jnp.bfloat16),
    )


def gather_layer(shards, layer_index):
    return (
        lax.all_gather(shards[0][layer_index], "fsdp", axis=0, tiled=True),
        lax.all_gather(shards[1][layer_index], "fsdp", axis=0, tiled=True),
        lax.all_gather(shards[2][layer_index], "fsdp", axis=0, tiled=True),
        lax.all_gather(shards[3][layer_index], "fsdp", axis=0, tiled=True),
        lax.all_gather(shards[4][layer_index], "fsdp", axis=0, tiled=True),
        lax.all_gather(shards[5][layer_index], "fsdp", axis=0, tiled=True),
        lax.all_gather(shards[6][layer_index], "fsdp", axis=0, tiled=True),
        lax.all_gather(shards[7][layer_index], "fsdp", axis=0, tiled=True),
        lax.all_gather(shards[8][layer_index], "fsdp", axis=0, tiled=True),
        lax.all_gather(shards[9][layer_index], "fsdp", axis=0, tiled=True),
        lax.all_gather(shards[10][layer_index], "fsdp", axis=0, tiled=True),
        lax.all_gather(shards[11][layer_index], "fsdp", axis=0, tiled=True),
        lax.all_gather(shards[12][layer_index], "fsdp", axis=0, tiled=True),
    )


def regather_layer(shards, layer_index):
    return (
        lax.all_gather(shards[0][layer_index], "fsdp", axis=0, tiled=True),
        lax.all_gather(shards[1][layer_index], "fsdp", axis=0, tiled=True),
        lax.all_gather(shards[2][layer_index], "fsdp", axis=0, tiled=True),
        lax.all_gather(shards[3][layer_index], "fsdp", axis=0, tiled=True),
        lax.all_gather(shards[4][layer_index], "fsdp", axis=0, tiled=True),
        lax.all_gather(shards[5][layer_index], "fsdp", axis=0, tiled=True),
        lax.all_gather(shards[6][layer_index], "fsdp", axis=0, tiled=True),
        lax.all_gather(shards[7][layer_index], "fsdp", axis=0, tiled=True),
        lax.all_gather(shards[8][layer_index], "fsdp", axis=0, tiled=True),
        lax.all_gather(shards[9][layer_index], "fsdp", axis=0, tiled=True),
        lax.all_gather(shards[10][layer_index], "fsdp", axis=0, tiled=True),
        lax.all_gather(shards[11][layer_index], "fsdp", axis=0, tiled=True),
        lax.all_gather(shards[12][layer_index], "fsdp", axis=0, tiled=True),
    )


def forward_layer(residual, layer_set, image_ids, batch_size):
    (
        norm_gain,
        norm_bias,
        qkv_full,
        q_bias,
        v_bias,
        proj_full,
        proj_shift,
        mlp_gain,
        mlp_bias,
        in_full,
        in_shift,
        out_full,
        out_shift,
    ) = layer_set
    model_width = residual.shape[1]
    attn_in = layer_norm(residual, norm_gain, norm_bias).astype(jnp.bfloat16)
    projected = jnp.dot(attn_in, qkv_full, preferred_element_type=jnp.float32)
    queries = (
        (projected[:, :model_width] + q_bias)
        .astype(jnp.bfloat16)
        .reshape(batch_size, -1, model_width)
    )
    key_rows = (
        projected[:, model_width : 2 * model_width]
        .astype(jnp.bfloat16)
        .reshape(batch_size, -1, model_width)
    )
    value_rows = (
        (projected[:, 2 * model_width :] + v_bias)
        .astype(jnp.bfloat16)
        .reshape(batch_size, -1, model_width)
    )
    q_heads, k_heads, v_heads = (
        lax.all_to_all(queries, "seq", split_axis=2, concat_axis=1, tiled=True),
        lax.all_to_all(key_rows, "seq", split_axis=2, concat_axis=1, tiled=True),
        lax.all_to_all(value_rows, "seq", split_axis=2, concat_axis=1, tiled=True),
    )
    attended, log_total = lax.map(attend_forward, (q_heads, k_heads, v_heads, image_ids))
    tok_out = (
        lax.all_to_all(shortened(attended), "seq", split_axis=1, concat_axis=2, tiled=True)
        .astype(attended.dtype)
        .reshape(-1, model_width)
    )
    middle = residual + (
        jnp.dot(tok_out, proj_full, preferred_element_type=jnp.float32) + proj_shift
    )
    mlp_in = layer_norm(middle, mlp_gain, mlp_bias).astype(jnp.bfloat16)
    hidden_pre = jnp.dot(mlp_in, in_full, preferred_element_type=jnp.float32) + in_shift
    hidden = gelu_exact(hidden_pre).astype(jnp.bfloat16)
    result = middle + (jnp.dot(hidden, out_full, preferred_element_type=jnp.float32) + out_shift)
    return (result, (residual, q_heads, k_heads, v_heads, log_total, tok_out, middle, hidden_pre))


def backward_layer(grad_stream, layer_set, saved_state, image_ids, batch_size):
    (
        norm_gain,
        norm_bias,
        qkv_full,
        q_bias,
        v_bias,
        proj_full,
        proj_shift,
        mlp_gain,
        mlp_bias,
        in_full,
        in_shift,
        out_full,
        out_shift,
    ) = layer_set
    residual, q_heads, k_heads, v_heads, log_total, tok_out, middle, hidden_pre = saved_state
    model_width = residual.shape[1]
    grad_branch = grad_stream.astype(jnp.bfloat16)
    out_shift_grad = jnp.sum(grad_branch, 0, dtype=jnp.float32)
    hidden_full, gelu_pull = jax.vjp(gelu_exact, hidden_pre)
    hidden = hidden_full.astype(jnp.bfloat16)
    out_full_grad = jnp.einsum("rf,rd->fd", hidden, grad_branch, preferred_element_type=jnp.float32)
    grad_hidden = jnp.einsum("rd,fd->rf", grad_branch, out_full, preferred_element_type=jnp.float32)
    grad_pre = gelu_pull(grad_hidden)[0].astype(jnp.bfloat16)
    in_shift_grad = jnp.sum(grad_pre, 0, dtype=jnp.float32)
    mlp_normed, mlp_pull = jax.vjp(layer_norm, middle, mlp_gain, mlp_bias)
    mlp_in = mlp_normed.astype(jnp.bfloat16)
    in_full_grad = jnp.einsum("rd,rf->df", mlp_in, grad_pre, preferred_element_type=jnp.float32)
    grad_mlp_in = jnp.einsum("rf,df->rd", grad_pre, in_full, preferred_element_type=jnp.float32)
    grad_middle_norm, mlp_gain_grad, mlp_bias_grad = mlp_pull(grad_mlp_in)
    grad_middle = grad_stream + grad_middle_norm
    grad_attn = grad_middle.astype(jnp.bfloat16)
    proj_shift_grad = jnp.sum(grad_attn, 0, dtype=jnp.float32)
    proj_full_grad = jnp.einsum("rd,re->de", tok_out, grad_attn, preferred_element_type=jnp.float32)
    grad_tok = jnp.einsum("re,de->rd", grad_attn, proj_full, preferred_element_type=jnp.float32)
    grad_tok = grad_tok.astype(jnp.bfloat16).reshape(batch_size, -1, model_width)
    grad_heads = lax.all_to_all(grad_tok, "seq", split_axis=2, concat_axis=1, tiled=True)
    head_query, head_key, head_value = lax.map(
        attend_backward, (q_heads, k_heads, v_heads, image_ids, log_total, grad_heads)
    )
    grad_query, grad_key, grad_value = (
        lax.all_to_all(head_query, "seq", split_axis=1, concat_axis=2, tiled=True),
        lax.all_to_all(head_key, "seq", split_axis=1, concat_axis=2, tiled=True),
        lax.all_to_all(head_value, "seq", split_axis=1, concat_axis=2, tiled=True),
    )
    grad_query = grad_query.reshape(-1, model_width)
    grad_key = grad_key.reshape(-1, model_width)
    grad_value = grad_value.reshape(-1, model_width)
    q_bias_grad = jnp.sum(grad_query, 0, dtype=jnp.float32)
    v_bias_grad = jnp.sum(grad_value, 0, dtype=jnp.float32)
    grad_projected = jnp.concatenate([grad_query, grad_key, grad_value], 1)
    attn_normed, attn_pull = jax.vjp(layer_norm, residual, norm_gain, norm_bias)
    attn_in = attn_normed.astype(jnp.bfloat16)
    qkv_full_grad = jnp.einsum(
        "rd,rc->dc", attn_in, grad_projected, preferred_element_type=jnp.float32
    )
    grad_attn_in = jnp.einsum(
        "rc,dc->rd", grad_projected, qkv_full, preferred_element_type=jnp.float32
    )
    grad_res_norm, norm_gain_grad, norm_bias_grad = attn_pull(grad_attn_in)
    layer_grads = (
        norm_gain_grad,
        norm_bias_grad,
        qkv_full_grad,
        q_bias_grad,
        v_bias_grad,
        proj_full_grad,
        proj_shift_grad,
        mlp_gain_grad,
        mlp_bias_grad,
        in_full_grad,
        in_shift_grad,
        out_full_grad,
        out_shift_grad,
    )
    return (grad_middle + grad_res_norm, layer_grads)


def reduce_grads(grads):
    parts = (
        lax.psum_scatter(grads[0], "fsdp", scatter_dimension=0, tiled=True).astype(jnp.float32),
        lax.psum_scatter(grads[1], "fsdp", scatter_dimension=0, tiled=True).astype(jnp.float32),
        lax.psum_scatter(
            grads[2].astype(jnp.bfloat16), "fsdp", scatter_dimension=0, tiled=True
        ).astype(jnp.float32),
        lax.psum_scatter(
            grads[3].astype(jnp.bfloat16), "fsdp", scatter_dimension=0, tiled=True
        ).astype(jnp.float32),
        lax.psum_scatter(
            grads[4].astype(jnp.bfloat16), "fsdp", scatter_dimension=0, tiled=True
        ).astype(jnp.float32),
        lax.psum_scatter(
            grads[5].astype(jnp.bfloat16), "fsdp", scatter_dimension=0, tiled=True
        ).astype(jnp.float32),
        lax.psum_scatter(
            grads[6].astype(jnp.bfloat16), "fsdp", scatter_dimension=0, tiled=True
        ).astype(jnp.float32),
        lax.psum_scatter(grads[7], "fsdp", scatter_dimension=0, tiled=True).astype(jnp.float32),
        lax.psum_scatter(grads[8], "fsdp", scatter_dimension=0, tiled=True).astype(jnp.float32),
        lax.psum_scatter(
            grads[9].astype(jnp.bfloat16), "fsdp", scatter_dimension=0, tiled=True
        ).astype(jnp.float32),
        lax.psum_scatter(
            grads[10].astype(jnp.bfloat16), "fsdp", scatter_dimension=0, tiled=True
        ).astype(jnp.float32),
        lax.psum_scatter(
            grads[11].astype(jnp.bfloat16), "fsdp", scatter_dimension=0, tiled=True
        ).astype(jnp.float32),
        lax.psum_scatter(
            grads[12].astype(jnp.bfloat16), "fsdp", scatter_dimension=0, tiled=True
        ).astype(jnp.float32),
    )
    return (
        lax.psum(parts[0].astype(jnp.bfloat16), "seq").astype(jnp.float32),
        lax.psum(parts[1].astype(jnp.bfloat16), "seq").astype(jnp.float32),
        lax.psum(parts[2].astype(jnp.bfloat16), "seq").astype(jnp.float32),
        lax.psum(parts[3].astype(jnp.bfloat16), "seq").astype(jnp.float32),
        lax.psum(parts[4].astype(jnp.bfloat16), "seq").astype(jnp.float32),
        lax.psum(parts[5].astype(jnp.bfloat16), "seq").astype(jnp.float32),
        lax.psum(parts[6].astype(jnp.bfloat16), "seq").astype(jnp.float32),
        lax.psum(parts[7].astype(jnp.bfloat16), "seq").astype(jnp.float32),
        lax.psum(parts[8].astype(jnp.bfloat16), "seq").astype(jnp.float32),
        lax.psum(parts[9].astype(jnp.bfloat16), "seq").astype(jnp.float32),
        lax.psum(parts[10].astype(jnp.bfloat16), "seq").astype(jnp.float32),
        lax.psum(parts[11].astype(jnp.bfloat16), "seq").astype(jnp.float32),
        lax.psum(parts[12].astype(jnp.bfloat16), "seq").astype(jnp.float32),
    )


def body(
    tokens,
    image_ids,
    cotangent,
    attn_norm_gain,
    attn_norm_bias,
    qkv_weight,
    query_bias,
    value_bias,
    proj_weight,
    proj_bias,
    mlp_norm_gain,
    mlp_norm_bias,
    fc_in_weight,
    fc_in_bias,
    fc_out_weight,
    fc_out_bias,
):
    shards = (
        attn_norm_gain,
        attn_norm_bias,
        qkv_weight,
        query_bias,
        value_bias,
        proj_weight,
        proj_bias,
        mlp_norm_gain,
        mlp_norm_bias,
        fc_in_weight,
        fc_in_bias,
        fc_out_weight,
        fc_out_bias,
    )
    layer_count = qkv_weight.shape[0]
    batch_size = tokens.shape[0]
    model_width = tokens.shape[2]
    residual = tokens.astype(jnp.float32).reshape(-1, model_width)
    stored = []
    fetched = []
    for layer_index in range(layer_count):
        layer_set = gather_layer(shards, layer_index)
        residual, saved_state = forward_layer(residual, layer_set, image_ids, batch_size)
        stored.append(saved_state)
        fetched.append(layer_set)
    block_output = residual.astype(jnp.bfloat16).reshape(tokens.shape)
    grad_stream = cotangent.astype(jnp.float32).reshape(-1, model_width)
    reduced = [None] * layer_count
    for layer_index in reversed(range(layer_count)):
        layer_set = regather_layer(shards, layer_index)
        grad_stream, layer_grads = backward_layer(
            grad_stream, layer_set, stored[layer_index], image_ids, batch_size
        )
        reduced[layer_index] = reduce_grads(layer_grads)
    stacked = tuple(
        (
            jnp.stack([reduced[layer_index][member_index] for layer_index in range(layer_count)])
            for member_index in range(13)
        )
    )
    return (
        block_output,
        grad_stream.reshape(tokens.shape),
        stacked[0],
        stacked[1],
        stacked[2],
        stacked[3],
        stacked[4],
        stacked[5],
        stacked[6],
        stacked[7],
        stacked[8],
        stacked[9],
        stacked[10],
        stacked[11],
        stacked[12],
    )


def solution(mesh):
    return jax.shard_map(
        body,
        mesh=mesh,
        in_specs=(
            P("fsdp", "seq", None),
            P("fsdp", None),
            P("fsdp", "seq", None),
            P(None, "fsdp"),
            P(None, "fsdp"),
            P(None, "fsdp", None),
            P(None, "fsdp"),
            P(None, "fsdp"),
            P(None, "fsdp", None),
            P(None, "fsdp"),
            P(None, "fsdp"),
            P(None, "fsdp"),
            P(None, "fsdp", None),
            P(None, "fsdp"),
            P(None, "fsdp", None),
            P(None, "fsdp"),
        ),
        out_specs=(
            P("fsdp", "seq", None),
            P("fsdp", "seq", None),
            P(None, "fsdp"),
            P(None, "fsdp"),
            P(None, "fsdp", None),
            P(None, "fsdp"),
            P(None, "fsdp"),
            P(None, "fsdp", None),
            P(None, "fsdp"),
            P(None, "fsdp"),
            P(None, "fsdp"),
            P(None, "fsdp", None),
            P(None, "fsdp"),
            P(None, "fsdp", None),
            P(None, "fsdp"),
        ),
        check_vma=False,
    )
```

profile of v0, /device:TPU:1, one launch (start us, length us, event | category | flops | bytes accessed | tf_op | source)
XLA Modules:
  0.0 2812.8 jit_solution(9834910995193917683)
XLA Ops:
  42.8 135.2 %all-reduce.37 = (bf16[768]{0:T(1024)(128)(2,1)S(1)}, bf16[768]{0:T(1024)(128)(2,1)S(1)}, bf16[768]{0:T(1024)(128)(2,1)S(1)}, bf16[768]{0:T(1024)(128)(2,1)S(1)}...) all-reduce(bf16[768]{0:T(1024)(128)(2,1)S(1)} %dynamic-update-slice, ...), channel_id=3, replica_groups=mesh['seq'=4,'fsdp'=32] {'fsdp'}, use_global_device_ids=true, to_apply=%add.1 | all-reduce | flops 17664 | bytes 70656
  192.1 30.6 %all-to-all-start.1 = ((bf16[4,2,24576]{2,1,0:T(2,128)(2,1)}), bf16[4,2,24576]{2,1,0:T(2,128)(2,1)}, u32[]{:S(2)}, u32[]{:S(2)}) async-start(bf16[4,2,24576]{2,1,0:T(2,128)(2,1)} %reshape.701), calls=%async_computation.1 | async-start | bytes 786432 | tf_op jit(solution)/shard_map/all_to_all | solution.py:180
  283.6 7.6 all-to-all-done.3
  295.9 7.3 all-gather.37.cloned.1.call-done
  305.4 161.5 %all-gather.39.cloned.1.call-done = bf16[1,768,3072]{2,1,0:T(8,128)(2,1)} async-done(((bf16[1,24,3072]{2,1,0:T(8,128)(2,1)}), bf16[1,768,3072]{2,1,0:T(8,128)(2,1)}) %all-gather.39.cloned.1.call-update) | async-done | bytes 4718608 | tf_op jit(solution)/shard_map/all_gather | solution.py:120
  466.8 11.7 multiply_convert_fusion.5
  478.5 148.1 %all-gather.41.cloned.1.call-done = bf16[1,3072,768]{2,1,0:T(8,128)(2,1)} async-done(((bf16[1,96,768]{2,1,0:T(8,128)(2,1)}), bf16[1,3072,768]{2,1,0:T(8,128)(2,1)}) %all-gather.41.cloned.1.call-update) | async-done | bytes 4718608 | tf_op jit(solution)/shard_map/all_gather | solution.py:122
  631.3 151.1 %all-gather.43.cloned.1.call-done = bf16[1,768,2304]{2,1,0:T(8,128)(2,1)} async-done(((bf16[1,24,2304]{2,1,0:T(8,128)(2,1)}), bf16[1,768,2304]{2,1,0:T(8,128)(2,1)}) %all-gather.43.cloned.1.call-update) | async-done | bytes 3538960 | tf_op jit(solution)/shard_map/all_gather | solution.py:113
  791.6 23.4 all-to-all-start.5
  885.8 48.0 %all-gather.45.cloned.1.call-done = bf16[1,768,768]{2,1,0:T(8,128)(2,1)} async-done(((bf16[1,24,768]{2,1,0:T(8,128)(2,1)}), bf16[1,768,768]{2,1,0:T(8,128)(2,1)}) %all-gather.45.cloned.1.call-update) | async-done | bytes 1179664 | tf_op jit(solution)/shard_map/all_gather | solution.py:116
  935.9 162.1 %all-gather.47.cloned.1.call-done = bf16[1,768,3072]{2,1,0:T(8,128)(2,1)} async-done(((bf16[1,24,3072]{2,1,0:T(8,128)(2,1)}), bf16[1,768,3072]{2,1,0:T(8,128)(2,1)}) %all-gather.47.cloned.1.call-update) | async-done | bytes 4718608 | tf_op jit(solution)/shard_map/all_gather | solution.py:120
  1098.0 11.7 multiply_convert_fusion.4
  1109.7 148.3 %all-gather.49.cloned.1.call-done = bf16[1,3072,768]{2,1,0:T(8,128)(2,1)} async-done(((bf16[1,96,768]{2,1,0:T(8,128)(2,1)}), bf16[1,3072,768]{2,1,0:T(8,128)(2,1)}) %all-gather.49.cloned.1.call-update) | async-done | bytes 4718608 | tf_op jit(solution)/shard_map/all_gather | solution.py:122
  1274.3 22.1 all-to-all-start.8
  1520.3 132.3 %all-reduce.36 = (bf16[768]{0:T(1024)(128)(2,1)}, bf16[768]{0:T(1024)(128)(2,1)}, bf16[768]{0:T(1024)(128)(2,1)}, bf16[768]{0:T(1024)(128)(2,1)}, bf16[768]{0:T(...) all-reduce(bf16[768]{0:T(1024)(128)(2,1)} %copy-done.127, ...), channel_id=27, replica_groups=mesh['seq'=4,'fsdp'=32] {'fsdp'}, use_global_device_ids=true, to_apply=%add.17 | all-reduce | flops 19200 | bytes 76800
  1664.5 18.4 reduce-scatter.13.cloned.1.call-done
  1721.3 29.1 %all-reduce.43.cloned.1.call-done = (bf16[1,24]{1,0:T(2,128)(2,1)}, bf16[1,24]{1,0:T(2,128)(2,1)}, bf16[1,24]{1,0:T(2,128)(2,1)}, bf16[1,24]{1,0:T(2,128)(2,1)},...) async-done(((bf16[1,24]{1,0:T(2,128)(2,1)}, ...) | async-done | bytes 74896 | tf_op jit(solution)/shard_map/psum | solution.py:314
  1752.9 144.2 %reduce-scatter.11.cloned.1.call-done = bf16[24,2304]{1,0:T(8,128)(2,1)} async-done(((bf16[768,2304]{1,0:T(8,128)(2,1)}), bf16[24,2304]{1,0:T(8,128)(2,1)}) %reduce-scatter.11.cloned.1.call-update) | async-done | bytes 110608 | tf_op jit(solution)/shard_map/reduce_scatter | solution.py:283
  1897.1 165.9 %reduce-scatter.9.cloned.1.call-done = bf16[24,2304]{1,0:T(8,128)(2,1)} async-done(((bf16[768,2304]{1,0:T(8,128)(2,1)}), bf16[24,2304]{1,0:T(8,128)(2,1)}) %reduce-scatter.9.cloned.1.call-update) | async-done | bytes 110608 | tf_op jit(solution)/shard_map/reduce_scatter | solution.py:283
  2063.0 168.1 %reduce-scatter.19.cloned.1.call-done = bf16[24,3072]{1,0:T(8,128)(2,1)} async-done(((bf16[768,3072]{1,0:T(8,128)(2,1)}), bf16[24,3072]{1,0:T(8,128)(2,1)}) %reduce-scatter.19.cloned.1.call-update) | async-done | bytes 147472 | tf_op jit(solution)/shard_map/reduce_scatter | solution.py:300
  2231.1 167.1 %reduce-scatter.23.cloned.1.call-done = bf16[96,768]{1,0:T(8,128)(2,1)} async-done(((bf16[3072,768]{1,0:T(8,128)(2,1)}), bf16[96,768]{1,0:T(8,128)(2,1)}) %reduce-scatter.23.cloned.1.call-update) | async-done | bytes 147472 | tf_op jit(solution)/shard_map/reduce_scatter | solution.py:306
  2398.2 168.3 %reduce-scatter.17.cloned.1.call-done = bf16[24,3072]{1,0:T(8,128)(2,1)} async-done(((bf16[768,3072]{1,0:T(8,128)(2,1)}), bf16[24,3072]{1,0:T(8,128)(2,1)}) %reduce-scatter.17.cloned.1.call-update) | async-done | bytes 147472 | tf_op jit(solution)/shard_map/reduce_scatter | solution.py:300
  2566.5 168.9 %reduce-scatter.21.cloned.1.call-done = bf16[96,768]{1,0:T(8,128)(2,1)} async-done(((bf16[3072,768]{1,0:T(8,128)(2,1)}), bf16[96,768]{1,0:T(8,128)(2,1)}) %reduce-scatter.21.cloned.1.call-update) | async-done | bytes 147472 | tf_op jit(solution)/shard_map/reduce_scatter | solution.py:306
  2745.4 54.9 %all-reduce.45.cloned.1.call-done = (bf16[1,24,2304]{2,1,0:T(8,128)(2,1)}, bf16[1,24,2304]{2,1,0:T(8,128)(2,1)}, bf16[1,24,3072]{2,1,0:T(8,128)(2,1)}, bf16[1,24...) async-done(((bf16[1,24,2304]{2,1,0:T(8,128)(2,1)}, bf16[1,24,2304]{2,1,0:T(8,128)(2,1)}, bf16[1,24,3072]{2,1,0:T(8,128)(2,1)}, ...) | async-done | bytes 811024 | tf_op jit(solution)/shard_map/psum | solution.py:316
  (711 shorter events, 507.0 us)
Async XLA Ops:
  7.2 172.3 %all-gather.35.cloned.1.call-start = ((), (), s32[]{:S(2)}) async-start(), calls=%async_computation.32 | async-start | bytes 3649536 | tf_op jit(solution)/shard_map/all_gather | solution.py:113
  8.9 294.3 %all-gather.37.cloned.1.call-start = ((), (), s32[]{:S(2)}) async-start(), calls=%async_computation.33 | async-start | bytes 1216512 | tf_op jit(solution)/shard_map/all_gather | solution.py:116
  10.5 456.4 %all-gather.39.cloned.1.call-start = ((), (), s32[]{:S(2)}) async-start(), calls=%async_computation.34 | async-start | bytes 4866048 | tf_op jit(solution)/shard_map/all_gather | solution.py:120
  12.2 614.4 %all-gather.41.cloned.1.call-start = ((), (), s32[]{:S(2)}) async-start(), calls=%async_computation.35 | async-start | bytes 4866048 | tf_op jit(solution)/shard_map/all_gather | solution.py:122
  14.0 768.3 %all-gather.43.cloned.1.call-start = ((), (), s32[]{:S(2)}) async-start(), calls=%async_computation.36 | async-start | bytes 3649536 | tf_op jit(solution)/shard_map/all_gather | solution.py:113
  14.6 919.2 %all-gather.45.cloned.1.call-start = ((), (), s32[]{:S(2)}) async-start(), calls=%async_computation.37 | async-start | bytes 1216512 | tf_op jit(solution)/shard_map/all_gather | solution.py:116
  15.2 1082.8 %all-gather.47.cloned.1.call-start = ((), (), s32[]{:S(2)}) async-start(), calls=%async_computation.38 | async-start | bytes 4866048 | tf_op jit(solution)/shard_map/all_gather | solution.py:120
  192.1 39.0 %all-to-all-start.1 = ((bf16[4,2,24576]{2,1,0:T(2,128)(2,1)}), bf16[4,2,24576]{2,1,0:T(2,128)(2,1)}, u32[]{:S(2)}, u32[]{:S(2)}) async-start(bf16[4,2,24576]{2,1,0:T(2,128)(2,1)} %reshape.701), calls=%async_computation.1 | async-start | bytes 786432 | tf_op jit(solution)/shard_map/all_to_all | solution.py:180
  282.7 975.3 %all-gather.49.cloned.1.call-start = ((), (), s32[]{:S(2)}) async-start(), calls=%async_computation.39 | async-start | bytes 4866048 | tf_op jit(solution)/shard_map/all_gather | solution.py:122
  791.6 33.1 %all-to-all-start.5 = ((bf16[4,2,24576]{2,1,0:T(2,128)(2,1)}), bf16[4,2,24576]{2,1,0:T(2,128)(2,1)S(1)}, u32[]{:S(2)}, u32[]{:S(2)}) async-start(bf16[4,2,24576]{2,1,0:T(2,128)(2,1)} %reshape.709), calls=%async_computation.5 | async-start | bytes 786432 | tf_op jit(solution)/shard_map/all_to_all | solution.py:180
  1274.3 30.2 %all-to-all-start.8 = ((bf16[4,2,24576]{2,1,0:T(2,128)(2,1)}), bf16[4,2,24576]{2,1,0:T(2,128)(2,1)S(1)}, u32[]{:S(2)}, u32[]{:S(2)}) async-start(bf16[4,2,24576]{2,1,0:T(2,128)(2,1)} %reshape.715), calls=%async_computation.8 | async-start | bytes 786432 | tf_op jit(solution)/shard_map/all_to_all | solution.py:237
  1331.2 32.8 %all-to-all-start.11 = ((bf16[4,2,24576]{2,1,0:T(2,128)(2,1)}), bf16[4,2,24576]{2,1,0:T(2,128)(2,1)}, u32[]{:S(2)}, u32[]{:S(2)}) async-start(bf16[4,2,24576]{2,1,0:T(2,128)(2,1)} %reshape.717), calls=%async_computation.11 | async-start | bytes 786432 | tf_op jit(solution)/shard_map/all_to_all | solution.py:244
  1381.4 283.1 %reduce-scatter.15.cloned.1.call-start = ((), (), s32[]{:S(2)}) async-start(), calls=%async_computation.27 | async-start | bytes 1216512 | tf_op jit(solution)/shard_map/reduce_scatter | solution.py:292
  1415.8 267.1 %reduce-scatter.13.cloned.1.call-start = ((), (), s32[]{:S(2)}) async-start(), calls=%async_computation.26 | async-start | bytes 1216512 | tf_op jit(solution)/shard_map/reduce_scatter | solution.py:292
  1450.8 32.7 %all-to-all-start.15 = ((bf16[4,2,24576]{2,1,0:T(2,128)(2,1)}), bf16[4,2,24576]{2,1,0:T(2,128)(2,1)}, u32[]{:S(2)}, u32[]{:S(2)}) async-start(bf16[4,2,24576]{2,1,0:T(2,128)(2,1)} %reshape.725), calls=%async_computation.15 | async-start | bytes 786432 | tf_op jit(solution)/shard_map/all_to_all | solution.py:244
  1497.3 15.0 all-to-all-start.13
  1501.6 248.8 %all-reduce.43.cloned.1.call-start = ((), (), s32[]{:S(2)}) async-start(), calls=%async_computation.40 | async-start | bytes 165888 | tf_op jit(solution)/shard_map/psum | solution.py:314
  1682.9 214.2 %reduce-scatter.11.cloned.1.call-start = ((), (), s32[]{:S(2)}) async-start(), calls=%async_computation.25 | async-start | bytes 3649536 | tf_op jit(solution)/shard_map/reduce_scatter | solution.py:283
  1687.0 376.0 %reduce-scatter.9.cloned.1.call-start = ((), (), s32[]{:S(2)}) async-start(), calls=%async_computation.24 | async-start | bytes 3649536 | tf_op jit(solution)/shard_map/reduce_scatter | solution.py:283
  1691.3 539.8 %reduce-scatter.19.cloned.1.call-start = ((), (), s32[]{:S(2)}) async-start(), calls=%async_computation.29 | async-start | bytes 4866048 | tf_op jit(solution)/shard_map/reduce_scatter | solution.py:300
  1696.7 701.5 %reduce-scatter.23.cloned.1.call-start = ((), (), s32[]{:S(2)}) async-start(), calls=%async_computation.31 | async-start | bytes 4866048 | tf_op jit(solution)/shard_map/reduce_scatter | solution.py:306
  1701.9 864.6 %reduce-scatter.17.cloned.1.call-start = ((), (), s32[]{:S(2)}) async-start(), calls=%async_computation.28 | async-start | bytes 4866048 | tf_op jit(solution)/shard_map/reduce_scatter | solution.py:300
  1708.0 1027.4 %reduce-scatter.21.cloned.1.call-start = ((), (), s32[]{:S(2)}) async-start(), calls=%async_computation.30 | async-start | bytes 4866048 | tf_op jit(solution)/shard_map/reduce_scatter | solution.py:306
  1713.2 1087.1 %all-reduce.45.cloned.1.call-start = ((), (), s32[]{:S(2)}) async-start(), calls=%async_computation.41 | async-start | bytes 1622016 | tf_op jit(solution)/shard_map/psum | solution.py:316
  (167 other events, 6339.8 us)
Sparse Core Ops, SparseCore 0:
  10.2 139.1 all-gather.34
  151.1 152.0 all-gather.36
  305.4 161.3 all-gather.38
  468.3 158.3 all-gather.40
  628.2 154.1 all-gather.42
  783.9 149.8 all-gather.44
  936.0 161.9 all-gather.46
  1099.6 158.3 all-gather.48
  1384.5 138.8 reduce-scatter.14
  1525.8 157.0 reduce-scatter.12
  1687.6 62.8 all-reduce.42
  1752.8 144.2 reduce-scatter.10
  1899.5 163.4 reduce-scatter.8
  2065.4 165.7 reduce-scatter.18
  2233.5 164.6 reduce-scatter.22
  2400.6 165.8 reduce-scatter.16
  2568.9 166.4 reduce-scatter.20
  2738.5 61.7 all-reduce.44
where the time goes:
time: 2820 us; the launch traced here: 2810 us
  waiting for transfers between devices  1960 us (70%)
  blocking collectives  268 us (10%)
  local copies, waits for them, and re-layouts  156 us (6%)
  matrix products  156 us (6%)
  starting transfers between devices  138 us (5%)
  other arithmetic  115 us (4%)
    reduce_scatter x2, waiting for transfers between devices, reduce_grads(): lax.psum_scatter(grads[9].astype(jnp.bfloat16), 'fsdp', scatter_dimension...  336 us
    reduce_scatter x2, waiting for transfers between devices, reduce_grads(): lax.psum_scatter(grads[11].astype(jnp.bfloat16), 'fsdp', scatter_dimensio...  336 us
    all_gather x2, waiting for transfers between devices, gather_layer(): lax.all_gather(shards[9][layer_index], 'fsdp', axis=0, tiled=True)  324 us
    reduce_scatter x2, waiting for transfers between devices, reduce_grads(): lax.psum_scatter(grads[2].astype(jnp.bfloat16), 'fsdp', scatter_dimension...  310 us
    all_gather x2, waiting for transfers between devices, gather_layer(): lax.all_gather(shards[11][layer_index], 'fsdp', axis=0, tiled=True)  296 us
    unnamed x2, blocking collectives  268 us
    all_gather x2, waiting for transfers between devices, gather_layer(): lax.all_gather(shards[2][layer_index], 'fsdp', axis=0, tiled=True)  151 us
    unnamed x401, local copies, waits for them, and re-layouts  91.3 us
  transfers between devices with their start and end apart: 34, of which 27 were waited for; matrix products, arithmetic and copies ran while one was open for 13% of the time, Pallas kernels for 0%

commit v1 on v0

v1 whole, which is shorter than its diff:
```python
import functools

import jax
import jax.numpy as jnp
from jax import lax
from jax.experimental import pallas as pl
from jax.experimental.pallas import tpu as pltpu
from jax.sharding import Mesh
from jax.sharding import PartitionSpec as P

HD = 64
AXES = ("xh", "core", "z", "xl", "y")
SIZES = (2, 2, 4, 2, 4)
FSDP = ("z", "xl", "y")
SEQ = ("xh", "core")
UNIT = 384
ROWS = 24
BF = jnp.bfloat16
F32 = jnp.float32
ANY = pl.BlockSpec(memory_space=pl.ANY)
SMEM = pl.BlockSpec(memory_space=pltpu.SMEM)
VMEM = pl.BlockSpec(memory_space=pltpu.VMEM)
ROOMY = pltpu.CompilerParams(vmem_limit_bytes=48 * 2**20)


def ravel(coords):
    index = 0
    for size, coord in zip(SIZES, coords):
        index = index * size + coord % size
    return index


def all_coords():
    xh_n, core_n, z_n, xl_n, y_n = SIZES
    return [
        (xh, core, z, xl, y)
        for xh in range(xh_n)
        for core in range(core_n)
        for z in range(z_n)
        for xl in range(xl_n)
        for y in range(y_n)
    ]


def shift(array, move):
    pairs = [(ravel(c), ravel(move(*c))) for c in all_coords()]
    return lax.ppermute(array, AXES, pairs)


def to_core(array):
    return shift(array, lambda xh, core, z, xl, y: (xh, core + 1, z, xl, y))


def to_xh(array):
    return shift(array, lambda xh, core, z, xl, y: (xh + 1, core, z, xl, y))


def to_xl(array):
    return shift(array, lambda xh, core, z, xl, y: (xh, core, z, xl + 1, y))


def to_inner(array, d):
    return shift(
        array,
        lambda xh, core, z, xl, y: (xh, core, z, xl, y + d) if core == 0 else (xh, core, z + d, xl, y),
    )


def to_outer(array, d):
    return shift(
        array,
        lambda xh, core, z, xl, y: (xh, core, z + d, xl, y) if core == 0 else (xh, core, z, xl, y + d),
    )


def slot_table(sign):
    core, z, xl, y = (lax.axis_index(n) for n in ("core", "z", "xl", "y"))
    inner = jnp.where(core == 0, y, z)
    outer = jnp.where(core == 0, z, y)
    dq = jnp.arange(4, dtype=jnp.int32)[:, None, None]
    dp = jnp.arange(4, dtype=jnp.int32)[None, :, None]
    dx = jnp.arange(2, dtype=jnp.int32)[None, None, :]
    q = (outer + sign * dq + 4) % 4
    if sign < 0:
        p = (inner - dp + 4) % 4
        x = (xl + dx) % 2
    else:
        p = dp
        x = dx
    owner = jnp.where(core == 0, q * 8 + x * 4 + p, p * 8 + x * 4 + q)
    return owner.astype(jnp.int32).reshape(32)


def assemble_kernel(wide, table, s0, s1, s2, s3, *rest):
    outs, sem = rest[:-1], rest[-1]
    copies = []
    for dq, src in enumerate((s0, s1, s2, s3)):
        for dp in range(4):
            for dx in range(2):
                n = dq * 8 + dp * 2 + dx
                f = table[n]
                copies.append(
                    pltpu.make_async_copy(
                        src.at[dp, dx, pl.ds(0, wide)], outs[0].at[:, f], sem.at[n, 0]
                    )
                )
                if len(outs) > 1:
                    copies.append(
                        pltpu.make_async_copy(
                            src.at[dp, dx, pl.ds(wide, 4)], outs[1].at[f], sem.at[n, 1]
                        )
                    )
    for copy in copies:
        copy.start()
    for copy in copies:
        copy.wait()


def gather_units(units, wide, table):
    count = units.shape[0]
    pair = jnp.stack([units, to_xl(units)])
    inner = jnp.stack([pair] + [to_inner(pair, d) for d in (1, 2, 3)])
    outer = [inner] + [to_outer(inner, d) for d in (1, 2, 3)]
    shapes = [jax.ShapeDtypeStruct((wide, 32, ROWS, UNIT), BF)]
    if count > wide:
        shapes.append(jax.ShapeDtypeStruct((32, 4, ROWS, UNIT), BF))
    return pl.pallas_call(
        functools.partial(assemble_kernel, wide),
        out_shape=shapes,
        in_specs=[SMEM] + [ANY] * 4,
        out_specs=[VMEM] * len(shapes),
        scratch_shapes=[pltpu.SemaphoreType.DMA((32, 2))],
        compiler_params=ROOMY,
    )(table, *outer)


def split_kernel(table, *rest):
    sem = rest[-1]
    outs = rest[-5:-1]
    srcs = rest[:-5]
    copies = []
    for dq, dst in enumerate(outs):
        for p in range(4):
            for x in range(2):
                n = dq * 8 + p * 2 + x
                f = table[n]
                wide = srcs[0].shape[0]
                copies.append(
                    pltpu.make_async_copy(
                        srcs[0].at[:, f], dst.at[p, x, pl.ds(0, wide)], sem.at[n, 0]
                    )
                )
                if len(srcs) > 1:
                    copies.append(
                        pltpu.make_async_copy(
                            srcs[1].at[f], dst.at[p, x, pl.ds(wide, 4)], sem.at[n, 1]
                        )
                    )
    for copy in copies:
        copy.start()
    for copy in copies:
        copy.wait()


def add_all(*parts):
    total = parts[0].astype(F32)
    for part in parts[1:]:
        total = total + part.astype(F32)
    return total.astype(BF)


def scatter_units(grads, table):
    count = grads[0].shape[0] + (4 if len(grads) > 1 else 0)
    blocks = pl.pallas_call(
        split_kernel,
        out_shape=[jax.ShapeDtypeStruct((4, 2, count, ROWS, UNIT), BF)] * 4,
        in_specs=[SMEM] + [ANY] * len(grads),
        out_specs=[VMEM] * 4,
        scratch_shapes=[pltpu.SemaphoreType.DMA((32, 2))],
        compiler_params=ROOMY,
    )(table, *grads)
    total = add_all(blocks[0], *[to_outer(blocks[d], d) for d in (1, 2, 3)])
    core, z, xl, y = (lax.axis_index(n) for n in ("core", "z", "xl", "y"))
    inner = jnp.where(core == 0, y, z)
    parts = [lax.dynamic_index_in_dim(total, (inner + d) % 4, 0, keepdims=False) for d in range(4)]
    total = add_all(parts[0], *[to_inner(parts[d], d) for d in (1, 2, 3)])
    mine = lax.dynamic_index_in_dim(total, xl, 0, keepdims=False)
    other = lax.dynamic_index_in_dim(total, 1 - xl, 0, keepdims=False)
    total = add_all(mine, to_xl(other))
    return add_all(total, to_xh(total))


def norm_parts(values):
    centred = values - jnp.mean(values, -1, keepdims=True)
    scale = lax.rsqrt(jnp.mean(centred * centred, -1, keepdims=True) + 1e-06)
    return centred * scale, scale


def layer_norm(values, gain, bias):
    return norm_parts(values)[0] * gain + bias


def norm_back(values, gain, grad):
    n, scale = norm_parts(values)
    dg = grad * gain
    out = scale * (
        dg - jnp.mean(dg, -1, keepdims=True) - n * jnp.mean(dg * n, -1, keepdims=True)
    )
    return out, jnp.sum(grad * n, 0), jnp.sum(grad, 0)


def dot(a, b):
    return jnp.dot(a, b, preferred_element_type=F32)


def dot_nt(a, b):
    return lax.dot_general(a, b, (((1,), (1,)), ((), ())), preferred_element_type=F32)


def dot_tn(a, b):
    return lax.dot_general(a, b, (((0,), (0,)), ((), ())), preferred_element_type=F32)


def pick(flag, first, second, axis):
    return jnp.concatenate(
        [jnp.where(flag, first, second), jnp.where(flag, second, first)], axis
    )


def heads_of(rows):
    return rows.reshape(rows.shape[0], -1, HD)


def attend(q, k, v, ids_q, ids_k):
    s = jnp.einsum("qhe,khe->hqk", heads_of(q), heads_of(k), preferred_element_type=F32)
    s = jnp.where((ids_q[:, None] == ids_k[None, :])[None], s * HD**-0.5, -1e30)
    peak = jnp.max(s, -1, keepdims=True)
    e = jnp.exp(s - peak)
    total = jnp.sum(e, -1, keepdims=True)
    prob = (e / total).astype(BF)
    o = jnp.einsum("hqk,khe->qhe", prob, heads_of(v), preferred_element_type=F32)
    return o.astype(BF).reshape(q.shape), (peak + jnp.log(total))[..., 0]


def attend_back(q, k, v, ids_q, ids_k, lse, go):
    qh, kh, vh, gh = heads_of(q), heads_of(k), heads_of(v), heads_of(go)
    s = jnp.einsum("qhe,khe->hqk", qh, kh, preferred_element_type=F32)
    s = jnp.where((ids_q[:, None] == ids_k[None, :])[None], s * HD**-0.5, -1e30)
    prob = jnp.exp(s - lse[..., None])
    gv = jnp.einsum("hqk,qhe->khe", prob.astype(BF), gh, preferred_element_type=F32)
    dp = jnp.einsum("qhe,khe->hqk", gh, vh, preferred_element_type=F32)
    gs = (prob * (dp - jnp.sum(dp * prob, -1, keepdims=True))).astype(BF)
    gq = jnp.einsum("hqk,khe->qhe", gs, kh, preferred_element_type=F32) * HD**-0.5
    gk = jnp.einsum("hqk,qhe->khe", gs, qh, preferred_element_type=F32) * HD**-0.5
    return (
        gq.astype(BF).reshape(q.shape),
        gk.astype(BF).reshape(k.shape),
        gv.astype(BF).reshape(v.shape),
    )


def gelu(u):
    return jax.nn.gelu(u, approximate=False)


def body(
    tokens,
    image_ids,
    cotangent,
    attn_norm_gain,
    attn_norm_bias,
    qkv_weight,
    query_bias,
    value_bias,
    proj_weight,
    proj_bias,
    mlp_norm_gain,
    mlp_norm_bias,
    fc_in_weight,
    fc_in_bias,
    fc_out_weight,
    fc_out_bias,
):
    core, xh, xl = (lax.axis_index(n) for n in ("core", "xh", "xl"))
    first = core == 0
    width = tokens.shape[2]
    half = width // 2
    tok = tokens.shape[1]

    def column(vec):
        return vec[:, None]

    vec_list = []
    for l in range(2):
        for vec in (
            attn_norm_gain,
            attn_norm_bias,
            query_bias,
            value_bias,
            proj_bias,
            mlp_norm_gain,
            mlp_norm_bias,
            fc_out_bias,
        ):
            vec_list.append(column(vec[l]))
        vec_list.append(fc_in_bias[l].reshape(4, ROWS).T)
    vec_unit = jnp.concatenate(vec_list, 1)
    vec_unit = jnp.pad(vec_unit, ((0, 0), (0, UNIT - vec_unit.shape[1])))

    def mine(part, start):
        return lax.dynamic_slice_in_dim(part, start + core * UNIT, UNIT, 1)

    def attn_units(l):
        return [mine(qkv_weight[l], j * width) for j in range(3)] + [mine(proj_weight[l], 0)]

    def mlp_units(l):
        inner = lax.dynamic_slice_in_dim(fc_in_weight[l], core * 4 * UNIT, 4 * UNIT, 1)
        outs = mine(fc_out_weight[l], 0).reshape(4, ROWS, UNIT)
        return [inner[:, j * UNIT : (j + 1) * UNIT] for j in range(4)] + [outs[j] for j in range(4)]

    table_in = slot_table(-1)
    table_out = slot_table(1)

    g1 = gather_units(jnp.stack(attn_units(0) + [vec_unit]), 5, table_in)[0]
    g2 = gather_units(jnp.stack(mlp_units(0)), 4, table_in)
    g3 = gather_units(jnp.stack(attn_units(1)), 4, table_in)[0]
    g4 = gather_units(jnp.stack(mlp_units(1)), 4, table_in)

    vec_rows = g1[4].reshape(width, UNIT)[:, :32].T.astype(F32)

    def weights(attn, mlp, l):
        wq, wk, wv, proj_h = (attn[j].reshape(width, UNIT) for j in range(4))
        proj = pick(first, proj_h, to_core(proj_h), 1)
        inner = mlp[0].reshape(4, width, UNIT)
        other = to_core(inner)
        inner = pick(first, inner, other, 0)
        fc_in = jnp.concatenate([inner[j] for j in range(8)], 1)
        out_h = mlp[1].reshape(4 * width, UNIT)
        fc_out = pick(first, out_h, to_core(out_h), 1)
        vec = vec_rows[l * 12 : l * 12 + 8]
        fin = vec_rows[l * 12 + 8 : l * 12 + 12].reshape(4, 32, ROWS).transpose(1, 0, 2).reshape(-1)
        return dict(wq=wq, wk=wk, wv=wv, proj=proj, fc_in=fc_in, fc_out=fc_out, vec=vec, fin=fin)

    sets = [weights(g1, g2, 0), weights(g3, g4, 1)]

    def segment(dx, dc):
        return lax.dynamic_slice_in_dim(
            image_ids[0], (((xh + dx) % 2) * 2 + (core + dc) % 2) * tok, tok, 0
        )

    ids = jnp.concatenate([segment(0, 0), segment(0, 1), segment(1, 0), segment(1, 1)])
    ids_q = ids[: 2 * tok]

    def half_vec(vec):
        return lax.dynamic_slice_in_dim(vec, core * half, half, 0)

    def forward(x, w):
        vec = w["vec"]
        a = layer_norm(x, vec[0], vec[1]).astype(BF)
        far = to_xh(a)
        a_all = jnp.concatenate([a, to_core(a), far, to_core(far)], 0)
        q = (dot(a_all[: 2 * tok], w["wq"]) + half_vec(vec[2])).astype(BF)
        k = dot(a_all, w["wk"]).astype(BF)
        v = (dot(a_all, w["wv"]) + half_vec(vec[3])).astype(BF)
        o, lse = attend(q, k, v, ids_q, ids)
        o_full = pick(first, o[:tok], to_core(o[tok:]), 1)
        m = x + (dot(o_full, w["proj"]) + vec[4])
        c = layer_norm(m, vec[5], vec[6]).astype(BF)
        u = dot(c, w["fc_in"]) + w["fin"]
        z = gelu(u).astype(BF)
        out = m + (dot(z, w["fc_out"]) + vec[7])
        return out, (x, a_all, q, k, v, lse, o_full, m, c, u, z)

    def backward(gx, w, saved):
        x, a_all, q, k, v, lse, o_full, m, c, u, z = saved
        vec = w["vec"]
        gm = gx.astype(BF)
        dz = dot_nt(gm, w["fc_out"])
        gu = jax.vjp(gelu, u)[1](dz)[0].astype(BF)
        dc = dot_nt(gu, w["fc_in"])
        dm, mlp_gain_g, mlp_bias_g = norm_back(m, vec[5], dc)
        gmid = gx + dm
        ga = gmid.astype(BF)
        go = dot_nt(ga, w["proj"]).astype(BF)
        go_mine = lax.dynamic_slice_in_dim(go, core * half, half, 1)
        go_other = lax.dynamic_slice_in_dim(go, (1 - core) * half, half, 1)
        go_heads = jnp.concatenate([go_mine, to_core(go_other)], 0)
        d_out = dot_tn(z, gm).astype(BF)
        d_in = dot_tn(c, gu).astype(BF)
        d_proj = dot_tn(o_full, ga).astype(BF)
        gq, gk, gv = attend_back(q, k, v, ids_q, ids, lse, go_heads)
        da = dot_nt(gk, w["wk"]) + dot_nt(gv, w["wv"])
        da_near = da[: 2 * tok] + dot_nt(gq, w["wq"])
        da_far = da[2 * tok :]
        recv = to_core(da_far[tok:].astype(BF))
        far = to_xh((da_far[:tok] + recv.astype(F32)).astype(BF))
        near = to_core(da_near[tok:].astype(BF))
        da_own = da_near[:tok] + near.astype(F32) + far.astype(F32)
        dx, gain_g, bias_g = norm_back(x, vec[0], da_own)
        d_q = dot_tn(a_all[: 2 * tok], gq).astype(BF)
        d_k = dot_tn(a_all, gk).astype(BF)
        d_v = dot_tn(a_all, gv).astype(BF)

        def spread(vec_half):
            zero = jnp.zeros((half,), F32)
            return pick(first, vec_half, zero, 0)

        def total(g):
            return jnp.sum(g.astype(F32), 0)

        rows = [
            gain_g,
            bias_g,
            spread(total(gq)),
            spread(total(gv)),
            total(ga),
            mlp_gain_g,
            mlp_bias_g,
            total(gm),
        ]
        fin = total(gu).reshape(32, 4, ROWS).transpose(1, 0, 2).reshape(4, width)
        table = jnp.concatenate([jnp.stack(rows), fin], 0).astype(BF)
        table = jnp.pad(table, ((0, UNIT - 12), (0, 0)))
        table = table.T
        table = add_all(table, to_core(table))

        def halves(grad):
            keep = lax.dynamic_slice_in_dim(grad, core * (grad.shape[1] // 2), grad.shape[1] // 2, 1)
            send = lax.dynamic_slice_in_dim(
                grad, (1 - core) * (grad.shape[1] // 2), grad.shape[1] // 2, 1
            )
            return add_all(keep, to_core(send))

        d_in = halves(d_in)
        wide = [d_in[:, j * UNIT : (j + 1) * UNIT] for j in range(4)] + [halves(d_proj)]
        part1 = scatter_units(
            [
                jnp.stack(wide).reshape(5, 32, ROWS, UNIT),
                halves(d_out).reshape(32, 4, ROWS, UNIT),
            ],
            table_out,
        )
        part2 = scatter_units(
            [jnp.stack([d_q, d_k, d_v, table]).reshape(4, 32, ROWS, UNIT)], table_out
        )
        return gmid + dx, (part1, part2)

    x = tokens[0].astype(F32)
    saved = []
    for l in range(2):
        x, keep = forward(x, sets[l])
        saved.append(keep)
    gx = cotangent[0].astype(F32)
    parts = [None, None]
    for l in (1, 0):
        gx, parts[l] = backward(gx, sets[l], saved[l])

    def finish(l):
        part1, part2 = parts[l]
        own = jnp.concatenate([part1, part2], 0)
        other = to_core(own)
        lo = jnp.where(first, own, other).astype(F32)
        hi = jnp.where(first, other, own).astype(F32)
        fc_in = jnp.concatenate([lo[j] for j in range(4)] + [hi[j] for j in range(4)], 1)
        proj = jnp.concatenate([lo[4], hi[4]], 1)
        fc_out = jnp.concatenate(
            [lo[5:9].reshape(4 * ROWS, UNIT), hi[5:9].reshape(4 * ROWS, UNIT)], 1
        )
        qkv = jnp.concatenate([lo[9], hi[9], lo[10], hi[10], lo[11], hi[11]], 1)
        vecs = lo[12]
        cols = [vecs[:, j] for j in range(8)]
        fin = vecs[:, 8:12].T.reshape(-1)
        return (
            cols[0],
            cols[1],
            qkv,
            cols[2],
            cols[3],
            proj,
            cols[4],
            cols[5],
            cols[6],
            fc_in,
            fin,
            fc_out,
            cols[7],
        )

    done = [finish(0), finish(1)]
    stacked = tuple(jnp.stack([done[0][j], done[1][j]]) for j in range(13))
    return (x.astype(BF)[None], gx[None]) + stacked


def solution(mesh):
    fine = Mesh(mesh.devices.reshape(SIZES), AXES)
    row = P(None, FSDP)
    mat = P(None, FSDP, None)
    tok = P(FSDP, SEQ, None)
    return jax.shard_map(
        body,
        mesh=fine,
        in_specs=(
            tok,
            P(FSDP, None),
            tok,
            row,
            row,
            mat,
            row,
            row,
            mat,
            row,
            row,
            row,
            mat,
            row,
            mat,
            row,
        ),
        out_specs=(tok, tok, row, row, mat, row, row, mat, row, row, row, mat, row, mat, row),
        check_vma=False,
    )
```

time: 2820 us -> 634 us (0.22)
  waiting for transfers between devices: 1960 us -> 167 us
  blocking collectives: 268 us -> 0 us
  local copies, waits for them, and re-layouts: 156 us -> 79.8 us
  other arithmetic: 115 us -> 80.6 us
    reduce_scatter x8 -> x0, waiting for transfers between devices: 1000 us -> none  [the longest x2 336 us: reduce_grads(): lax.psum_scatter(grads[9].astype(jnp.bfloat16), 'fsdp', scatter_dimension...]
    all_gather x8 -> x0, waiting for transfers between devices: 827 us -> none  [the longest x2 324 us: gather_layer(): lax.all_gather(shards[9][layer_index], 'fsdp', axis=0, tiled=True)]
    unnamed x2 -> x0, blocking collectives: 268 us -> none
    ppermute x0 -> x92, waiting for transfers between devices: none -> 167 us  [shift(): return lax.ppermute(array, AXES, pairs)]
    all_to_all x16 -> x0, starting transfers between devices: 137 us -> none  [the longest x2 54 us: forward_layer(): lax.all_to_all(queries, 'seq', split_axis=2, concat_axis=1, tiled=True)]
    ppermute x0 -> x92, starting transfers between devices: none -> 127 us  [shift(): return lax.ppermute(array, AXES, pairs)]
    psum x2 -> x0, waiting for transfers between devices: 84 us -> none  [the longest x1 54.9 us: reduce_grads(): lax.psum(parts[2].astype(jnp.bfloat16), 'seq').astype(jnp.float32)]
    unnamed x401 -> x340, local copies, waits for them, and re-layouts: 91.3 us -> 12.7 us
  transfers between devices with their start and end apart: 34 -> 92, of which waited for: 27 -> 37; matrix products, arithmetic and copies ran while one was open for 13% -> 38% of each run, Pallas kernels for 0% -> 4%
where the time goes in v1:
time: 634 us; the launch traced here: 624 us
  waiting for transfers between devices  167 us (26%)
  matrix products  137 us (22%)
  starting transfers between devices  127 us (20%)
  other arithmetic  80.6 us (13%)
  local copies, waits for them, and re-layouts  79.8 us (13%)
  Pallas kernels  28 us (4%)
    ppermute x92, waiting for transfers between devices, shift(): return lax.ppermute(array, AXES, pairs)  167 us
    ppermute x92, starting transfers between devices, shift(): return lax.ppermute(array, AXES, pairs)  127 us
    dot_general x12, matrix products, dot(): return jnp.dot(a, b, preferred_element_type=F32)  33.1 us
    dot_general x12, matrix products, dot_tn(): lax.dot_general(a, b, (((0,), (0,)), ((), ())), preferred_element_type=F32)  30.1 us
    convert_element_type x24, other arithmetic, add_all(): return total.astype(BF)  24.1 us
    dot_general x12, matrix products, dot_nt(): lax.dot_general(a, b, (((1,), (1,)), ((), ())), preferred_element_type=F32)  20.7 us
    dot_general x2, matrix products, attend_back(): dp = jnp.einsum('qhe,khe->hqk', gh, vh, preferred_element_type=F32)  18 us
    pallas_call x4, Pallas kernels, gather_units(): pl.pallas_call(functools.partial(assemble_kernel, wide), out_shape=shapes...  16.5 us
  transfers between devices with their start and end apart: 92, of which 37 were waited for; matrix products, arithmetic and copies ran while one was open for 38% of the time, Pallas kernels for 4%

profile of v1, /device:TPU:1, one launch (start us, length us, event | category | flops | bytes accessed | tf_op | source)
XLA Modules:
  0.0 623.7 jit_solution(15092073951157922128)
XLA Ops:
  52.5 4.3 collective-permute-start.35
  63.6 10.4 %collective-permute-done.6.s3 = bf16[4,2,5,24,384]{4,3,2,1,0:T(8,128)(2,1)S(1)} collective-permute-done((bf16[4,2,5,24,384]{4,3,2,1,0:T(8,128)(2,1)S(1)}, bf16[4,2,5,24,384]{4,3,2,1,0:T(8,128)(2,1)S(1)}, u32[]{:S(2)}, u32[]{:S(2)}) %collective-permute-start.6) | collective-permute-done | bytes 737312 | tf_op jit(solution)/shard_map/ppermute | solution.py:47
  82.1 10.0 %collective-permute-start.32 = (bf16[768,384]{1,0:T(8,128)(2,1)}, bf16[768,384]{1,0:T(8,128)(2,1)}, u32[]{:S(2)}, u32[]{:S(2)}) collective-permute-start(bf16[768,384]{1,0:T(8,128)(2,1)} %bitcast.79), channel_id=1, source_target_pairs={{0,32},{1,33},{2,34},{3,35},{4,36},{5,37},{6,38},{7,39},{8,40},{9,... | collective-permute-start | bytes 1769480 | tf_op jit(solution)/shard_map/ppermute | solution.py:47
  107.9 6.4 %collective-permute-done.8 = bf16[256,768]{1,0:T(8,128)(2,1)} collective-permute-done((bf16[256,768]{1,0:T(8,128)(2,1)}, bf16[256,768]{1,0:T(8,128)(2,1)}, u32[]{:S(2)}, u32[]{:S(2)}) %collective-permute-start.8) | collective-permute-done | bytes 393248 | tf_op jit(solution)/shard_map/ppermute | solution.py:47
  138.0 18.5 %collective-permute-done.16.s1 = bf16[4,2,8,24,384]{4,3,2,1,0:T(8,128)(2,1)} collective-permute-done((bf16[4,2,8,24,384]{4,3,2,1,0:T(8,128)(2,1)S(1)}, bf16[4,2,8,24,384]{4,3,2,1,0:T(8,128)(2,1)}, u32[]{:S(2)}, u32[]{:S(2)}) %collective-permute-start.16) | collective-permute-done | bytes 1179680 | tf_op jit(solution)/shard_map/ppermute | solution.py:47
  156.5 6.0 shard_map.272
  164.8 6.4 %shard_map.274 = (bf16[4,32,24,384]{3,2,1,0:T(8,128)(2,1)}, bf16[32,4,24,384]{3,2,1,0:T(8,128)(2,1)}) custom-call(s32[32]{0:T(128)S(1)} %select_n.424.table, bf16[4,2,8,24,384]{4,3,2,1,0:T(8,128)(2,1)S(1)} %pad_maximum_fusion.27.s0, bf16[4,2,8,24,384]{4,3,2,1,0:T(8,128)(2,1)} %collective-permute-done.37.s1, ...), custom_call_target="tpu_custom_call" | custom-call | tf_op jit(solution)/shard_map/pallas_call | solution.py:127
  190.5 11.1 %multiply_convert_fusion.3 = (bf16[256,3072]{1,0:T(8,128)(2,1)S(1)}, f32[256,3072]{1,0:T(8,128)}, f32[256,3072]{1,0:T(8,128)}) fusion(f32[3072]{0:T(1024)S(1)} %copy-done.103, bf16[768,3072]{1,0:T(8,128)(2,1)S(1)} %fusion.83, f32[256,768]{1,0:T(8,128)S(1)} %get-tuple-element.264, f32[768]{0:T(1024)S(1)} %copy-done.81, f32[768]{0:T(1024)S(1)} %get-tuple-element.214, ...), kind=kOutput, calls=%fused_computation.54 | convolution fusion | flops 1260847104 | bytes 13389824 | tf_op jit(solution)/shard_map/dot_general | solution.py:213
  211.2 5.6 collective-permute-done.22
  233.7 8.1 %multiply_convert_fusion.2 = (bf16[256,3072]{1,0:T(8,128)(2,1)S(1)}, f32[256,3072]{1,0:T(8,128)S(1)}, f32[256,3072]{1,0:T(8,128)S(1)}) fusion(f32[3072]{0:T(1024)S(1)} %copy-done.102, bf16[768,3072]{1,0:T(8,128)(2,1)S(1)} %fusion.75, f32[256,768]{1,0:T(8,128)S(1)} %get-tuple-element.271, f32[768]{0:T(1024)S(1)} %copy-done.82, ...), kind=kOutput, calls=%fused_computation.41 | convolution fusion | flops 1260847104 | bytes 13389824 | tf_op jit(solution)/shard_map/dot_general | solution.py:213
  271.5 7.5 %convert_reduce_fusion = (bf16[6,64]{1,0:T(8,128)(2,1)S(1)}, bf16[6,64,1024]{2,1,0:T(8,128)(2,1)}) fusion(bf16[512,6,64]{0,2,1:T(8,128)(2,1)S(1)} %bitcast.607, f32[6,512,1024]{2,1,0:T(8,128)} %copy-done.1, f32[6,512]{1,0:T(8,128)S(1)} %copy-done.73), kind=kOutput, calls=%fused_computation.90 | convolution fusion | flops 410123904 | bytes 13775616 | tf_op jit(solution)/shard_map/hqk,qhe->khe/dot_general | solution.py:250
  279.1 8.9 %multiply_reduce_fusion.1 = (f32[6,512]{1,0:T(8,128)S(1)}, f32[6,512,1024]{2,1,0:T(8,128)}) fusion(f32[6,512,1024]{2,1,0:T(8,128)} %copy-done.1, f32[6,512]{1,0:T(8,128)S(1)} %copy-done.73, bf16[512,6,64]{0,2,1:T(8,128)(2,1)S(1)} %bitcast.608, bf16[1024,6,64]{0,2,1:T(8,128)(2,1)S(1)} %bitcast.660), kind=kOutput, calls=%fused_computation.4 | convolution fusion | flops 412087296 | bytes 26370048 | tf_op jit(solution)/shard_map/qhe,khe->hqk/dot_general | solution.py:251
  288.0 6.2 multiply_convert_fusion.1
  319.3 5.9 collective-permute-done.45
  351.2 7.0 %convert_reduce_fusion.1 = (bf16[6,64]{1,0:T(8,128)(2,1)S(1)}, bf16[6,64,1024]{2,1,0:T(8,128)(2,1)}) fusion(bf16[512,6,64]{0,2,1:T(8,128)(2,1)S(1)} %bitcast.609, f32[6,512,1024]{2,1,0:T(8,128)} %copy-done, f32[6,512]{1,0:T(8,128)S(1)} %copy-done.72), kind=kOutput, calls=%fused_computation.91 | convolution fusion | flops 410123904 | bytes 13775616 | tf_op jit(solution)/shard_map/hqk,qhe->khe/dot_general | solution.py:250
  358.2 9.0 %multiply_reduce_fusion = (f32[6,512]{1,0:T(8,128)S(1)}, f32[6,512,1024]{2,1,0:T(8,128)}) fusion(f32[6,512,1024]{2,1,0:T(8,128)} %copy-done, f32[6,512]{1,0:T(8,128)S(1)} %copy-done.72, bf16[512,6,64]{0,2,1:T(8,128)(2,1)S(1)} %bitcast.610, bf16[1024,6,64]{0,2,1:T(8,128)(2,1)S(1)} %bitcast.658), kind=kOutput, calls=%fused_computation.1 | convolution fusion | flops 412087296 | bytes 26370048 | tf_op jit(solution)/shard_map/qhe,khe->hqk/dot_general | solution.py:251
  367.2 6.3 %multiply_convert_fusion = bf16[6,512,1024]{2,1,0:T(8,128)(2,1)S(1)} fusion(f32[6,512,1024]{2,1,0:T(8,128)} %get-tuple-element.278, f32[6,512,1024]{2,1,0:T(8,128)S(1)} %bitcast.596, f32[6,512]{1,0:T(8,128)S(1)} %get-tuple-element.277, f32[6,512]{1,0:T(8,128)S(1)} %copy-done.72), kind=kLoop, calls=%fused_computation | loop fusion | flops 12582912 | bytes 31481856 | tf_op jit(solution)/shard_map/convert_element_type | solution.py:252
  417.8 8.9 %collective-permute-done.83 = bf16[4,2,4,24,384]{4,3,2,1,0:T(8,128)(2,1)S(1)} collective-permute-done((bf16[4,2,4,24,384]{4,3,2,1,0:T(8,128)(2,1)S(1)}, bf16[4,2,4,24,384]{4,3,2,1,0:T(8,128)(2,1)S(1)}, u32[]{:S(2)}, u32[]{:S(2)}) %collective-permute-start.83) | collective-permute-done | bytes 589856 | tf_op jit(solution)/shard_map/ppermute | solution.py:47
  442.9 4.3 add_convert_fusion
  467.8 7.3 %collective-permute-done.62 = bf16[4,2,4,24,384]{4,3,2,1,0:T(8,128)(2,1)S(1)} collective-permute-done((bf16[4,2,4,24,384]{4,3,2,1,0:T(8,128)(2,1)S(1)}, bf16[4,2,4,24,384]{4,3,2,1,0:T(8,128)(2,1)S(1)}, u32[]{:S(2)}, u32[]{:S(2)}) %collective-permute-start.62) | collective-permute-done | bytes 589856 | tf_op jit(solution)/shard_map/ppermute | solution.py:47
  495.4 20.3 %collective-permute-done.74 = bf16[4,2,9,24,384]{4,3,2,1,0:T(8,128)(2,1)S(1)} collective-permute-done((bf16[4,2,9,24,384]{4,3,2,1,0:T(8,128)(2,1)S(1)}, bf16[4,2,9,24,384]{4,3,2,1,0:T(8,128)(2,1)S(1)}, u32[]{:S(2)}, u32[]{:S(2)}) %collective-permute-start.74) | collective-permute-done | bytes 1327136 | tf_op jit(solution)/shard_map/ppermute | solution.py:47
  540.6 7.2 %collective-permute-start.91 = (bf16[13,24,384]{2,1,0:T(8,128)(2,1)S(1)}, bf16[13,24,384]{2,1,0:T(8,128)(2,1)S(1)}, u32[]{:S(2)}, u32[]{:S(2)}) collective-permute-start(bf16[13,24,384]{2,1,0:T(8,128)(2,1)S(1)} %pad_maximum_fusion.54), channel_id=1, source_target_pairs={{0,32},{1,33},{2,34},{3,35},{4,36},{5,37},{6,38},{7,39},{8,40},{9,... | collective-permute-start | bytes 718856 | tf_op jit(solution)/shard_map/ppermute | solution.py:47
  556.4 15.0 %collective-permute-done.53 = bf16[4,2,9,24,384]{4,3,2,1,0:T(8,128)(2,1)S(1)} collective-permute-done((bf16[4,2,9,24,384]{4,3,2,1,0:T(8,128)(2,1)S(1)}, bf16[4,2,9,24,384]{4,3,2,1,0:T(8,128)(2,1)S(1)}, u32[]{:S(2)}, u32[]{:S(2)}) %collective-permute-start.53) | collective-permute-done | bytes 1327136 | tf_op jit(solution)/shard_map/ppermute | solution.py:47
  571.4 14.4 %collective-permute-done.54 = bf16[4,2,9,24,384]{4,3,2,1,0:T(8,128)(2,1)S(1)} collective-permute-done((bf16[4,2,9,24,384]{4,3,2,1,0:T(8,128)(2,1)S(1)}, bf16[4,2,9,24,384]{4,3,2,1,0:T(8,128)(2,1)S(1)}, u32[]{:S(2)}, u32[]{:S(2)}) %collective-permute-start.54) | collective-permute-done | bytes 1327136 | tf_op jit(solution)/shard_map/ppermute | solution.py:47
  (828 shorter events, 404.9 us)
Async XLA Ops:
  49.0 33.1 %collective-permute-start.4 = (bf16[4,2,5,24,384]{4,3,2,1,0:T(8,128)(2,1)S(1)}, bf16[4,2,5,24,384]{4,3,2,1,0:T(8,128)(2,1)S(1)}, u32[]{:S(2)}, u32[]{:S(2)}) collective-permute-start(bf16[4,2,5,24,384]{4,3,2,1,0:T(8,128)(2,1)S(1)} %pad_maximum_fusion.34.s0), channel_id=1, source_target_pairs={{0,8},{1,9},{2,10},{3,11},{4,12},{5,13},{6,14},{7,15},{8,16},{9,17... | collective-permute-start | bytes 2211848 | tf_op jit(solution)/shard_map/ppermute | solution.py:47
  52.5 45.4 %collective-permute-start.35 = (bf16[2,8,24,384]{3,2,1,0:T(8,128)(2,1)}, bf16[2,8,24,384]{3,2,1,0:T(8,128)(2,1)}, u32[]{:S(2)}, u32[]{:S(2)}) collective-permute-start(bf16[2,8,24,384]{3,2,1,0:T(8,128)(2,1)} %get-tuple-element.191), channel_id=1, source_target_pairs={{0,2},{1,3},{2,0},{3,1},{4,6},{5,7},{6,4},{7,5},{8,10},{9,11},{10,... | collective-permute-start | bytes 884744 | tf_op jit(solution)/shard_map/ppermute | solution.py:47
  60.0 38.9 %collective-permute-start.34 = (bf16[2,8,24,384]{3,2,1,0:T(8,128)(2,1)}, bf16[2,8,24,384]{3,2,1,0:T(8,128)(2,1)}, u32[]{:S(2)}, u32[]{:S(2)}) collective-permute-start(bf16[2,8,24,384]{3,2,1,0:T(8,128)(2,1)} %get-tuple-element.191), channel_id=1, source_target_pairs={{0,1},{1,2},{2,3},{3,0},{4,5},{5,6},{6,7},{7,4},{8,9},{9,10},{10,1... | collective-permute-start | bytes 884744 | tf_op jit(solution)/shard_map/ppermute | solution.py:47
  75.8 40.0 %collective-permute-start.18 = (bf16[4,2,8,24,384]{4,3,2,1,0:T(8,128)(2,1)S(1)}, bf16[4,2,8,24,384]{4,3,2,1,0:T(8,128)(2,1)S(1)}, u32[]{:S(2)}, u32[]{:S(2)}) collective-permute-start(bf16[4,2,8,24,384]{4,3,2,1,0:T(8,128)(2,1)S(1)} %pad_maximum_fusion.25.s0), channel_id=1, source_target_pairs={{0,24},{1,25},{2,26},{3,27},{4,28},{5,29},{6,30},{7,31},{8,0},{9,1... | collective-permute-start | bytes 3538952 | tf_op jit(solution)/shard_map/ppermute | solution.py:47
  98.9 33.6 %collective-permute-start.17 = (bf16[4,2,8,24,384]{4,3,2,1,0:T(8,128)(2,1)S(1)}, bf16[4,2,8,24,384]{4,3,2,1,0:T(8,128)(2,1)}, u32[]{:S(2)}, u32[]{:S(2)}) collective-permute-start(bf16[4,2,8,24,384]{4,3,2,1,0:T(8,128)(2,1)S(1)} %pad_maximum_fusion.25.s0), channel_id=1, source_target_pairs={{0,16},{1,17},{2,18},{3,19},{4,20},{5,21},{6,22},{7,23},{8,24},{9,... | collective-permute-start | bytes 3538952 | tf_op jit(solution)/shard_map/ppermute | solution.py:47
  114.2 50.5 %collective-permute-start.39 = (bf16[4,2,8,24,384]{4,3,2,1,0:T(8,128)(2,1)S(1)}, bf16[4,2,8,24,384]{4,3,2,1,0:T(8,128)(2,1)}, u32[]{:S(2)}, u32[]{:S(2)}) collective-permute-start(bf16[4,2,8,24,384]{4,3,2,1,0:T(8,128)(2,1)S(1)} %pad_maximum_fusion.27.s0), channel_id=1, source_target_pairs={{0,24},{1,25},{2,26},{3,27},{4,28},{5,29},{6,30},{7,31},{8,0},{9,1... | collective-permute-start | bytes 3538952 | tf_op jit(solution)/shard_map/ppermute | solution.py:47
  114.2 50.6 %collective-permute-start.38 = (bf16[4,2,8,24,384]{4,3,2,1,0:T(8,128)(2,1)S(1)}, bf16[4,2,8,24,384]{4,3,2,1,0:T(8,128)(2,1)}, u32[]{:S(2)}, u32[]{:S(2)}) collective-permute-start(bf16[4,2,8,24,384]{4,3,2,1,0:T(8,128)(2,1)S(1)} %pad_maximum_fusion.27.s0), channel_id=1, source_target_pairs={{0,16},{1,17},{2,18},{3,19},{4,20},{5,21},{6,22},{7,23},{8,24},{9,... | collective-permute-start | bytes 3538952 | tf_op jit(solution)/shard_map/ppermute | solution.py:47
  115.5 49.3 %collective-permute-start.37 = (bf16[4,2,8,24,384]{4,3,2,1,0:T(8,128)(2,1)S(1)}, bf16[4,2,8,24,384]{4,3,2,1,0:T(8,128)(2,1)}, u32[]{:S(2)}, u32[]{:S(2)}) collective-permute-start(bf16[4,2,8,24,384]{4,3,2,1,0:T(8,128)(2,1)S(1)} %pad_maximum_fusion.27.s0), channel_id=1, source_target_pairs={{0,8},{1,9},{2,10},{3,11},{4,12},{5,13},{6,14},{7,15},{8,16},{9,17... | collective-permute-start | bytes 3538952 | tf_op jit(solution)/shard_map/ppermute | solution.py:47
  115.8 40.7 %collective-permute-start.16 = (bf16[4,2,8,24,384]{4,3,2,1,0:T(8,128)(2,1)S(1)}, bf16[4,2,8,24,384]{4,3,2,1,0:T(8,128)(2,1)}, u32[]{:S(2)}, u32[]{:S(2)}) collective-permute-start(bf16[4,2,8,24,384]{4,3,2,1,0:T(8,128)(2,1)S(1)} %pad_maximum_fusion.25.s0), channel_id=1, source_target_pairs={{0,8},{1,9},{2,10},{3,11},{4,12},{5,13},{6,14},{7,15},{8,16},{9,17... | collective-permute-start | bytes 3538952 | tf_op jit(solution)/shard_map/ppermute | solution.py:47
  132.6 39.2 %collective-permute-start.9 = (bf16[256,768]{1,0:T(8,128)(2,1)}, bf16[256,768]{1,0:T(8,128)(2,1)S(1)}, u32[]{:S(2)}, u32[]{:S(2)}) collective-permute-start(bf16[256,768]{1,0:T(8,128)(2,1)} %collective-permute-done.8), channel_id=1, source_target_pairs={{0,32},{1,33},{2,34},{3,35},{4,36},{5,37},{6,38},{7,39},{8,40},{9,... | collective-permute-start | bytes 1179656 | tf_op jit(solution)/shard_map/ppermute | solution.py:47
  162.4 39.1 %collective-permute-start.20 = (bf16[3072,384]{1,0:T(8,128)(2,1)}, bf16[3072,384]{1,0:T(8,128)(2,1)S(1)}, u32[]{:S(2)}, u32[]{:S(2)}) collective-permute-start(bf16[3072,384]{1,0:T(8,128)(2,1)} %bitcast.642), channel_id=1, source_target_pairs={{0,32},{1,33},{2,34},{3,35},{4,36},{5,37},{6,38},{7,39},{8,40},{9,... | collective-permute-start | bytes 7077896 | tf_op jit(solution)/shard_map/ppermute | solution.py:47
  171.2 38.1 %collective-permute-start.41 = (bf16[3072,384]{1,0:T(8,128)(2,1)}, bf16[3072,384]{1,0:T(8,128)(2,1)S(1)}, u32[]{:S(2)}, u32[]{:S(2)}) collective-permute-start(bf16[3072,384]{1,0:T(8,128)(2,1)} %bitcast.640), channel_id=1, source_target_pairs={{0,32},{1,33},{2,34},{3,35},{4,36},{5,37},{6,38},{7,39},{8,40},{9,... | collective-permute-start | bytes 7077896 | tf_op jit(solution)/shard_map/ppermute | solution.py:47
  171.7 36.2 %collective-permute-start.40 = (bf16[4,768,384]{2,1,0:T(8,128)(2,1)}, bf16[4,768,384]{2,1,0:T(8,128)(2,1)S(1)}, u32[]{:S(2)}, u32[]{:S(2)}) collective-permute-start(bf16[4,768,384]{2,1,0:T(8,128)(2,1)} %bitcast.641), channel_id=1, source_target_pairs={{0,32},{1,33},{2,34},{3,35},{4,36},{5,37},{6,38},{7,39},{8,40},{9,... | collective-permute-start | bytes 7077896 | tf_op jit(solution)/shard_map/ppermute | solution.py:47
  265.5 51.5 %collective-permute-start.72 = (bf16[768,384]{1,0:T(8,128)(2,1)}, bf16[768,384]{1,0:T(8,128)(2,1)}, u32[]{:S(2)}, u32[]{:S(2)}) collective-permute-start(bf16[768,384]{1,0:T(8,128)(2,1)} %constant_dynamic-slice_fusion.1), channel_id=1, source_target_pairs={{0,32},{1,33},{2,34},{3,35},{4,36},{5,37},{6,38},{7,39},{8,40},{9,... | collective-permute-start | bytes 1769480 | tf_op jit(solution)/shard_map/ppermute | solution.py:47
  269.1 178.1 %collective-permute-start.71 = (bf16[768,1536]{1,0:T(8,128)(2,1)}, bf16[768,1536]{1,0:T(8,128)(2,1)}, u32[]{:S(2)}, u32[]{:S(2)}) collective-permute-start(bf16[768,1536]{1,0:T(8,128)(2,1)} %constant_dynamic-slice_fusion.2), channel_id=1, source_target_pairs={{0,32},{1,33},{2,34},{3,35},{4,36},{5,37},{6,38},{7,39},{8,40},{9,... | collective-permute-start | bytes 7077896 | tf_op jit(solution)/shard_map/ppermute | solution.py:47
  271.1 171.7 %collective-permute-start.73 = (bf16[3072,384]{1,0:T(8,128)(2,1)}, bf16[3072,384]{1,0:T(8,128)(2,1)}, u32[]{:S(2)}, u32[]{:S(2)}) collective-permute-start(bf16[3072,384]{1,0:T(8,128)(2,1)} %constant_dynamic-slice_fusion), channel_id=1, source_target_pairs={{0,32},{1,33},{2,34},{3,35},{4,36},{5,37},{6,38},{7,39},{8,40},{9,... | collective-permute-start | bytes 7077896 | tf_op jit(solution)/shard_map/ppermute | solution.py:47
  344.4 56.2 %collective-permute-start.82 = (bf16[768,384]{0,1:T(8,128)(2,1)}, bf16[768,384]{0,1:T(8,128)(2,1)}, u32[]{:S(2)}, u32[]{:S(2)}) collective-permute-start(bf16[768,384]{0,1:T(8,128)(2,1)} %pad_bitcast_fusion), channel_id=1, source_target_pairs={{0,32},{1,33},{2,34},{3,35},{4,36},{5,37},{6,38},{7,39},{8,40},{9,... | collective-permute-start | bytes 1769480 | tf_op jit(solution)/shard_map/ppermute | solution.py:47
  345.4 64.7 %collective-permute-start.51 = (bf16[768,384]{1,0:T(8,128)(2,1)}, bf16[768,384]{1,0:T(8,128)(2,1)}, u32[]{:S(2)}, u32[]{:S(2)}) collective-permute-start(bf16[768,384]{1,0:T(8,128)(2,1)} %constant_dynamic-slice_fusion.4), channel_id=1, source_target_pairs={{0,32},{1,33},{2,34},{3,35},{4,36},{5,37},{6,38},{7,39},{8,40},{9,... | collective-permute-start | bytes 1769480 | tf_op jit(solution)/shard_map/ppermute | solution.py:47
  435.0 56.6 %collective-permute-start.52 = (bf16[3072,384]{1,0:T(8,128)(2,1)}, bf16[3072,384]{1,0:T(8,128)(2,1)}, u32[]{:S(2)}, u32[]{:S(2)}) collective-permute-start(bf16[3072,384]{1,0:T(8,128)(2,1)} %constant_dynamic-slice_fusion.3), channel_id=1, source_target_pairs={{0,32},{1,33},{2,34},{3,35},{4,36},{5,37},{6,38},{7,39},{8,40},{9,... | collective-permute-start | bytes 7077896 | tf_op jit(solution)/shard_map/ppermute | solution.py:47
  437.9 49.1 %collective-permute-start.50 = (bf16[768,1536]{1,0:T(8,128)(2,1)}, bf16[768,1536]{1,0:T(8,128)(2,1)}, u32[]{:S(2)}, u32[]{:S(2)}) collective-permute-start(bf16[768,1536]{1,0:T(8,128)(2,1)} %constant_dynamic-slice_fusion.5), channel_id=1, source_target_pairs={{0,32},{1,33},{2,34},{3,35},{4,36},{5,37},{6,38},{7,39},{8,40},{9,... | collective-permute-start | bytes 7077896 | tf_op jit(solution)/shard_map/ppermute | solution.py:47
  482.6 33.1 %collective-permute-start.74 = (bf16[4,2,9,24,384]{4,3,2,1,0:T(8,128)(2,1)S(1)}, bf16[4,2,9,24,384]{4,3,2,1,0:T(8,128)(2,1)S(1)}, u32[]{:S(2)}, u32[]{:S(2)}) collective-permute-start(bf16[4,2,9,24,384]{4,3,2,1,0:T(8,128)(2,1)S(1)} %get-tuple-element.48), channel_id=1, source_target_pairs={{0,8},{1,9},{2,10},{3,11},{4,12},{5,13},{6,14},{7,15},{8,16},{9,17... | collective-permute-start | bytes 3981320 | tf_op jit(solution)/shard_map/ppermute | solution.py:47
  482.6 33.1 %collective-permute-start.75 = (bf16[4,2,9,24,384]{4,3,2,1,0:T(8,128)(2,1)S(1)}, bf16[4,2,9,24,384]{4,3,2,1,0:T(8,128)(2,1)S(1)}, u32[]{:S(2)}, u32[]{:S(2)}) collective-permute-start(bf16[4,2,9,24,384]{4,3,2,1,0:T(8,128)(2,1)S(1)} %get-tuple-element.49), channel_id=1, source_target_pairs={{0,16},{1,17},{2,18},{3,19},{4,20},{5,21},{6,22},{7,23},{8,24},{9,... | collective-permute-start | bytes 3981320 | tf_op jit(solution)/shard_map/ppermute | solution.py:47
  487.0 47.6 %collective-permute-start.68 = (bf16[4,24,384]{2,1,0:T(8,128)(2,1)S(1)}, bf16[4,24,384]{2,1,0:T(8,128)(2,1)S(1)}, u32[]{:S(2)}, u32[]{:S(2)}) collective-permute-start(bf16[4,24,384]{2,1,0:T(8,128)(2,1)S(1)} %dynamic-slice_bitcast_fusion.15), channel_id=1, source_target_pairs={{0,4},{1,5},{2,6},{3,7},{4,0},{5,1},{6,2},{7,3},{8,12},{9,13},{10,... | collective-permute-start | bytes 221192 | tf_op jit(solution)/shard_map/ppermute | solution.py:47
  553.6 32.2 %collective-permute-start.54 = (bf16[4,2,9,24,384]{4,3,2,1,0:T(8,128)(2,1)S(1)}, bf16[4,2,9,24,384]{4,3,2,1,0:T(8,128)(2,1)S(1)}, u32[]{:S(2)}, u32[]{:S(2)}) collective-permute-start(bf16[4,2,9,24,384]{4,3,2,1,0:T(8,128)(2,1)S(1)} %get-tuple-element.41), channel_id=1, source_target_pairs={{0,16},{1,17},{2,18},{3,19},{4,20},{5,21},{6,22},{7,23},{8,24},{9,... | collective-permute-start | bytes 3981320 | tf_op jit(solution)/shard_map/ppermute | solution.py:47
  (209 other events, 1918.7 us)

commit v2 on v1

v2 whole, which is shorter than its diff:
```python
import functools

import jax
import jax.numpy as jnp
from jax import lax
from jax.experimental import pallas as pl
from jax.experimental.pallas import tpu as pltpu
from jax.sharding import Mesh
from jax.sharding import PartitionSpec as P

HD = 64
AXES = ("xh", "core", "z", "xl", "y")
SIZES = (2, 2, 4, 2, 4)
FSDP = ("z", "xl", "y")
SEQ = ("xh", "core")
UNIT = 384
ROWS = 24
BF = jnp.bfloat16
F32 = jnp.float32
ANY = pl.BlockSpec(memory_space=pl.ANY)
SMEM = pl.BlockSpec(memory_space=pltpu.SMEM)
VMEM = pl.BlockSpec(memory_space=pltpu.VMEM)
LIGHT = pl.CostEstimate(flops=10**6, bytes_accessed=10**5, transcendentals=0)
ROOMY = pltpu.CompilerParams(vmem_limit_bytes=48 * 2**20)


def ravel(coords):
    index = 0
    for size, coord in zip(SIZES, coords):
        index = index * size + coord % size
    return index


def all_coords():
    xh_n, core_n, z_n, xl_n, y_n = SIZES
    return [
        (xh, core, z, xl, y)
        for xh in range(xh_n)
        for core in range(core_n)
        for z in range(z_n)
        for xl in range(xl_n)
        for y in range(y_n)
    ]


def shift(array, move):
    pairs = [(ravel(c), ravel(move(*c))) for c in all_coords()]
    return lax.ppermute(array, AXES, pairs)


def to_core(array):
    return shift(array, lambda xh, core, z, xl, y: (xh, core + 1, z, xl, y))


def to_xh(array):
    return shift(array, lambda xh, core, z, xl, y: (xh + 1, core, z, xl, y))


def to_xl(array):
    return shift(array, lambda xh, core, z, xl, y: (xh, core, z, xl + 1, y))


def to_next_x(array, d):
    def move(xh, core, z, xl, y):
        x = (2 * xh + xl + d) % 4
        return (x // 2, core, z, x % 2, y)

    return shift(array, move)


def to_inner(array, d):
    return shift(
        array,
        lambda xh, core, z, xl, y: (xh, core, z, xl, y + d) if core == 0 else (xh, core, z + d, xl, y),
    )


def to_outer(array, d):
    return shift(
        array,
        lambda xh, core, z, xl, y: (xh, core, z + d, xl, y) if core == 0 else (xh, core, z, xl, y + d),
    )


def nothing(*refs):
    del refs


def after(array, *deps):
    return pl.pallas_call(
        nothing,
        out_shape=jax.ShapeDtypeStruct(array.shape, array.dtype),
        in_specs=[ANY] * (1 + len(deps)),
        out_specs=ANY,
        input_output_aliases={0: 0},
    )(array, *deps)


def groups(outer):
    sets = []
    for xh in range(2):
        for core in range(2):
            for xl in range(2):
                for other in range(4):
                    along_z = (core == 0) == outer
                    sets.append(
                        [
                            ravel((xh, core, i, xl, other) if along_z else (xh, core, other, xl, i))
                            for i in range(4)
                        ]
                    )
    return sets


OUTER = groups(True)
INNER = groups(False)
PLANE = [
    [ravel((xh, core, z, xl, y)) for z in range(4) for y in range(4)]
    for xh in range(2)
    for core in range(2)
    for xl in range(2)
]


def pin(*arrays):
    return [pltpu.with_memory_space_constraint(array, pltpu.HBM) for array in arrays]


def slot_table(sign, core, absolute=False):
    z, xl, y = (lax.axis_index(n) for n in ("z", "xl", "y"))
    inner = jnp.where(core == 0, y, z)
    outer = jnp.where(core == 0, z, y)
    dq = jnp.arange(4, dtype=jnp.int32)[:, None, None]
    dp = jnp.arange(4, dtype=jnp.int32)[None, :, None]
    dx = jnp.arange(2, dtype=jnp.int32)[None, None, :]
    q = dq + 0 * outer if absolute and sign > 0 else (outer + sign * dq + 4) % 4
    if sign < 0:
        p = dp + 0 * inner if absolute else (inner - dp + 4) % 4
        x = (xl + dx) % 2
    else:
        p = dp
        x = dx
    owner = jnp.where(core == 0, q * 8 + x * 4 + p, p * 8 + x * 4 + q)
    return owner.astype(jnp.int32).reshape(32)


SLOTS = [(dq, dp, dx) for dq in range(4) for dp in range(4) for dx in range(2)]


def run_all(copies):
    for copy in copies:
        copy.start()
    for copy in copies:
        copy.wait()


def pieces_of(srcs):
    if len(srcs) == 1:
        return [srcs[0].at[dq] for dq in range(4)]
    return srcs


def assemble_kernel(n_dep, table, *refs):
    srcs, (out, sem) = refs[:4], refs[4 + n_dep :]
    copies = []
    for n, (dq, dp, dx) in enumerate(SLOTS):
        src = srcs[dq].at[dp, dx, pl.ds(0, 3)]
        copies.append(pltpu.make_async_copy(src, out.at[:, table[n]], sem.at[n]))
    run_all(copies)


def assemble(table, pieces, deps):
    return pl.pallas_call(
        functools.partial(assemble_kernel, len(deps)),
        out_shape=pltpu.HBM((3, 32, ROWS, UNIT), BF),
        in_specs=[SMEM] + [ANY] * (4 + len(deps)),
        out_specs=VMEM,
        scratch_shapes=[pltpu.SemaphoreType.DMA((32,))],
        compiler_params=ROOMY,
        cost_estimate=LIGHT,
    )(table, *pieces, *deps)


def window(f):
    return (f * 96 // 128) * 128, f * 96 % 128


def assemble_first_kernel(n_dep, table, *refs):
    srcs, (out, rows_ref, fins_ref, vun, fbuf, sem) = refs[:4], refs[4 + n_dep :]
    copies = []
    for n, (dq, dp, dx) in enumerate(SLOTS):
        src = srcs[dq].at[dp, dx]
        f = table[n]
        copies.append(pltpu.make_async_copy(src.at[3], vun.at[f], sem.at[n, 0]))
        copies.append(pltpu.make_async_copy(src.at[pl.ds(0, 3)], out.at[:, f], sem.at[n, 1]))
    run_all(copies)
    vectors = vun[...].astype(F32)
    rows_ref[...] = vectors[:, :, :128].reshape(32 * ROWS, 128).T[:32]
    fbuf[...] = jnp.zeros(fbuf.shape, F32)
    for f in range(32):
        base, off = window(f)
        piece = jnp.concatenate([vectors[f, :8, 128:256], jnp.zeros((8, 128), F32)], 1)
        if off:
            piece = pltpu.roll(piece, off, 1)
        fbuf[:, base : base + 256] += piece
    fins_ref[...] = fbuf[:, : fins_ref.shape[1]]


def assemble_first(table, pieces, deps):
    return pl.pallas_call(
        functools.partial(assemble_first_kernel, len(deps)),
        out_shape=[
            pltpu.HBM((3, 32, ROWS, UNIT), BF),
            pltpu.HBM((32, 32 * ROWS), F32),
            pltpu.HBM((8, 128 * ROWS), F32),
        ],
        in_specs=[SMEM] + [ANY] * (4 + len(deps)),
        out_specs=[VMEM] * 3,
        scratch_shapes=[
            pltpu.VMEM((32, ROWS, UNIT), BF),
            pltpu.VMEM((8, 128 * ROWS + 128), F32),
            pltpu.SemaphoreType.DMA((32, 2)),
        ],
        compiler_params=ROOMY,
        cost_estimate=LIGHT,
    )(table, *pieces, *deps)


def assemble_both_kernel(begin, core, table, table_o, *refs):
    srcs, (wide, outs, sem) = refs[:8], refs[-3:]
    copies = []
    for side, at, tab in ((0, core[0], table), (1, 1 - core[0], table_o)):
        for n, (dq, dp, dx) in enumerate(SLOTS):
            src = srcs[4 * side + dq].at[dp, dx]
            f = tab[n]
            copies.append(
                pltpu.make_async_copy(src.at[pl.ds(begin, 5)], wide.at[at, :, f], sem.at[n, side, 0])
            )
            copies.append(
                pltpu.make_async_copy(
                    src.at[pl.ds(begin + 5, 4)], outs.at[at, f], sem.at[n, side, 1]
                )
            )
    run_all(copies)


def assemble_both(begin, core, tables, pieces, others, deps):
    wide, outs = pl.pallas_call(
        functools.partial(assemble_both_kernel, begin),
        out_shape=[
            pltpu.HBM((2, 5, 32, ROWS, UNIT), BF),
            pltpu.HBM((2, 32, 4, ROWS, UNIT), BF),
        ],
        in_specs=[SMEM] * (1 + len(tables)) + [ANY] * (2 * len(pieces) + len(deps)),
        out_specs=[VMEM] * 2,
        scratch_shapes=[pltpu.SemaphoreType.DMA((32, 2, 5))],
        compiler_params=ROOMY,
        cost_estimate=LIGHT,
    )(core, *tables, *pieces, *others, *deps)
    return wide.reshape(2, 5, 32 * ROWS, UNIT), outs.reshape(2, 128 * ROWS, UNIT)


def prep_kernel(core, *refs):
    vecs, (fin, qkv, proj, fc_in, fc_out, u12, u3, vbuf, ubuf) = refs[:8], refs[8:]
    at = pl.multiple_of(core[0] * UNIT, 128)
    wide = pl.multiple_of(core[0] * 4 * UNIT, 128)
    for l in range(2):
        units = [qkv[l, :, pl.ds(at + 2 * j * UNIT, UNIT)] for j in range(3)]
        units.append(proj[l, :, pl.ds(at, UNIT)])
        units += [fc_in[l, :, pl.ds(wide + j * UNIT, UNIT)] for j in range(4)]
        rows = fc_out[l, :, pl.ds(at, UNIT)].astype(F32)
        units += [rows[j * ROWS : (j + 1) * ROWS].astype(BF) for j in range(4)]
        for j, unit in enumerate(units):
            if l == 0:
                u12[j if j < 3 else j + 1] = unit
            else:
                u3[j] = unit
    vbuf[...] = jnp.zeros(vbuf.shape, F32)
    for j, vec in enumerate(vecs):
        value = vec[...].astype(F32)
        for l in range(2):
            vbuf[l * 12 + j : l * 12 + j + 1, :ROWS] = value[l : l + 1]
    ubuf[...] = jnp.zeros(ubuf.shape, F32)
    ubuf[:, :128] = vbuf[...].T[:ROWS]
    ubuf[0:2, 128:224] = fin[...].astype(F32)
    u12[3] = ubuf[...].astype(BF)


def prep(core, arrays):
    return pl.pallas_call(
        prep_kernel,
        out_shape=[pltpu.HBM((count, ROWS, UNIT), BF) for count in (13, 12)],
        in_specs=[SMEM] + [VMEM] * 13,
        out_specs=[VMEM] * 2,
        scratch_shapes=[pltpu.VMEM((128, 128), F32), pltpu.VMEM((ROWS, UNIT), F32)],
        compiler_params=ROOMY,
        cost_estimate=LIGHT,
    )(core, *arrays)


def inner_of(pair, got, units=slice(None)):
    return jnp.stack([part[:, units] for part in [pair] + got])


def three_inner(pair):
    return [to_inner(pair, d) for d in (1, 2, 3)]


def three_outer(block):
    return [to_outer(block, d) for d in (1, 2, 3)]


def send_outer(blocks):
    return [blocks[0]] + [to_outer(blocks[d], d) for d in (1, 2, 3)]


def take_sets(sizes, refs):
    sets = []
    for size in sizes:
        sets.append(refs[:size])
        refs = refs[size:]
    return sets


def sum_outer_kernel(n_set, n_dep, place_at, *refs):
    sets, outs = take_sets(n_set, refs), refs[sum(n_set) + n_dep :]
    for d, out in enumerate(outs):
        at = lax.rem(place_at[0] + d, 4)
        begin = 0
        for parts in sets:
            count = parts[0].shape[2]
            for x in range(2):
                total = parts[0][at, x].astype(F32)
                for part in parts[1:]:
                    total = total + part[at, x].astype(F32)
                out[x, begin : begin + count] = total.astype(BF)
            begin += count


def sum_outer(place_at, sets, deps=()):
    flat = [part for parts in sets for part in parts]
    count = sum(parts[0].shape[2] for parts in sets)
    return pl.pallas_call(
        functools.partial(sum_outer_kernel, [len(s) for s in sets], len(deps)),
        out_shape=[pltpu.HBM((2, count, ROWS, UNIT), BF)] * 4,
        in_specs=[SMEM] + [VMEM] * len(flat) + [ANY] * len(deps),
        out_specs=[VMEM] * 4,
        compiler_params=ROOMY,
        cost_estimate=LIGHT,
    )(place_at, *flat, *deps)


def sum_inner_kernel(n_set, n_dep, xl, *refs):
    sets, outs = take_sets(n_set, refs), refs[sum(n_set) + n_dep :]
    for j, out in enumerate(outs):
        at = xl[0] if j == 0 else 1 - xl[0]
        begin = 0
        for parts in sets:
            count = parts[0].shape[1]
            total = parts[0][at].astype(F32)
            for part in parts[1:]:
                total = total + part[at].astype(F32)
            out[begin : begin + count] = total.astype(BF)
            begin += count


def sum_inner(xl, sets, deps=()):
    flat = [part for parts in sets for part in parts]
    count = sum(parts[0].shape[1] for parts in sets)
    return pl.pallas_call(
        functools.partial(sum_inner_kernel, [len(s) for s in sets], len(deps)),
        out_shape=[pltpu.HBM((count, ROWS, UNIT), BF)] * 2,
        in_specs=[SMEM] + [VMEM] * len(flat) + [ANY] * len(deps),
        out_specs=[VMEM] * 2,
        compiler_params=ROOMY,
        cost_estimate=LIGHT,
    )(xl, *flat, *deps)


def add_all(*parts):
    total = parts[0].astype(F32)
    for part in parts[1:]:
        total = total + part.astype(F32)
    return total.astype(BF)


def norm_parts(values):
    centred = values - jnp.mean(values, -1, keepdims=True)
    scale = lax.rsqrt(jnp.mean(centred * centred, -1, keepdims=True) + 1e-06)
    return centred * scale, scale


def layer_norm(values, gain, bias):
    return norm_parts(values)[0] * gain + bias


def norm_back(values, gain, grad):
    n, scale = norm_parts(values)
    dg = grad * gain
    out = scale * (
        dg - jnp.mean(dg, -1, keepdims=True) - n * jnp.mean(dg * n, -1, keepdims=True)
    )
    return out, jnp.sum(grad * n, 0, keepdims=True), jnp.sum(grad, 0, keepdims=True)


def fdot(a, b, ca=1, cb=0):
    return lax.dot_general(a, b, (((ca,), (cb,)), ((), ())), preferred_element_type=F32)


def lanes(rows):
    return lax.broadcasted_iota(jnp.int32, (rows, 128), 1)


def place(lane, base, columns):
    out = jnp.zeros(lane.shape, F32)
    for j, column in enumerate(columns):
        out = jnp.where(lane == base + j, column, out)
    return out


def load_qkv(units, wbuf, sem):
    return [
        pltpu.make_async_copy(units.at[j], wbuf.at[:, pl.ds(j * UNIT, UNIT)], sem.at[j])
        for j in range(3)
    ]


def three(column):
    hi = column.astype(BF).astype(F32)
    mid = (column - hi).astype(BF).astype(F32)
    return [hi, mid, column - hi - mid]


def attn_fwd_kernel(raw, row, n_dep, core, x0, x1, x2, x3, units, vec, idc, *rest):
    rest = rest[n_dep:]
    a_ref, q_ref, k_ref, v_ref, lse_ref, o32_ref, own_ref, oth_ref, wbuf, sem = rest
    copies = load_qkv(units, wbuf, sem)
    for copy in copies:
        copy.start()
    tok = x0.shape[0]
    for j, x in enumerate((x0, x1, x2, x3)):
        if raw:
            a = layer_norm(x[...].astype(F32), vec[row : row + 1, :], vec[row + 1 : row + 2, :])
            a_ref[j * tok : (j + 1) * tok, :] = a.astype(BF)
        else:
            a_ref[j * tok : (j + 1) * tok, :] = x[...]
    start = pl.multiple_of(core[0] * UNIT, 128)
    qb = vec[row + 2 : row + 3, pl.ds(start, UNIT)]
    vb = vec[row + 3 : row + 4, pl.ds(start, UNIT)]
    for copy in copies:
        copy.wait()
    k_ref[...] = fdot(a_ref[...], wbuf[:, UNIT : 2 * UNIT]).astype(BF)
    v_ref[...] = (fdot(a_ref[...], wbuf[:, 2 * UNIT :]) + vb).astype(BF)
    q_ref[...] = (fdot(a_ref[: 2 * tok, :], wbuf[:, :UNIT]) + qb).astype(BF)
    ids = idc[...]
    lane_k = lanes(4 * tok)
    lane_q = lanes(tok)
    lse_all = [jnp.zeros((tok, 128), F32) for _ in range(2)]
    for t in range(3):
        cols = slice(t * 128, (t + 1) * 128)
        tiles = [[], []]
        for hh in range(2):
            base = 64 * (1 - hh)
            sel_k = (lane_k < 64) == (hh == 0)
            sel_q = (lane_q < 64) == (hh == 0)
            kk = jnp.where(
                sel_k, k_ref[:, cols].astype(F32), place(lane_k, base, [-1e30 * (1 - ids), -1e30 * ids])
            ).astype(BF)
            vv = jnp.where(sel_k, v_ref[:, cols].astype(F32), 1.0).astype(BF)
            for b in range(2):
                rows = slice(b * tok, (b + 1) * tok)
                idq = ids[rows, :]
                qq = jnp.where(
                    sel_q,
                    q_ref[rows, cols].astype(F32) * HD**-0.5,
                    place(lane_q, base, [idq, 1 - idq]),
                ).astype(BF)
                s = fdot(qq, kk, 1, 1)
                peak = jnp.max(s, -1, keepdims=True)
                e = jnp.exp(s - peak).astype(BF)
                o = fdot(e, vv)
                total = o[:, base : base + 1]
                lse = peak + jnp.log(total)
                lse_all[b] = jnp.where(lane_q == 2 * t + hh, lse, lse_all[b])
                tiles[b].append(o / total)
        for b, out in enumerate((own_ref, oth_ref)):
            o = jnp.where(lane_q < 64, tiles[b][0], tiles[b][1])
            o32_ref[b * tok : (b + 1) * tok, cols] = o
            out[:, cols] = o.astype(BF)
    for b in range(2):
        lse_ref[b * tok : (b + 1) * tok, :] = lse_all[b]


def attn_fwd(raw, row, core, parts, units, vec, idc, deps=()):
    tok = parts[0].shape[0]
    width = parts[0].shape[1]
    sds = pltpu.HBM
    shapes = [
        sds((4 * tok, width), BF),
        sds((2 * tok, UNIT), BF),
        sds((4 * tok, UNIT), BF),
        sds((4 * tok, UNIT), BF),
        sds((2 * tok, 128), F32),
        sds((2 * tok, UNIT), F32),
        sds((tok, UNIT), BF),
        sds((tok, UNIT), BF),
    ]
    scratch = [pltpu.VMEM((width, 3 * UNIT), BF), pltpu.SemaphoreType.DMA((3,))]
    return pl.pallas_call(
        functools.partial(attn_fwd_kernel, raw, row, len(deps)),
        out_shape=shapes,
        in_specs=[SMEM] + [VMEM] * 4 + [ANY] + [VMEM] * 2 + [ANY] * len(deps),
        out_specs=[VMEM] * len(shapes),
        scratch_shapes=scratch,
        compiler_params=ROOMY,
        cost_estimate=LIGHT,
    )(core, *pin(parts[0]), *parts[1:], *pin(units, vec), idc, *deps)


def load_mlp(wide, outs, pbuf, ibuf, obuf, sem):
    proj, inner, last = [], [], []
    for side in range(2):
        cols = pl.ds(side * UNIT, UNIT)
        proj.append(pltpu.make_async_copy(wide.at[side, 0], pbuf.at[:, cols], sem.at[side, 0]))
        for j in range(4):
            at = pl.ds((side * 4 + j) * UNIT, UNIT)
            inner.append(
                pltpu.make_async_copy(wide.at[side, 1 + j], ibuf.at[:, at], sem.at[side, 1 + j])
            )
        last.append(pltpu.make_async_copy(outs.at[side], obuf.at[:, cols], sem.at[side, 5]))
    return proj, inner, last


def wait_all(copies):
    for copy in copies:
        copy.wait()


def mlp_fwd_kernel(row, last, core, x, o_own, o_oth, vec, fin, *rest):
    wide, outs_w, outs = rest[0], rest[1], rest[2:-5]
    pbuf, ibuf, obuf, full, sem = rest[-5:]
    m_ref, pack, d_ref, y_ref = outs[:4]
    proj, inner, outer = load_mlp(wide, outs_w, pbuf, ibuf, obuf, sem)
    for copy in proj + inner + outer:
        copy.start()
    width = x.shape[1]
    here = pl.multiple_of(core[0] * UNIT, 128)
    there = pl.multiple_of((1 - core[0]) * UNIT, 128)
    full[:, pl.ds(here, UNIT)] = o_own[...]
    full[:, pl.ds(there, UNIT)] = o_oth[...]
    pack[:, 5 * width :] = full[...]
    wait_all(proj)
    m = x[...].astype(F32) + (fdot(full[...], pbuf[...]) + vec[row + 4 : row + 5, :])
    m_ref[...] = m
    c = layer_norm(m, vec[row + 5 : row + 6, :], vec[row + 6 : row + 7, :]).astype(BF)
    pack[:, :width] = c
    wait_all(inner)
    total = None
    for j in range(4):
        cols = slice(j * width, (j + 1) * width)
        u = fdot(c, ibuf[:, cols]) + fin[row // 12 : row // 12 + 1, cols]
        cdf = 0.5 + 0.5 * lax.erf(u * 0.5**0.5)
        z = (u * cdf).astype(BF)
        pack[:, (j + 1) * width : (j + 2) * width] = z
        d_ref[:, cols] = (cdf + u * (jnp.exp(-0.5 * u * u) * (0.5 / jnp.pi) ** 0.5)).astype(d_ref.dtype)
        if j == 0:
            wait_all(outer)
        part = fdot(z, obuf[cols, :])
        total = part if total is None else total + part
    y = m + (total + vec[row + 7 : row + 8, :])
    y_ref[...] = y.astype(y_ref.dtype)
    if not last:
        a = layer_norm(y, vec[row + 12 : row + 13, :], vec[row + 13 : row + 14, :])
        outs[4][...] = a.astype(BF)


def mlp_scratch(width):
    return [
        pltpu.VMEM((width, width), BF),
        pltpu.VMEM((width, 4 * width), BF),
        pltpu.VMEM((4 * width, width), BF),
        pltpu.VMEM((8, 128), F32),
        pltpu.SemaphoreType.DMA((2, 6)),
    ]


def mlp_fwd(row, last, core, x, o_own, o_oth, vec, fin, weights):
    tok, width = x.shape
    sds = pltpu.HBM
    shapes = [
        sds((tok, width), F32),
        sds((tok, 6 * width), BF),
        sds((tok, 4 * width), F32),
        sds((tok, width), BF if last else F32),
    ]
    if not last:
        shapes.append(sds((tok, width), BF))
    scratch = mlp_scratch(width)
    scratch[3] = pltpu.VMEM((tok, width), BF)
    return pl.pallas_call(
        functools.partial(mlp_fwd_kernel, row, last),
        out_shape=shapes,
        in_specs=[SMEM] + [VMEM] * 5 + [ANY] * 2,
        out_specs=[VMEM] * len(shapes),
        scratch_shapes=scratch,
        compiler_params=ROOMY,
        cost_estimate=LIGHT,
    )(core, *pin(x, o_own), o_oth, *pin(vec, fin, *weights))


def norm_back_kernel(row, vec, x, gmid, da, near, far):
    grad = da[...] + near[: da.shape[0], :].astype(F32) + far[...].astype(F32)
    dx, gain_g, bias_g = norm_back(x[...].astype(F32), vec[row : row + 1, :], grad)
    return gmid[...] + dx, gain_g, bias_g


def mlp_bwd_kernel(row, first, n_dep, core, vec, m_ref, d_ref, *rest):
    n_in = 1 if first else 5
    ins, (wide, outs_w), rest = rest[:n_in], rest[n_in : n_in + 2], rest[n_in + 2 + n_dep :]
    pbuf, ibuf, obuf, full, sem = rest[-5:]
    gmid_ref, own, oth, rows_ref, fin_ref = rest[:-5]
    proj, inner, outer = load_mlp(wide, outs_w, pbuf, ibuf, obuf, sem)
    for copy in outer + inner + proj:
        copy.start()
    width = m_ref.shape[1]
    half = width // 2

    def split(value, at):
        full[:, :width] = value
        here = pl.multiple_of(core[0] * half, 128)
        there = pl.multiple_of((1 - core[0]) * half, 128)
        own[:, at : at + half] = full[:, pl.ds(here, half)]
        oth[:, at : at + half] = full[:, pl.ds(there, half)]

    rows_ref[...] = jnp.zeros(rows_ref.shape, F32)
    if first:
        gx = ins[0][...].astype(F32)
    else:
        gx, gain_g, bias_g = norm_back_kernel(row + 12, vec, *ins)
        rows_ref[8:9, :] = gain_g
        rows_ref[9:10, :] = bias_g
    gm = gx.astype(BF)
    rows_ref[7:8, :] = jnp.sum(gm.astype(F32), 0, keepdims=True)
    split(gm, 2 * width)
    wait_all(outer)
    total = None
    for j in range(4):
        cols = slice(j * width, (j + 1) * width)
        dz = fdot(gm, obuf[cols, :], 1, 1)
        gu = (d_ref[:, cols].astype(F32) * dz).astype(BF)
        full[:, cols] = gu
        fin_ref[:, cols] = jnp.sum(gu.astype(F32), 0, keepdims=True)
        if j == 0:
            wait_all(inner)
        part = fdot(gu, ibuf[:, cols], 1, 1)
        total = part if total is None else total + part
    own[:, : 2 * width] = full[:, pl.ds(pl.multiple_of(core[0] * 2 * width, 128), 2 * width)]
    oth[:, : 2 * width] = full[:, pl.ds(pl.multiple_of((1 - core[0]) * 2 * width, 128), 2 * width)]
    dm, gain_g, bias_g = norm_back(m_ref[...], vec[row + 5 : row + 6, :], total)
    rows_ref[5:6, :] = gain_g
    rows_ref[6:7, :] = bias_g
    gmid = gx + dm
    gmid_ref[...] = gmid
    ga = gmid.astype(BF)
    rows_ref[4:5, :] = jnp.sum(ga.astype(F32), 0, keepdims=True)
    split(ga, 2 * width + half)
    wait_all(proj)
    split(fdot(ga, pbuf[...], 1, 1).astype(BF), 3 * width)


def mlp_bwd(row, first, core, vec, m, d, ins, weights, deps):
    tok, width = m.shape
    sds = pltpu.HBM
    shapes = (
        [sds((tok, width), F32)]
        + [sds((tok, 7 * width // 2), BF)] * 2
        + [sds((16, width), F32), sds((1, 4 * width), F32)]
    )
    scratch = mlp_scratch(width)
    scratch[3] = pltpu.VMEM((tok, 4 * width), BF)
    return pl.pallas_call(
        functools.partial(mlp_bwd_kernel, row, first, len(deps)),
        out_shape=shapes,
        in_specs=[SMEM] + [VMEM] * (3 + len(ins)) + [ANY] * (2 + len(deps)),
        out_specs=[VMEM] * len(shapes),
        scratch_shapes=scratch,
        compiler_params=ROOMY,
        cost_estimate=LIGHT,
    )(core, *pin(vec, m, d, *ins[:3]), *ins[3:], *pin(*weights), *deps)


def last_norm_kernel(row, vec, x, gmid, da, near, far, gx_ref):
    gx_ref[...] = norm_back_kernel(row, vec, x, gmid, da, near, far)[0]


def last_norm(row, vec, ins):
    return pl.pallas_call(
        functools.partial(last_norm_kernel, row),
        out_shape=pltpu.HBM(ins[1].shape, F32),
        in_specs=[VMEM] * 6,
        out_specs=VMEM,
        compiler_params=ROOMY,
        cost_estimate=LIGHT,
    )(*pin(vec, *ins[:3]), *ins[3:])


def attn_bwd_kernel(row, n_raw, n_dep, q_ref, k_ref, v_ref, lse_ref, o32_ref, idc, *rest):
    raw, rest = rest[:n_raw], rest[n_raw:]
    (go_own, go_oth, units), rest = rest[:3], rest[3 + n_dep :]
    (
        gq_ref,
        gk_ref,
        gv_ref,
        da_own,
        da_keep,
        da_send,
        sums,
        rows_ref,
        go_ref,
        wbuf,
        sem,
    ) = rest
    tok = go_own.shape[0]
    width = units.shape[1]
    at = pl.ds(3 * width, UNIT)
    first = [
        pltpu.make_async_copy(go_own.at[:, at], go_ref.at[pl.ds(0, tok)], sem.at[3]),
        pltpu.make_async_copy(go_oth.at[:, at], go_ref.at[pl.ds(tok, tok)], sem.at[4]),
    ]
    copies = load_qkv(units, wbuf, sem)
    for copy in first + copies:
        copy.start()
    wait_all(first)
    ids = idc[...]
    near = 2 * tok
    lane_q = lanes(near)
    lane_k = lanes(near)
    for t in range(3):
        cols = slice(t * 128, (t + 1) * 128)
        gq_tile = []
        gk_tile = [[], []]
        gv_tile = [[], []]
        for hh in range(2):
            base = 64 * (1 - hh)
            h = 2 * t + hh
            sel = (lane_q < 64) == (hh == 0)
            go32 = go_ref[:, cols].astype(F32)
            inner = jnp.sum(jnp.where(sel, go32 * o32_ref[:, cols], 0.0), -1, keepdims=True)
            lse = lse_ref[:, h : h + 1]
            idq = ids[:near, :]
            qq = jnp.where(
                sel,
                q_ref[:, cols].astype(F32) * HD**-0.5,
                place(lane_q, base, [idq, 1 - idq] + three(-lse)),
            ).astype(BF)
            gg = jnp.where(sel, go32, place(lane_q, base, three(-inner))).astype(BF)
            gq = None
            for b in range(2):
                rows = slice(b * near, (b + 1) * near)
                idk = ids[rows, :]
                kk = jnp.where(
                    sel,
                    k_ref[rows, cols].astype(F32),
                    place(lane_k, base, [-1e30 * (1 - idk), -1e30 * idk, 1.0, 1.0, 1.0]),
                ).astype(BF)
                vv = jnp.where(
                    sel, v_ref[rows, cols].astype(F32), place(lane_k, base, [1.0, 1.0, 1.0])
                ).astype(BF)
                prob = jnp.exp(fdot(kk, qq, 1, 1))
                gs = (prob * fdot(vv, gg, 1, 1)).astype(BF)
                gv_tile[b].append(fdot(prob.astype(BF), go_ref[:, cols]))
                gk_tile[b].append(fdot(gs, q_ref[:, cols]))
                part = fdot(gs, k_ref[rows, cols], 0, 0)
                gq = part if gq is None else gq + part
            gq_tile.append(gq)
        left = lane_q < 64
        gq_ref[:, cols] = (jnp.where(left, gq_tile[0], gq_tile[1]) * HD**-0.5).astype(BF)
        for b in range(2):
            rows = slice(b * near, (b + 1) * near)
            gk_ref[rows, cols] = (jnp.where(left, *gk_tile[b]) * HD**-0.5).astype(BF)
            gv_ref[rows, cols] = jnp.where(left, *gv_tile[b]).astype(BF)
    for copy in copies:
        copy.wait()
    far = fdot(gk_ref[near:, :], wbuf[:, UNIT : 2 * UNIT], 1, 1) + fdot(
        gv_ref[near:, :], wbuf[:, 2 * UNIT :], 1, 1
    )
    da_keep[...] = far[:tok]
    da_send[tok:, :] = far[tok:].astype(BF)
    own = (
        fdot(gk_ref[:near, :], wbuf[:, UNIT : 2 * UNIT], 1, 1)
        + fdot(gv_ref[:near, :], wbuf[:, 2 * UNIT :], 1, 1)
        + fdot(gq_ref[...], wbuf[:, :UNIT], 1, 1)
    )
    da_own[...] = own[:tok]
    da_send[:tok, :] = own[tok:].astype(BF)
    rows_ref[...] = jnp.zeros(rows_ref.shape, F32)
    if raw:
        gain_g, bias_g = 0.0, 0.0
        for x, grad in zip(raw, (own[:tok], own[tok:], far[:tok], far[tok:])):
            n = norm_parts(x[...].astype(F32))[0]
            gain_g = gain_g + jnp.sum(grad * n, 0, keepdims=True)
            bias_g = bias_g + jnp.sum(grad, 0, keepdims=True)
        rows_ref[0:1, :] = gain_g
        rows_ref[1:2, :] = bias_g
    sums[...] = jnp.zeros(sums.shape, F32)
    sums[0:1, :] = jnp.sum(gq_ref[...].astype(F32), 0, keepdims=True)
    sums[1:2, :] = jnp.sum(gv_ref[...].astype(F32), 0, keepdims=True)


def attn_bwd(row, saved, raw, go_own, go_oth, idc, units, deps):
    tok = go_own.shape[0]
    width = units.shape[1]
    sds = pltpu.HBM
    shapes = [
        sds((2 * tok, UNIT), BF),
        sds((4 * tok, UNIT), BF),
        sds((4 * tok, UNIT), BF),
        sds((tok, width), F32),
        sds((tok, width), F32),
        sds((2 * tok, width), BF),
        sds((8, UNIT), F32),
        sds((8, width), F32),
    ]
    return pl.pallas_call(
        functools.partial(attn_bwd_kernel, row, len(raw), len(deps)),
        out_shape=shapes,
        in_specs=[VMEM] * (6 + len(raw)) + [ANY] * (3 + len(deps)),
        out_specs=[VMEM] * len(shapes),
        scratch_shapes=[
            pltpu.VMEM((2 * tok, UNIT), BF),
            pltpu.VMEM((width, 3 * UNIT), BF),
            pltpu.SemaphoreType.DMA((5,)),
        ],
        compiler_params=ROOMY,
        cost_estimate=LIGHT,
    )(*pin(*saved, idc, *raw, go_own), go_oth, *pin(units), *deps)


def deal(table, outs, buf, value, j, at):
    buf[at] = value.reshape(32, ROWS, UNIT)
    for dq, out in enumerate(outs):
        for p in range(4):
            for x in range(2):
                out[p, x, j] = buf[at, table[dq * 8 + p * 2 + x]].astype(BF)


def blocks_shape(count):
    return [pltpu.HBM((4, 2, count, ROWS, UNIT), BF)] * 4


def qkv_grad_kernel(with_vec, n_dep, table, core, a_ref, gq, gk, gv, *rest):
    n_vec = 7 if with_vec else 0
    vecs, rest = rest[:n_vec], rest[n_vec + n_dep :]
    outs, buf = rest[:4], rest[4]
    near = gq.shape[0]
    deal(table, outs, buf, fdot(a_ref[:near, :], gq[...], 0, 0), 0, 0)
    deal(table, outs, buf, fdot(a_ref[...], gk[...], 0, 0), 1, 1)
    deal(table, outs, buf, fdot(a_ref[...], gv[...], 0, 0), 2, 0)
    if with_vec:
        vbuf, tbuf, fbuf, wbuf = rest[5:9]
        rows0, rows1, sums0, sums1, fin0, fin1, norm0 = vecs
        vbuf[...] = jnp.zeros(vbuf.shape, F32)
        fbuf[...] = jnp.zeros(fbuf.shape, F32)
        cols = pl.ds(pl.multiple_of(core[0] * UNIT, 128), UNIT)
        vbuf[0:2, :] = norm0[0:2, :]
        vbuf[12:14, :] = rows0[8:10, :]
        for l, (rows, sums, fin) in enumerate(((rows0, sums0, fin0), (rows1, sums1, fin1))):
            vbuf[l * 12 + 2 : l * 12 + 3, cols] = sums[0:1, :]
            vbuf[l * 12 + 3 : l * 12 + 4, cols] = sums[1:2, :]
            vbuf[l * 12 + 4 : l * 12 + 8, :] = rows[4:8, :]
            fbuf[l : l + 1, : fin.shape[1]] = fin[...]
        tbuf[...] = vbuf[...].T.reshape(32, ROWS, 128)
        wbuf[...] = jnp.zeros(wbuf.shape, F32)
        for f in range(32):
            base, off = window(f)
            piece = fbuf[:, base : base + 256]
            if off:
                piece = pltpu.roll(piece, 256 - off, 1)
            wbuf[f, :8, :] = piece[:, :128]
        none = jnp.zeros((ROWS, 128), F32)
        for n, (dq, p, x) in enumerate(SLOTS):
            unit = jnp.concatenate([tbuf[table[n]], wbuf[table[n]], none], 1)
            outs[dq][p, x, 3] = unit.astype(BF)


def qkv_grad(table, core, a_all, gq, gk, gv, vecs, deps):
    count = 4 if vecs else 3
    scratch = [pltpu.VMEM((2, 32, ROWS, UNIT), F32)]
    if vecs:
        scratch += [
            pltpu.VMEM((128, a_all.shape[1]), F32),
            pltpu.VMEM((32, ROWS, 128), F32),
            pltpu.VMEM((8, 4 * a_all.shape[1] + 128), F32),
            pltpu.VMEM((32, ROWS, 128), F32),
        ]
    return pl.pallas_call(
        functools.partial(qkv_grad_kernel, bool(vecs), len(deps)),
        out_shape=blocks_shape(count),
        in_specs=[SMEM] * 2 + [VMEM] * (4 + len(vecs)) + [ANY] * len(deps),
        out_specs=[VMEM] * 4,
        scratch_shapes=scratch,
        compiler_params=ROOMY,
        cost_estimate=LIGHT,
    )(table, core, *pin(a_all, gq, gk, gv, *vecs), *deps)


def mlp_grad_kernel(joint, table, f0, f1, b0, b1, *rest):
    if joint:
        dests, (out, sem, buf, obuf) = rest[4:8], rest[8:]
    else:
        out, buf, obuf = rest
    outs = [out.at[q] for q in range(4)]
    width = f0.shape[1] // 6

    def both(lc, rc):
        return fdot(f0[:, lc], b0[:, rc], 0, 0) + fdot(f1[:, lc], b1[:, rc], 0, 0)

    def cols(begin, size):
        return slice(begin, begin + size)

    for j in range(4):
        deal(table, outs, buf, both(cols(0, width), cols(j * UNIT, UNIT)), j, j % 2)
    ga = cols(2 * width + UNIT, UNIT)
    deal(table, outs, buf, both(cols(5 * width, width), ga), 4, 0)
    for j in range(4):
        part = both(cols((j + 1) * width, width), cols(2 * width, UNIT))
        obuf[j * 8 : (j + 1) * 8] = part.reshape(8, 4, ROWS, UNIT)
    for n, (dq, p, x) in enumerate(SLOTS):
        outs[dq][p, x, pl.ds(5, 4)] = obuf[table[n]].astype(BF)
    if joint:
        spread_units(out, dests, sem, 0)


def mlp_grad(table, packs, joint=()):
    more = len(joint)
    blocks = (4, 4, 2, 9, ROWS, UNIT)
    scratch = [
        pltpu.VMEM((2, 32, ROWS, UNIT), F32),
        pltpu.VMEM((32, 4, ROWS, UNIT), F32),
    ]
    if more:
        scratch = [pltpu.VMEM(blocks, BF), pltpu.SemaphoreType.DMA((4,))] + scratch
    return pl.pallas_call(
        functools.partial(mlp_grad_kernel, more),
        out_shape=blocks_shape(12) if more else pltpu.HBM(blocks, BF),
        in_specs=[SMEM] + [VMEM] * 4 + [ANY] * more,
        out_specs=[ANY] * 4 if more else VMEM,
        input_output_aliases={5 + i: i for i in range(more)},
        scratch_shapes=scratch,
        compiler_params=ROOMY,
        cost_estimate=LIGHT,
    )(table, *pin(packs[0]), packs[1], *pin(packs[2]), packs[3], *joint)


def spread_units(out, dests, sem, begin):
    count = out.shape[3]
    run_all(
        [
            pltpu.make_async_copy(out.at[q], dest.at[:, :, pl.ds(begin, count)], sem.at[q])
            for q, dest in enumerate(dests)
        ]
    )


def qkv_grad_rest_kernel(n_dep, table, a_ref, gq, gk, gv, *rest):
    rest = rest[n_dep:]
    dests, (out, buf, sem) = rest[:4], rest[4:]
    outs = [out.at[q] for q in range(4)]
    near = gq.shape[0]
    deal(table, outs, buf, fdot(a_ref[:near, :], gq[...], 0, 0), 0, 0)
    deal(table, outs, buf, fdot(a_ref[...], gk[...], 0, 0), 1, 1)
    deal(table, outs, buf, fdot(a_ref[...], gv[...], 0, 0), 2, 0)
    spread_units(out, dests, sem, 9)


def qkv_grad_rest(table, a_all, gq, gk, gv, deps):
    return pl.pallas_call(
        functools.partial(qkv_grad_rest_kernel, len(deps)),
        out_shape=blocks_shape(12),
        in_specs=[SMEM] + [VMEM] * 4 + [ANY] * len(deps),
        out_specs=[ANY] * 4,
        scratch_shapes=[
            pltpu.VMEM((4, 4, 2, 3, ROWS, UNIT), BF),
            pltpu.VMEM((2, 32, ROWS, UNIT), F32),
            pltpu.SemaphoreType.DMA((4,)),
        ],
        compiler_params=ROOMY,
        cost_estimate=LIGHT,
    )(table, *pin(a_all, gq, gk, gv), *deps)


def reduce_along(blocks, sets):
    flat = blocks.reshape(-1, ROWS, UNIT)
    got = lax.psum_scatter(flat, AXES, scatter_dimension=0, axis_index_groups=sets, tiled=True)
    return got.reshape(blocks.shape[1:])


def gather_along(block, sets):
    flat = block.reshape(-1, ROWS, UNIT)
    got = lax.all_gather(flat, AXES, axis=0, axis_index_groups=sets, tiled=True)
    return got.reshape(4, *block.shape)


def finish_kernel(core, own0, oth0, own1, oth1, *rest):
    qkv, proj, fc_in, fc_out, fin = rest[:5]
    vecs, vbuf = rest[5:13], rest[13]
    first = core[0] == 0
    for l, (own, oth) in enumerate(((own0, oth0), (own1, oth1))):

        def put(out, rows, at, unit, own=own, oth=oth):
            lo = jnp.where(first, own[unit], oth[unit]).astype(F32)
            hi = jnp.where(first, oth[unit], own[unit]).astype(F32)
            out[l, rows, at[0] : at[0] + UNIT] = lo
            out[l, rows, at[1] : at[1] + UNIT] = hi

        every = slice(0, ROWS)
        for j in range(4):
            put(fc_in, every, (j * UNIT, (j + 4) * UNIT), j)
            put(fc_out, slice(j * ROWS, (j + 1) * ROWS), (0, UNIT), 5 + j)
        put(proj, every, (0, UNIT), 4)
        for j in range(3):
            at = 12 + j if l == 0 else 9 + j
            put(qkv, every, (2 * j * UNIT, (2 * j + 1) * UNIT), at, own0, oth0)
    both = own0[15].astype(F32) + oth0[15].astype(F32)
    fin[...] = both[0:2, 128:224]
    vbuf[...] = jnp.zeros(vbuf.shape, F32)
    vbuf[:ROWS, :] = both[:, :128]
    turned = vbuf[...].T
    for j, vec in enumerate(vecs):
        for l in range(2):
            vec[l : l + 1, :] = turned[l * 12 + j : l * 12 + j + 1, :ROWS]


def finish(core, parts):
    sds = jax.ShapeDtypeStruct
    width = 2 * UNIT
    return pl.pallas_call(
        finish_kernel,
        out_shape=[
            sds((2, ROWS, 3 * width), F32),
            sds((2, ROWS, width), F32),
            sds((2, ROWS, 4 * width), F32),
            sds((2, 4 * ROWS, width), F32),
            sds((2, 4 * ROWS), F32),
        ]
        + [sds((2, ROWS), F32)] * 8,
        in_specs=[SMEM] + [VMEM] * 4,
        out_specs=[VMEM] * 13,
        scratch_shapes=[pltpu.VMEM((128, 128), F32)],
        compiler_params=ROOMY,
        cost_estimate=LIGHT,
    )(core, *parts)


def body(
    tokens,
    image_ids,
    cotangent,
    attn_norm_gain,
    attn_norm_bias,
    qkv_weight,
    query_bias,
    value_bias,
    proj_weight,
    proj_bias,
    mlp_norm_gain,
    mlp_norm_bias,
    fc_in_weight,
    fc_in_bias,
    fc_out_weight,
    fc_out_bias,
):
    core, xh, xl = (lax.axis_index(n) for n in ("core", "xh", "xl"))
    width = tokens.shape[2]
    tok = tokens.shape[1]

    one = core.astype(jnp.int32).reshape(1)
    xl_one = xl.astype(jnp.int32).reshape(1)
    z, y = lax.axis_index("z"), lax.axis_index("y")
    inner_at = jnp.where(core == 0, y, z).astype(jnp.int32).reshape(1)
    table = slot_table(-1, core)
    table_o = slot_table(-1, 1 - core)
    table_out = slot_table(1, core)
    table_abs = slot_table(-1, core, True)
    table_abs_o = slot_table(-1, 1 - core, True)
    table_sum = slot_table(1, core, True)

    def segment(dx, dc):
        return lax.dynamic_slice_in_dim(
            image_ids[0], (((xh + dx) % 2) * 2 + (core + dc) % 2) * tok, tok, 0
        )

    ids = jnp.concatenate([segment(0, 0), segment(0, 1), segment(1, 0), segment(1, 1)])
    idc = ids.astype(F32)[:, None]

    u12, u3 = prep(
        one,
        pin(
            attn_norm_gain,
            attn_norm_bias,
            query_bias,
            value_bias,
            proj_bias,
            mlp_norm_gain,
            mlp_norm_bias,
            fc_out_bias,
            fc_in_bias,
            qkv_weight,
            proj_weight,
            fc_in_weight,
            fc_out_weight,
        ),
    )
    tokens_own = tokens[0]
    u12_far = to_xl(u12)
    p1 = jnp.stack([u12[:4], u12_far[:4]])
    p2 = jnp.stack([u12[4:], u12_far[4:]])
    tokens_far = to_xh(tokens_own)
    share = [tokens_own, to_core(tokens_own), tokens_far, to_core(tokens_far)]
    s1 = three_inner(p1)
    inner1 = after(inner_of(p1, s1), tokens_far)
    pieces1 = [inner1] + three_outer(inner1)
    p2 = after(p2, *pieces1[1:])
    u3 = after(u3, inner1)
    p3 = jnp.stack([u3, to_xl(u3)])
    p3 = after(p3, *pieces1[1:])
    inner3 = gather_along(p3, INNER)
    s2 = three_inner(p2)
    qkv0, vec_rows, fins = assemble_first(table, pieces1, [p2, p3])
    qkv0 = qkv0.reshape(3, width, UNIT)
    fwd0 = attn_fwd(True, 0, one, share, qkv0, vec_rows, idc)
    o_own, o_oth = fwd0[6:]
    o_got = to_core(o_oth)
    inner2 = inner_of(p2, [after(part, o_own) for part in s2])
    pieces2 = [inner2] + three_outer(inner2)
    others2 = [to_core(piece) for piece in pieces2]
    inner3 = after(after(inner3, o_own), *pieces2[1:])
    pieces3 = [inner3] + three_outer(inner3)
    full0 = assemble_both(0, one, [table, table_o], pieces2, others2, [o_got, inner3])
    m0, pack0, d0, x1, a1 = mlp_fwd(0, False, one, tokens_own, o_own, o_got, vec_rows, fins, full0)
    pack0_o = to_core(pack0)
    a1_far = to_xh(a1)
    share1 = [a1, to_core(a1), a1_far, to_core(a1_far)]
    pieces3 = [inner3] + [after(piece, x1) for piece in pieces3[1:]]
    qkv1 = assemble(table_abs, pieces3, []).reshape(3, width, UNIT)
    fwd1 = attn_fwd(False, 12, one, share1, qkv1, vec_rows, idc, [pack0_o])
    o_own, o_oth = fwd1[6:]
    o_got = to_core(o_oth)
    others3 = [to_core(part) for part in pieces3]
    full1 = assemble_both(3, one, [table_abs, table_abs_o], pieces3, others3, [o_got])
    m1, pack1, d1, block_output = mlp_fwd(12, True, one, x1, o_own, o_got, vec_rows, fins, full1)
    pack1_o = to_core(pack1)

    gmid1, own1, oth1, rows1, fing1 = mlp_bwd(
        12, True, one, vec_rows, m1, d1, [cotangent[0]], full1, [block_output]
    )
    got1 = to_core(oth1)
    block_a = mlp_grad(table_sum, [pack1, pack1_o, own1, got1])
    sum_a = reduce_along(block_a, OUTER)
    gq, gk, gv, da, da_keep, da_send, sums1, _ = attn_bwd(
        12, fwd1[1:6], [], own1, got1, idc, qkv1, [block_a]
    )
    da_got = to_core(da_send)
    far_in = (da_keep + da_got[tok:].astype(F32)).astype(BF)
    far = to_xh(far_in)
    block_e = qkv_grad_rest(table_out, fwd1[0], gq, gk, gv, [far_in])

    gmid0, own0, oth0, rows0, fing0 = mlp_bwd(
        0, False, one, vec_rows, m0, d0, [x1, gmid1, da, da_got, far], full0, block_e
    )
    got0 = to_core(oth0)
    sum_a = after(sum_a, gmid0)
    mid_a = sum_a
    sum_a = reduce_along(sum_a, INNER)
    block_b = mlp_grad(table_out, [pack0, pack0_o, own0, got0], block_e)
    sent_b = send_outer(block_b)
    gq, gk, gv, da, da_keep, da_send, sums0, norm0 = attn_bwd(
        0, fwd0[1:6], share, own0, got0, idc, qkv0, [block_b[0], mid_a]
    )
    da_got = to_core(da_send)
    far = to_xh((da_keep + da_got[tok:].astype(F32)).astype(BF))

    vecs = [rows0, rows1, sums0, sums1, fing0, fing1, norm0]
    block_c = qkv_grad(table_out, one, fwd0[0], gq, gk, gv, vecs, [])
    sent_c = send_outer(block_c)
    gx = last_norm(0, vec_rows, [tokens_own, gmid0, da, da_got, far])
    mine_a, other_a = sum_inner(xl_one, [[sum_a]], [block_c[0]])
    part_a = add_all(mine_a, to_xl(other_a))
    part_a = add_all(part_a, to_xh(part_a))
    part_a_o = to_core(part_a)
    sum_bc = sum_outer(inner_at, [sent_b, sent_c], [far, other_a])
    sent_bc = [sum_bc[0]] + [to_inner(sum_bc[d], d) for d in (1, 2, 3)]
    mine_bc, other_bc = sum_inner(xl_one, [sent_bc], [gx])
    part_bc = add_all(mine_bc, to_xl(other_bc))
    part_bc = add_all(part_bc, to_xh(part_bc))
    done = finish(one, [part_bc, to_core(part_bc), part_a, part_a_o])
    qkv_g, proj_g, fc_in_g, fc_out_g, fin_g = done[:5]
    vec_g = done[5:]
    return (
        block_output[None],
        gx[None],
        vec_g[0],
        vec_g[1],
        qkv_g,
        vec_g[2],
        vec_g[3],
        proj_g,
        vec_g[4],
        vec_g[5],
        vec_g[6],
        fc_in_g,
        fin_g,
        fc_out_g,
        vec_g[7],
    )


def solution(mesh):
    fine = Mesh(mesh.devices.reshape(SIZES), AXES)
    row = P(None, FSDP)
    mat = P(None, FSDP, None)
    tok = P(FSDP, SEQ, None)
    return jax.shard_map(
        body,
        mesh=fine,
        in_specs=(
            tok,
            P(FSDP, None),
            tok,
            row,
            row,
            mat,
            row,
            row,
            mat,
            row,
            row,
            row,
            mat,
            row,
            mat,
            row,
        ),
        out_specs=(tok, tok, row, row, mat, row, row, mat, row, row, row, mat, row, mat, row),
        check_vma=False,
    )
```

time: 634 us -> 426 us (0.67)
  Pallas kernels: 28 us -> 180 us
  matrix products: 137 us -> 0 us
  other arithmetic: 80.6 us -> 14.3 us
  waiting for transfers between devices: 167 us -> 101 us
  local copies, waits for them, and re-layouts: 79.8 us -> 25 us
  starting transfers between devices: 127 us -> 86.1 us
  between operations: 3.83 us -> 14.8 us
    pallas_call x8 -> x35, Pallas kernels: 28 us -> 180 us  [the longest x2 33.8 us: attn_bwd(): pl.pallas_call(functools.partial(attn_bwd_kernel, row, len(raw), len(deps...]
    dot_general x48 -> x0, matrix products: 137 us -> none  [the longest x12 33.1 us: dot(): return jnp.dot(a, b, preferred_element_type=F32)]
    ppermute x92 -> x56, waiting for transfers between devices: 167 us -> 101 us  [shift(): return lax.ppermute(array, AXES, pairs)]
    ppermute x92 -> x56, starting transfers between devices: 127 us -> 85.3 us  [shift(): return lax.ppermute(array, AXES, pairs)]
    convert_element_type x24 -> x4, other arithmetic: 24.1 us -> 1.21 us  [add_all(): return total.astype(BF)]
    another operation x32 -> x5, other arithmetic: 21.2 us -> 6.02 us  [the longest x3 3.51 us: inner_of(): return jnp.stack([part[:, units] for part in [pair] + got])]
    dynamic_slice x16 -> x0, local copies, waits for them, and re-layouts: 14.7 us -> none  [the longest x6 11.7 us: halves(): lax.dynamic_slice_in_dim(grad, (1 - core) * (grad.shape[1] // 2), grad.sh...]
    slice x24 -> x0, local copies, waits for them, and re-layouts: 14 us -> none  [the longest x2 2.99 us: weights(): wq, wk, wv, proj_h = (attn[j].reshape(width, UNIT) for j in range(4))]
  transfers between devices with their start and end apart: 92 -> 59, of which waited for: 37 -> 22; matrix products, arithmetic and copies ran while one was open for 38% -> 5% of each run, Pallas kernels for 4% -> 33%
where the time goes in v2:
time: 426 us; the launch traced here: 421 us
  Pallas kernels  180 us (42%)
  waiting for transfers between devices  101 us (24%)
  starting transfers between devices  86.1 us (20%)
  local copies, waits for them, and re-layouts  25 us (6%)
  between operations  14.8 us (3%)
  other arithmetic  14.3 us (3%)
    ppermute x56, waiting for transfers between devices, shift(): return lax.ppermute(array, AXES, pairs)  101 us
    ppermute x56, starting transfers between devices, shift(): return lax.ppermute(array, AXES, pairs)  85.3 us
    pallas_call x2, Pallas kernels, attn_bwd(): pl.pallas_call(functools.partial(attn_bwd_kernel, row, len(raw), len(deps...  33.8 us
    pallas_call x2, Pallas kernels, attn_fwd(): pl.pallas_call(functools.partial(attn_fwd_kernel, raw, row, len(deps)), o...  25.2 us
    pallas_call x2, Pallas kernels, assemble_both(): pl.pallas_call(functools.partial(assemble_both_kernel, begin), out_shape=...  24.8 us
    pallas_call x2, Pallas kernels, mlp_bwd(): pl.pallas_call(functools.partial(mlp_bwd_kernel, row, first, len(deps)),...  23.3 us
    pallas_call x2, Pallas kernels, mlp_fwd(): pl.pallas_call(functools.partial(mlp_fwd_kernel, row, last), out_shape=sh...  21.4 us
    unnamed x84, local copies, waits for them, and re-layouts  20.1 us
  transfers between devices with their start and end apart: 59, of which 22 were waited for; matrix products, arithmetic and copies ran while one was open for 5% of the time, Pallas kernels for 33%

profile of v2, /device:TPU:1, one launch (start us, length us, event | category | flops | bytes accessed | tf_op | source)
XLA Modules:
  0.0 420.6 jit_solution(3579656746007324449)
XLA Ops:
  16.7 8.3 %collective-permute-done.3 = bf16[13,24,384]{2,1,0:T(8,128)(2,1)S(1)} collective-permute-done((bf16[13,24,384]{2,1,0:T(8,128)(2,1)}, bf16[13,24,384]{2,1,0:T(8,128)(2,1)S(1)}, u32[]{:S(2)}, u32[]{:S(2)}) %collective-permute-start.3) | collective-permute-done | bytes 239648 | tf_op jit(solution)/shard_map/ppermute | solution.py:48
  68.8 12.8 %shard_map.277 = (bf16[1024,768]{1,0:T(8,128)(2,1)}, bf16[512,384]{1,0:T(8,128)(2,1)}, bf16[1024,384]{1,0:T(8,128)(2,1)}, bf16[1024,384]{1,0:T(8,128)(2,1)}, f32...) custom-call(s32[1]{0:T(128)} %bitcast.core, ...), custom_call_target="tpu_custom_call" | custom-call | flops 1000000 | bytes 100000 | tf_op jit(solution)/shard_map/pallas_call | solution.py:509
  91.0 10.4 %collective-permute-done.17.refs_3_ = bf16[4,2,9,24,384]{4,3,2,1,0:T(8,128)(2,1)S(1)} collective-permute-done((bf16[4,2,9,24,384]{4,3,2,1,0:T(8,128)(2,1)}, bf16[4,2,9,24,384]{4,3,2,1,0:T(8,128)(2,1)S(1)}, u32[]{:S(2)}, u32[]{:S(2)}) %collective-permute-start.17) | collective-permute-done | bytes 1327136 | tf_op jit(solution)/shard_map/ppermute | solution.py:48
  101.5 5.5 %collective-permute-start.21 = (bf16[4,2,9,24,384]{4,3,2,1,0:T(8,128)(2,1)S(1)}, bf16[4,2,9,24,384]{4,3,2,1,0:T(8,128)(2,1)}, u32[]{:S(2)}, u32[]{:S(2)}) collective-permute-start(bf16[4,2,9,24,384]{4,3,2,1,0:T(8,128)(2,1)S(1)} %collective-permute-done.17.refs_3_), channel_id=1, source_target_pairs={{0,32},{1,33},{2,34},{3,35},{4,36},{5,37},{6,38},{7,39},{8,40},{9,... | collective-permute-start | bytes 3981320 | tf_op jit(solution)/shard_map/ppermute | solution.py:48
  107.1 11.0 %collective-permute-done.15.refs_1_ = bf16[4,2,9,24,384]{4,3,2,1,0:T(8,128)(2,1)} collective-permute-done((bf16[4,2,9,24,384]{4,3,2,1,0:T(8,128)(2,1)}, bf16[4,2,9,24,384]{4,3,2,1,0:T(8,128)(2,1)}, u32[]{:S(2)}, u32[]{:S(2)}) %collective-permute-start.15) | collective-permute-done | bytes 1327136 | tf_op jit(solution)/shard_map/ppermute | solution.py:48
  119.0 6.3 %collective-permute-start.20 = (bf16[4,2,9,24,384]{4,3,2,1,0:T(8,128)(2,1)}, bf16[4,2,9,24,384]{4,3,2,1,0:T(8,128)(2,1)S(1)}, u32[]{:S(2)}, u32[]{:S(2)}) collective-permute-start(bf16[4,2,9,24,384]{4,3,2,1,0:T(8,128)(2,1)} %copy-done.15), channel_id=1, source_target_pairs={{0,32},{1,33},{2,34},{3,35},{4,36},{5,37},{6,38},{7,39},{8,40},{9,... | collective-permute-start | bytes 3981320 | tf_op jit(solution)/shard_map/ppermute | solution.py:48
  133.7 12.2 %shard_map.283 = (bf16[2,5,32,24,384]{4,3,2,1,0:T(8,128)(2,1)}, bf16[2,32,4,24,384]{4,3,2,1,0:T(8,128)(2,1)}) custom-call(s32[1]{0:T(128)} %bitcast.core, s32[32]{0:T(128)S(1)} %select_n.201.table, s32[32]{0:T(128)S(1)} %select_n.216.table_o, bf16[4,2,9,24,384]{4,3,2,1,0:T(8,128)(2,1)} %pad_maximum_fusion.refs_0_, ...), custom_call_target="tpu_custom_call" | custom-call | flops 1000000 | bytes 100000 | tf_op jit(solution)/shard_map/pallas_call | solution.py:248
  146.0 10.8 %shard_map.284 = (f32[256,768]{1,0:T(8,128)}, bf16[256,4608]{1,0:T(8,128)(2,1)}, f32[256,3072]{1,0:T(8,128)}, f32[256,768]{1,0:T(8,128)}, bf16[256,768]{1,0:T(8,128)(2,1)}) custom-call(s32[1]{0:T(128)} %bitcast.core, bf16[256,768]{1,0:T(8,128)(2,1)} %bitcast.70, bf16[256,384]{1,0:T(8,128)(2,1)} %get-tuple-element.111.refs_1_.o_own, ...), custom_call_target="tpu_custom_call" | custom-call | flops 1000000 | bytes 100000 | tf_op jit(solution)/shard_map/pallas_call | solution.py:600
  159.1 10.5 %collective-permute-done.23.x2 = bf16[256,768]{1,0:T(8,128)(2,1)} collective-permute-done((bf16[256,768]{1,0:T(8,128)(2,1)}, bf16[256,768]{1,0:T(8,128)(2,1)}, u32[]{:S(2)}, u32[]{:S(2)}) %collective-permute-start.23) | collective-permute-done | bytes 393248 | tf_op jit(solution)/shard_map/ppermute | solution.py:48
  180.7 12.4 %shard_map.289 = (bf16[1024,768]{1,0:T(8,128)(2,1)}, bf16[512,384]{1,0:T(8,128)(2,1)}, bf16[1024,384]{1,0:T(8,128)(2,1)}, bf16[1024,384]{1,0:T(8,128)(2,1)}, f32...) custom-call(s32[1]{0:T(128)} %bitcast.core, ...), custom_call_target="tpu_custom_call" | custom-call | flops 1000000 | bytes 100000 | tf_op jit(solution)/shard_map/pallas_call | solution.py:509
  195.2 12.5 %shard_map.290 = (bf16[2,5,32,24,384]{4,3,2,1,0:T(8,128)(2,1)}, bf16[2,32,4,24,384]{4,3,2,1,0:T(8,128)(2,1)}) custom-call(s32[1]{0:T(128)} %bitcast.core, s32[32]{0:T(128)S(1)} %select_n.218.table, s32[32]{0:T(128)S(1)} %select_n.220.table_o, bf16[4,2,12,24,384]{4,3,2,1,0:T(8,128)(2,1)S(1)} %copy-done, bf16[4,2,12,24,384]{4,3,2,1,0:T(8,128)(2,1)} %shard_map.285.refs_1_, ...), custom_call_target="tpu_custom_call" | custom-call | flops 1000000 | bytes 100000 | tf_op jit(solution)/shard_map/pallas_call | solution.py:248
  207.7 10.5 %shard_map.291 = (f32[256,768]{1,0:T(8,128)}, bf16[256,4608]{1,0:T(8,128)(2,1)}, f32[256,3072]{1,0:T(8,128)}, bf16[256,768]{1,0:T(8,128)(2,1)}) custom-call(s32[1]{0:T(128)} %bitcast.core, f32[256,768]{1,0:T(8,128)} %get-tuple-element.116.refs_1_.x.rest_0_, bf16[256,384]{1,0:T(8,128)(2,1)} %get-tuple-element.119.o_own, ...), custom_call_target="tpu_custom_call" | custom-call | flops 1000000 | bytes 100000 | tf_op jit(solution)/shard_map/pallas_call | solution.py:600
  219.5 11.2 %shard_map.292 = (f32[256,768]{1,0:T(8,128)}, bf16[256,2688]{1,0:T(8,128)(2,1)}, bf16[256,2688]{1,0:T(8,128)(2,1)}, f32[16,768]{1,0:T(8,128)}, f32[1,3072]{1,0:T(1,128)}) custom-call(s32[1]{0:T(128)} %bitcast.core, f32[32,768]{1,0:T(8,128)} %get-tuple-element.110.vec, f32[256,768]{1,0:T(8,128)} %get-tuple-element.126.m_ref, ...), custom_call_target="tpu_custom_call" | custom-call | flops 1000000 | bytes 100000 | tf_op jit(solution)/shard_map/pallas_call | solution.py:681
  234.1 9.3 %shard_map.293.rest_3_ = bf16[4,4,2,9,24,384]{5,4,3,2,1,0:T(8,128)(2,1)} custom-call(s32[32]{0:T(128)S(1)} %select_n.222.table, bf16[256,4608]{1,0:T(8,128)(2,1)} %get-tuple-element.136.f0, bf16[256,4608]{1,0:T(8,128)(2,1)} %collective-permute-done.35.f1, bf16[256,2688]{1,0:T(8,128)(2,1)} %get-tuple-element.134.b0.rest_0_, ...), custom_call_target="tpu_custom_call" | custom-call | flops 1000000 | bytes 100000 | tf_op jit(solution)/shard_map/pallas_call | solution.py:943
  243.9 16.5 %shard_map.294 = (bf16[512,384]{1,0:T(8,128)(2,1)}, bf16[1024,384]{1,0:T(8,128)(2,1)}, bf16[1024,384]{1,0:T(8,128)(2,1)}, f32[256,768]{1,0:T(8,128)}, f32[256,76...) custom-call(bf16[512,384]{1,0:T(8,128)(2,1)} %get-tuple-element.129.q_ref, ...), custom_call_target="tpu_custom_call" | custom-call | flops 1000000 | bytes 100000 | tf_op jit(solution)/shard_map/pallas_call | solution.py:824
  266.4 5.6 %shard_map.295 = (bf16[4,2,12,24,384]{4,3,2,1,0:T(8,128)(2,1)}, bf16[4,2,12,24,384]{4,3,2,1,0:T(8,128)(2,1)}, bf16[4,2,12,24,384]{4,3,2,1,0:T(8,128)(2,1)}, bf16[4,2,12,24,384]{4,3,2,1,0:T(8,128)(2,1)}) custom-call(s32[32]{0:T(128)S(1)} %select_n.225.table, bf16[1024,768]{1,0:T(8,128)(2,1)} %get-tuple-element.140.a_ref, ...), custom_call_target="tpu_custom_call" | custom-call | flops 1000000 | bytes 100000 | tf_op jit(solution)/shard_map/pallas_call | solution.py:977
  279.3 12.1 %shard_map.296 = (f32[256,768]{1,0:T(8,128)}, bf16[256,2688]{1,0:T(8,128)(2,1)}, bf16[256,2688]{1,0:T(8,128)(2,1)}, f32[16,768]{1,0:T(8,128)}, f32[1,3072]{1,0:T(1,128)}) custom-call(s32[1]{0:T(128)} %bitcast.core, f32[32,768]{1,0:T(8,128)} %get-tuple-element.110.vec, f32[256,768]{1,0:T(8,128)} %get-tuple-element.124.m_ref, ...), custom_call_target="tpu_custom_call" | custom-call | flops 1000000 | bytes 100000 | tf_op jit(solution)/shard_map/pallas_call | solution.py:681
  295.6 9.4 %shard_map.297 = (bf16[4,2,12,24,384]{4,3,2,1,0:T(8,128)(2,1)}, bf16[4,2,12,24,384]{4,3,2,1,0:T(8,128)(2,1)}, bf16[4,2,12,24,384]{4,3,2,1,0:T(8,128)(2,1)}, bf16[4,2,12,24,384]{4,3,2,1,0:T(8,128)(2,1)}) custom-call(s32[32]{0:T(128)S(1)} %select_n.225.table, ...), custom_call_target="tpu_custom_call", output_to_operand_aliasing={{0}: (5, {}), {1}: (6, {}), {2}: (7, {}), {3}: (8, {})} | custom-call | flops 1000000 | bytes 100000 | tf_op jit(solution)/shard_map/pallas_call | solution.py:943
  311.7 17.3 %shard_map.299 = (bf16[512,384]{1,0:T(8,128)(2,1)}, bf16[1024,384]{1,0:T(8,128)(2,1)}, bf16[1024,384]{1,0:T(8,128)(2,1)}, f32[256,768]{1,0:T(8,128)}, f32[256,76...) custom-call(bf16[512,384]{1,0:T(8,128)(2,1)} %get-tuple-element.149.q_ref, ...), custom_call_target="tpu_custom_call" | custom-call | flops 1000000 | bytes 100000 | tf_op jit(solution)/shard_map/pallas_call | solution.py:824
  329.3 5.9 %shard_map.301 = (bf16[4,2,4,24,384]{4,3,2,1,0:T(8,128)(2,1)}, bf16[4,2,4,24,384]{4,3,2,1,0:T(8,128)(2,1)}, bf16[4,2,4,24,384]{4,3,2,1,0:T(8,128)(2,1)}, bf16[4,2,4,24,384]{4,3,2,1,0:T(8,128)(2,1)}) custom-call(s32[32]{0:T(128)S(1)} %select_n.225.table, s32[1]{0:T(128)} %bitcast.core, bf16[1024,768]{1,0:T(8,128)(2,1)} %get-tuple-element.163.a_ref, ...), custom_call_target="tpu_custom_call" | custom-call | flops 1000000 | bytes 100000 | tf_op jit(solution)/shard_map/pallas_call | solution.py:896
  339.9 9.0 %collective-permute-done.42.refs_2_ = bf16[4,2,12,24,384]{4,3,2,1,0:T(8,128)(2,1)S(1)} collective-permute-done((bf16[4,2,12,24,384]{4,3,2,1,0:T(8,128)(2,1)}, bf16[4,2,12,24,384]{4,3,2,1,0:T(8,128)(2,1)S(1)}, u32[]{:S(2)}, u32[]{:S(2)}) %collective-permute-start.42) | collective-permute-done | bytes 1769504 | tf_op jit(solution)/shard_map/ppermute | solution.py:48
  355.6 6.3 %collective-permute-done.45.refs_6_ = bf16[4,2,4,24,384]{4,3,2,1,0:T(8,128)(2,1)} collective-permute-done((bf16[4,2,4,24,384]{4,3,2,1,0:T(8,128)(2,1)}, bf16[4,2,4,24,384]{4,3,2,1,0:T(8,128)(2,1)}, u32[]{:S(2)}, u32[]{:S(2)}) %collective-permute-start.45) | collective-permute-done | bytes 589856 | tf_op jit(solution)/shard_map/ppermute | solution.py:48
  374.4 10.1 %collective-permute-done.47.refs_1_ = bf16[2,16,24,384]{3,2,1,0:T(8,128)(2,1)S(1)} collective-permute-done((bf16[2,16,24,384]{3,2,1,0:T(8,128)(2,1)}, bf16[2,16,24,384]{3,2,1,0:T(8,128)(2,1)S(1)}, u32[]{:S(2)}, u32[]{:S(2)}) %collective-permute-start.47) | collective-permute-done | bytes 589856 | tf_op jit(solution)/shard_map/ppermute | solution.py:48
  403.8 5.7 %collective-permute-start.52 = (bf16[16,24,384]{2,1,0:T(8,128)(2,1)S(1)}, bf16[16,24,384]{2,1,0:T(8,128)(2,1)S(1)}, u32[]{:S(2)}, u32[]{:S(2)}) collective-permute-start(bf16[16,24,384]{2,1,0:T(8,128)(2,1)S(1)} %add_convert_fusion.2.own0), channel_id=1, source_target_pairs={{0,32},{1,33},{2,34},{3,35},{4,36},{5,37},{6,38},{7,39},{8,40},{9,... | collective-permute-start | bytes 884744 | tf_op jit(solution)/shard_map/ppermute | solution.py:48
  (251 shorter events, 163.9 us)
Async XLA Ops:
  7.2 99.9 %all-gather.2.cloned.1.call-start = ((), (), s32[]{:S(2)}) async-start(), calls=%async_computation.2 | async-start | bytes 2211840 | tf_op jit(solution)/shard_map/all_gather | solution.py:1000
  7.2 27.7 %collective-permute-start.1 = (bf16[256,768]{1,0:T(8,128)(2,1)}, bf16[256,768]{1,0:T(8,128)(2,1)S(1)}, u32[]{:S(2)}, u32[]{:S(2)}) collective-permute-start(bf16[256,768]{1,0:T(8,128)(2,1)} %bitcast.67), channel_id=1, source_target_pairs={{0,64},{1,65},{2,66},{3,67},{4,68},{5,69},{6,70},{7,71},{8,72},{9,... | collective-permute-start | bytes 1179656 | tf_op jit(solution)/shard_map/ppermute | solution.py:48
  10.9 57.9 %collective-permute-start = (bf16[256,768]{1,0:T(8,128)(2,1)}, bf16[256,768]{1,0:T(8,128)(2,1)}, u32[]{:S(2)}, u32[]{:S(2)}) collective-permute-start(bf16[256,768]{1,0:T(8,128)(2,1)} %bitcast.68), channel_id=1, source_target_pairs={{0,32},{1,33},{2,34},{3,35},{4,36},{5,37},{6,38},{7,39},{8,40},{9,... | collective-permute-start | bytes 1179656 | tf_op jit(solution)/shard_map/ppermute | solution.py:48
  45.8 23.0 %collective-permute-start.2 = (bf16[256,768]{1,0:T(8,128)(2,1)S(1)}, bf16[256,768]{1,0:T(8,128)(2,1)}, u32[]{:S(2)}, u32[]{:S(2)}) collective-permute-start(bf16[256,768]{1,0:T(8,128)(2,1)S(1)} %copy-done.25), channel_id=1, source_target_pairs={{0,32},{1,33},{2,34},{3,35},{4,36},{5,37},{6,38},{7,39},{8,40},{9,... | collective-permute-start | bytes 1179656 | tf_op jit(solution)/shard_map/ppermute | solution.py:48
  56.3 25.3 %collective-permute-start.14 = (bf16[2,9,24,384]{3,2,1,0:T(8,128)(2,1)}, bf16[2,9,24,384]{3,2,1,0:T(8,128)(2,1)}, u32[]{:S(2)}, u32[]{:S(2)}) collective-permute-start(bf16[2,9,24,384]{3,2,1,0:T(8,128)(2,1)} %shard_map.273.refs_4_), channel_id=1, source_target_pairs={{0,3},{1,0},{2,1},{3,2},{4,7},{5,4},{6,5},{7,6},{8,11},{9,8},{10,9... | collective-permute-start | bytes 995336 | tf_op jit(solution)/shard_map/ppermute | solution.py:48
  59.0 22.6 %collective-permute-start.13 = (bf16[2,9,24,384]{3,2,1,0:T(8,128)(2,1)}, bf16[2,9,24,384]{3,2,1,0:T(8,128)(2,1)}, u32[]{:S(2)}, u32[]{:S(2)}) collective-permute-start(bf16[2,9,24,384]{3,2,1,0:T(8,128)(2,1)} %shard_map.273.refs_4_), channel_id=1, source_target_pairs={{0,2},{1,3},{2,0},{3,1},{4,6},{5,7},{6,4},{7,5},{8,10},{9,11},{10,... | collective-permute-start | bytes 995336 | tf_op jit(solution)/shard_map/ppermute | solution.py:48
  59.0 22.6 %collective-permute-start.12 = (bf16[2,9,24,384]{3,2,1,0:T(8,128)(2,1)}, bf16[2,9,24,384]{3,2,1,0:T(8,128)(2,1)}, u32[]{:S(2)}, u32[]{:S(2)}) collective-permute-start(bf16[2,9,24,384]{3,2,1,0:T(8,128)(2,1)} %shard_map.273.refs_4_), channel_id=1, source_target_pairs={{0,1},{1,2},{2,3},{3,0},{4,5},{5,6},{6,7},{7,4},{8,9},{9,10},{10,1... | collective-permute-start | bytes 995336 | tf_op jit(solution)/shard_map/ppermute | solution.py:48
  59.7 233.0 %reduce-scatter.3.cloned.1.call-start = ((), (), s32[]{:S(2)}) async-start(), calls=%async_computation.3 | async-start | bytes 6635520 | tf_op jit(solution)/shard_map/reduce_scatter | solution.py:994
  85.2 21.9 %collective-permute-start.16 = (bf16[4,2,9,24,384]{4,3,2,1,0:T(8,128)(2,1)}, bf16[4,2,9,24,384]{4,3,2,1,0:T(8,128)(2,1)S(1)}, u32[]{:S(2)}, u32[]{:S(2)}) collective-permute-start(bf16[4,2,9,24,384]{4,3,2,1,0:T(8,128)(2,1)} %pad_maximum_fusion.refs_0_), channel_id=1, source_target_pairs={{0,16},{1,17},{2,18},{3,19},{4,20},{5,21},{6,22},{7,23},{8,24},{9,... | collective-permute-start | bytes 3981320 | tf_op jit(solution)/shard_map/ppermute | solution.py:48
  85.2 32.9 %collective-permute-start.15 = (bf16[4,2,9,24,384]{4,3,2,1,0:T(8,128)(2,1)}, bf16[4,2,9,24,384]{4,3,2,1,0:T(8,128)(2,1)}, u32[]{:S(2)}, u32[]{:S(2)}) collective-permute-start(bf16[4,2,9,24,384]{4,3,2,1,0:T(8,128)(2,1)} %pad_maximum_fusion.refs_0_), channel_id=1, source_target_pairs={{0,8},{1,9},{2,10},{3,11},{4,12},{5,13},{6,14},{7,15},{8,16},{9,17... | collective-permute-start | bytes 3981320 | tf_op jit(solution)/shard_map/ppermute | solution.py:48
  85.8 39.5 %collective-permute-start.18 = (bf16[4,2,9,24,384]{4,3,2,1,0:T(8,128)(2,1)}, bf16[4,2,9,24,384]{4,3,2,1,0:T(8,128)(2,1)}, u32[]{:S(2)}, u32[]{:S(2)}) collective-permute-start(bf16[4,2,9,24,384]{4,3,2,1,0:T(8,128)(2,1)} %pad_maximum_fusion.refs_0_), channel_id=1, source_target_pairs={{0,32},{1,33},{2,34},{3,35},{4,36},{5,37},{6,38},{7,39},{8,40},{9,... | collective-permute-start | bytes 3981320 | tf_op jit(solution)/shard_map/ppermute | solution.py:48
  101.5 26.3 %collective-permute-start.21 = (bf16[4,2,9,24,384]{4,3,2,1,0:T(8,128)(2,1)S(1)}, bf16[4,2,9,24,384]{4,3,2,1,0:T(8,128)(2,1)}, u32[]{:S(2)}, u32[]{:S(2)}) collective-permute-start(bf16[4,2,9,24,384]{4,3,2,1,0:T(8,128)(2,1)S(1)} %collective-permute-done.17.refs_3_), channel_id=1, source_target_pairs={{0,32},{1,33},{2,34},{3,35},{4,36},{5,37},{6,38},{7,39},{8,40},{9,... | collective-permute-start | bytes 3981320 | tf_op jit(solution)/shard_map/ppermute | solution.py:48
  118.1 52.5 %collective-permute-start.27 = (bf16[4,2,12,24,384]{4,3,2,1,0:T(8,128)(2,1)}, bf16[4,2,12,24,384]{4,3,2,1,0:T(8,128)(2,1)}, u32[]{:S(2)}, u32[]{:S(2)}) collective-permute-start(bf16[4,2,12,24,384]{4,3,2,1,0:T(8,128)(2,1)} %shard_map.282.refs_9_.refs_0_), channel_id=1, source_target_pairs={{0,24},{1,25},{2,26},{3,27},{4,28},{5,29},{6,30},{7,31},{8,0},{9,1... | collective-permute-start | bytes 5308424 | tf_op jit(solution)/shard_map/ppermute | solution.py:48
  125.3 45.4 %collective-permute-start.25 = (bf16[4,2,12,24,384]{4,3,2,1,0:T(8,128)(2,1)}, bf16[4,2,12,24,384]{4,3,2,1,0:T(8,128)(2,1)}, u32[]{:S(2)}, u32[]{:S(2)}) collective-permute-start(bf16[4,2,12,24,384]{4,3,2,1,0:T(8,128)(2,1)} %shard_map.282.refs_9_.refs_0_), channel_id=1, source_target_pairs={{0,8},{1,9},{2,10},{3,11},{4,12},{5,13},{6,14},{7,15},{8,16},{9,17... | collective-permute-start | bytes 5308424 | tf_op jit(solution)/shard_map/ppermute | solution.py:48
  127.7 44.9 %collective-permute-start.26 = (bf16[4,2,12,24,384]{4,3,2,1,0:T(8,128)(2,1)}, bf16[4,2,12,24,384]{4,3,2,1,0:T(8,128)(2,1)S(1)}, u32[]{:S(2)}, u32[]{:S(2)}) collective-permute-start(bf16[4,2,12,24,384]{4,3,2,1,0:T(8,128)(2,1)} %shard_map.282.refs_9_.refs_0_), channel_id=1, source_target_pairs={{0,16},{1,17},{2,18},{3,19},{4,20},{5,21},{6,22},{7,23},{8,24},{9,... | collective-permute-start | bytes 5308424 | tf_op jit(solution)/shard_map/ppermute | solution.py:48
  156.8 23.8 %collective-permute-start.28 = (bf16[256,4608]{1,0:T(8,128)(2,1)}, bf16[256,4608]{1,0:T(8,128)(2,1)}, u32[]{:S(2)}, u32[]{:S(2)}) collective-permute-start(bf16[256,4608]{1,0:T(8,128)(2,1)} %get-tuple-element.118.f0), channel_id=1, source_target_pairs={{0,32},{1,33},{2,34},{3,35},{4,36},{5,37},{6,38},{7,39},{8,40},{9,... | collective-permute-start | bytes 7077896 | tf_op jit(solution)/shard_map/ppermute | solution.py:48
  172.1 21.5 %collective-permute-start.30 = (bf16[4,2,12,24,384]{4,3,2,1,0:T(8,128)(2,1)S(1)}, bf16[4,2,12,24,384]{4,3,2,1,0:T(8,128)(2,1)}, u32[]{:S(2)}, u32[]{:S(2)}) collective-permute-start(bf16[4,2,12,24,384]{4,3,2,1,0:T(8,128)(2,1)S(1)} %copy-done), channel_id=1, source_target_pairs={{0,32},{1,33},{2,34},{3,35},{4,36},{5,37},{6,38},{7,39},{8,40},{9,... | collective-permute-start | bytes 5308424 | tf_op jit(solution)/shard_map/ppermute | solution.py:48
  172.6 22.5 %collective-permute-start.31 = (bf16[4,2,12,24,384]{4,3,2,1,0:T(8,128)(2,1)}, bf16[4,2,12,24,384]{4,3,2,1,0:T(8,128)(2,1)}, u32[]{:S(2)}, u32[]{:S(2)}) collective-permute-start(bf16[4,2,12,24,384]{4,3,2,1,0:T(8,128)(2,1)} %shard_map.285.refs_1_), channel_id=1, source_target_pairs={{0,32},{1,33},{2,34},{3,35},{4,36},{5,37},{6,38},{7,39},{8,40},{9,... | collective-permute-start | bytes 5308424 | tf_op jit(solution)/shard_map/ppermute | solution.py:48
  243.4 109.1 %reduce-scatter.5.cloned.1.call-start = ((), (), s32[]{:S(2)}) async-start(), calls=%async_computation.4 | async-start | bytes 1658880 | tf_op jit(solution)/shard_map/reduce_scatter | solution.py:994
  305.0 31.6 %collective-permute-start.41 = (bf16[4,2,12,24,384]{4,3,2,1,0:T(8,128)(2,1)}, bf16[4,2,12,24,384]{4,3,2,1,0:T(8,128)(2,1)S(1)}, u32[]{:S(2)}, u32[]{:S(2)}) collective-permute-start(bf16[4,2,12,24,384]{4,3,2,1,0:T(8,128)(2,1)} %get-tuple-element.160), channel_id=1, source_target_pairs={{0,8},{1,9},{2,10},{3,11},{4,12},{5,13},{6,14},{7,15},{8,16},{9,17... | collective-permute-start | bytes 5308424 | tf_op jit(solution)/shard_map/ppermute | solution.py:48
  307.7 41.3 %collective-permute-start.42 = (bf16[4,2,12,24,384]{4,3,2,1,0:T(8,128)(2,1)}, bf16[4,2,12,24,384]{4,3,2,1,0:T(8,128)(2,1)S(1)}, u32[]{:S(2)}, u32[]{:S(2)}) collective-permute-start(bf16[4,2,12,24,384]{4,3,2,1,0:T(8,128)(2,1)} %get-tuple-element.161), channel_id=1, source_target_pairs={{0,16},{1,17},{2,18},{3,19},{4,20},{5,21},{6,22},{7,23},{8,24},{9,... | collective-permute-start | bytes 5308424 | tf_op jit(solution)/shard_map/ppermute | solution.py:48
  308.4 46.9 %collective-permute-start.43 = (bf16[4,2,12,24,384]{4,3,2,1,0:T(8,128)(2,1)}, bf16[4,2,12,24,384]{4,3,2,1,0:T(8,128)(2,1)}, u32[]{:S(2)}, u32[]{:S(2)}) collective-permute-start(bf16[4,2,12,24,384]{4,3,2,1,0:T(8,128)(2,1)} %get-tuple-element.162), channel_id=1, source_target_pairs={{0,24},{1,25},{2,26},{3,27},{4,28},{5,29},{6,30},{7,31},{8,0},{9,1... | collective-permute-start | bytes 5308424 | tf_op jit(solution)/shard_map/ppermute | solution.py:48
  336.6 25.2 %collective-permute-start.45 = (bf16[4,2,4,24,384]{4,3,2,1,0:T(8,128)(2,1)}, bf16[4,2,4,24,384]{4,3,2,1,0:T(8,128)(2,1)}, u32[]{:S(2)}, u32[]{:S(2)}) collective-permute-start(bf16[4,2,4,24,384]{4,3,2,1,0:T(8,128)(2,1)} %get-tuple-element.176), channel_id=1, source_target_pairs={{0,16},{1,17},{2,18},{3,19},{4,20},{5,21},{6,22},{7,23},{8,24},{9,... | collective-permute-start | bytes 1769480 | tf_op jit(solution)/shard_map/ppermute | solution.py:48
  337.5 24.3 %collective-permute-start.46 = (bf16[4,2,4,24,384]{4,3,2,1,0:T(8,128)(2,1)}, bf16[4,2,4,24,384]{4,3,2,1,0:T(8,128)(2,1)}, u32[]{:S(2)}, u32[]{:S(2)}) collective-permute-start(bf16[4,2,4,24,384]{4,3,2,1,0:T(8,128)(2,1)} %get-tuple-element.177), channel_id=1, source_target_pairs={{0,24},{1,25},{2,26},{3,27},{4,28},{5,29},{6,30},{7,31},{8,0},{9,1... | collective-permute-start | bytes 1769480 | tf_op jit(solution)/shard_map/ppermute | solution.py:48
  (77 other events, 654.9 us)
Sparse Core Ops, SparseCore 0:
  59.8 25.3 all-gather.1
  243.6 32.4 reduce-scatter.2
  292.8 19.4 reduce-scatter.4

commit v3 on v2

--- a/solution.py
+++ b/solution.py
@@ -160,25 +160,36 @@
     return srcs
 
 
-def assemble_kernel(n_dep, table, *refs):
-    srcs, (out, sem) = refs[:4], refs[4 + n_dep :]
+def assemble_kernel(specs, n_dep, table, *refs):
+    srcs, outs, sem = refs[:4], refs[4 + n_dep : -1], refs[-1]
     copies = []
     for n, (dq, dp, dx) in enumerate(SLOTS):
-        src = srcs[dq].at[dp, dx, pl.ds(0, 3)]
-        copies.append(pltpu.make_async_copy(src, out.at[:, table[n]], sem.at[n]))
+        f = table[n]
+        for m, (begin, count, rows_first) in enumerate(specs):
+            src = srcs[dq].at[dp, dx, pl.ds(begin, count)]
+            dst = outs[m].at[f] if rows_first else outs[m].at[:, f]
+            copies.append(pltpu.make_async_copy(src, dst, sem.at[n, m]))
     run_all(copies)
 
 
-def assemble(table, pieces, deps):
-    return pl.pallas_call(
-        functools.partial(assemble_kernel, len(deps)),
-        out_shape=pltpu.HBM((3, 32, ROWS, UNIT), BF),
+def assemble(specs, table, pieces, deps):
+    shapes = [
+        pltpu.HBM((32, count, ROWS, UNIT) if rows_first else (count, 32, ROWS, UNIT), BF)
+        for _, count, rows_first in specs
+    ]
+    outs = pl.pallas_call(
+        functools.partial(assemble_kernel, specs, len(deps)),
+        out_shape=shapes,
         in_specs=[SMEM] + [ANY] * (4 + len(deps)),
-        out_specs=VMEM,
-        scratch_shapes=[pltpu.SemaphoreType.DMA((32,))],
+        out_specs=[VMEM] * len(shapes),
+        scratch_shapes=[pltpu.SemaphoreType.DMA((32, len(shapes)))],
         compiler_params=ROOMY,
         cost_estimate=LIGHT,
     )(table, *pieces, *deps)
+    return [
+        out.reshape(32 * count * ROWS, UNIT) if rows_first else out.reshape(count, 32 * ROWS, UNIT)
+        for out, (_, count, rows_first) in zip(outs, specs)
+    ]
 
 
 def window(f):
@@ -261,7 +272,7 @@
 
 
 def prep_kernel(core, *refs):
-    vecs, (fin, qkv, proj, fc_in, fc_out, u12, u3, vbuf, ubuf) = refs[:8], refs[8:]
+    vecs, (fin, qkv, proj, fc_in, fc_out, u1, u2, u3, vbuf, ubuf) = refs[:8], refs[8:]
     at = pl.multiple_of(core[0] * UNIT, 128)
     wide = pl.multiple_of(core[0] * 4 * UNIT, 128)
     for l in range(2):
@@ -272,7 +283,10 @@
         units += [rows[j * ROWS : (j + 1) * ROWS].astype(BF) for j in range(4)]
         for j, unit in enumerate(units):
             if l == 0:
-                u12[j if j < 3 else j + 1] = unit
+                if j < 3:
+                    u1[j] = unit
+                else:
+                    u2[j - 3] = unit
             else:
                 u3[j] = unit
     vbuf[...] = jnp.zeros(vbuf.shape, F32)
@@ -283,15 +297,15 @@
     ubuf[...] = jnp.zeros(ubuf.shape, F32)
     ubuf[:, :128] = vbuf[...].T[:ROWS]
     ubuf[0:2, 128:224] = fin[...].astype(F32)
-    u12[3] = ubuf[...].astype(BF)
+    u1[3] = ubuf[...].astype(BF)
 
 
 def prep(core, arrays):
     return pl.pallas_call(
         prep_kernel,
-        out_shape=[pltpu.HBM((count, ROWS, UNIT), BF) for count in (13, 12)],
+        out_shape=[pltpu.HBM((count, ROWS, UNIT), BF) for count in (4, 9, 12)],
         in_specs=[SMEM] + [VMEM] * 13,
-        out_specs=[VMEM] * 2,
+        out_specs=[VMEM] * 3,
         scratch_shapes=[pltpu.VMEM((128, 128), F32), pltpu.VMEM((ROWS, UNIT), F32)],
         compiler_params=ROOMY,
         cost_estimate=LIGHT,
@@ -338,7 +352,7 @@
 
 
 def sum_outer(place_at, sets, deps=()):
-    flat = [part for parts in sets for part in parts]
+    flat = [part for parts in sets for part in pin(parts[0]) + list(parts[1:])]
     count = sum(parts[0].shape[2] for parts in sets)
     return pl.pallas_call(
         functools.partial(sum_outer_kernel, [len(s) for s in sets], len(deps)),
@@ -365,7 +379,7 @@
 
 
 def sum_inner(xl, sets, deps=()):
-    flat = [part for parts in sets for part in parts]
+    flat = [part for parts in sets for part in pin(parts[0]) + list(parts[1:])]
     count = sum(parts[0].shape[1] for parts in sets)
     return pl.pallas_call(
         functools.partial(sum_inner_kernel, [len(s) for s in sets], len(deps)),
@@ -517,17 +531,27 @@
     )(core, *pin(parts[0]), *parts[1:], *pin(units, vec), idc, *deps)
 
 
-def load_mlp(wide, outs, pbuf, ibuf, obuf, sem):
+def load_mlp(core, parts, pbuf, ibuf, obuf, sem):
     proj, inner, last = [], [], []
     for side in range(2):
-        cols = pl.ds(side * UNIT, UNIT)
-        proj.append(pltpu.make_async_copy(wide.at[side, 0], pbuf.at[:, cols], sem.at[side, 0]))
+        if len(parts) == 2:
+            wide, outs, place_at = parts[0].at[side], parts[1].at[side], side
+        else:
+            wide, outs = parts[2 * side : 2 * side + 2]
+            place_at = core[0] if side == 0 else 1 - core[0]
+
+        def cols(at):
+            return pl.ds(at if isinstance(at, int) else pl.multiple_of(at, 128), UNIT)
+
+        proj.append(
+            pltpu.make_async_copy(wide.at[0], pbuf.at[:, cols(place_at * UNIT)], sem.at[side, 0])
+        )
         for j in range(4):
-            at = pl.ds((side * 4 + j) * UNIT, UNIT)
+            at = cols((place_at * 4 + j) * UNIT)
             inner.append(
-                pltpu.make_async_copy(wide.at[side, 1 + j], ibuf.at[:, at], sem.at[side, 1 + j])
+                pltpu.make_async_copy(wide.at[1 + j], ibuf.at[:, at], sem.at[side, 1 + j])
             )
-        last.append(pltpu.make_async_copy(outs.at[side], obuf.at[:, cols], sem.at[side, 5]))
+        last.append(pltpu.make_async_copy(outs, obuf.at[:, cols(place_at * UNIT)], sem.at[side, 5]))
     return proj, inner, last
 
 
@@ -536,11 +560,11 @@
         copy.wait()
 
 
-def mlp_fwd_kernel(row, last, core, x, o_own, o_oth, vec, fin, *rest):
-    wide, outs_w, outs = rest[0], rest[1], rest[2:-5]
+def mlp_fwd_kernel(row, last, n_part, core, x, o_own, o_oth, vec, fin, *rest):
+    parts, outs = rest[:n_part], rest[n_part:-5]
     pbuf, ibuf, obuf, full, sem = rest[-5:]
     m_ref, pack, d_ref, y_ref = outs[:4]
-    proj, inner, outer = load_mlp(wide, outs_w, pbuf, ibuf, obuf, sem)
+    proj, inner, outer = load_mlp(core, parts, pbuf, ibuf, obuf, sem)
     for copy in proj + inner + outer:
         copy.start()
     width = x.shape[1]
@@ -598,14 +622,14 @@
     scratch = mlp_scratch(width)
     scratch[3] = pltpu.VMEM((tok, width), BF)
     return pl.pallas_call(
-        functools.partial(mlp_fwd_kernel, row, last),
+        functools.partial(mlp_fwd_kernel, row, last, len(weights)),
         out_shape=shapes,
-        in_specs=[SMEM] + [VMEM] * 5 + [ANY] * 2,
+        in_specs=[SMEM] + [VMEM] * 5 + [ANY] * len(weights),
         out_specs=[VMEM] * len(shapes),
         scratch_shapes=scratch,
         compiler_params=ROOMY,
         cost_estimate=LIGHT,
-    )(core, *pin(x, o_own), o_oth, *pin(vec, fin, *weights))
+    )(core, *pin(x, o_own), o_oth, *pin(vec, fin, *weights[:2]), *weights[2:])
 
 
 def norm_back_kernel(row, vec, x, gmid, da, near, far):
@@ -614,12 +638,12 @@
     return gmid[...] + dx, gain_g, bias_g
 
 
-def mlp_bwd_kernel(row, first, n_dep, core, vec, m_ref, d_ref, *rest):
+def mlp_bwd_kernel(row, first, n_part, n_dep, core, vec, m_ref, d_ref, *rest):
     n_in = 1 if first else 5
-    ins, (wide, outs_w), rest = rest[:n_in], rest[n_in : n_in + 2], rest[n_in + 2 + n_dep :]
+    ins, parts, rest = rest[:n_in], rest[n_in : n_in + n_part], rest[n_in + n_part + n_dep :]
     pbuf, ibuf, obuf, full, sem = rest[-5:]
     gmid_ref, own, oth, rows_ref, fin_ref = rest[:-5]
-    proj, inner, outer = load_mlp(wide, outs_w, pbuf, ibuf, obuf, sem)
+    proj, inner, outer = load_mlp(core, parts, pbuf, ibuf, obuf, sem)
     for copy in outer + inner + proj:
         copy.start()
     width = m_ref.shape[1]
@@ -679,14 +703,14 @@
     scratch = mlp_scratch(width)
     scratch[3] = pltpu.VMEM((tok, 4 * width), BF)
     return pl.pallas_call(
-        functools.partial(mlp_bwd_kernel, row, first, len(deps)),
+        functools.partial(mlp_bwd_kernel, row, first, len(weights), len(deps)),
         out_shape=shapes,
-        in_specs=[SMEM] + [VMEM] * (3 + len(ins)) + [ANY] * (2 + len(deps)),
+        in_specs=[SMEM] + [VMEM] * (3 + len(ins)) + [ANY] * (len(weights) + len(deps)),
         out_specs=[VMEM] * len(shapes),
         scratch_shapes=scratch,
         compiler_params=ROOMY,
         cost_estimate=LIGHT,
-    )(core, *pin(vec, m, d, *ins[:3]), *ins[3:], *pin(*weights), *deps)
+    )(core, *pin(vec, m, d, *ins[:3]), *ins[3:], *pin(*weights[:2]), *weights[2:], *deps)
 
 
 def last_norm_kernel(row, vec, x, gmid, da, near, far, gx_ref):
@@ -949,7 +973,7 @@
         scratch_shapes=scratch,
         compiler_params=ROOMY,
         cost_estimate=LIGHT,
-    )(table, *pin(packs[0]), packs[1], *pin(packs[2]), packs[3], *joint)
+    )(table, *pin(packs[0]), packs[1], *pin(packs[2]), packs[3], *pin(*joint))
 
 
 def spread_units(out, dests, sem, begin):
@@ -1082,7 +1106,6 @@
     table_o = slot_table(-1, 1 - core)
     table_out = slot_table(1, core)
     table_abs = slot_table(-1, core, True)
-    table_abs_o = slot_table(-1, 1 - core, True)
     table_sum = slot_table(1, core, True)
 
     def segment(dx, dc):
@@ -1093,7 +1116,7 @@
     ids = jnp.concatenate([segment(0, 0), segment(0, 1), segment(1, 0), segment(1, 1)])
     idc = ids.astype(F32)[:, None]
 
-    u12, u3 = prep(
+    u1, u2, u3 = prep(
         one,
         pin(
             attn_norm_gain,
@@ -1112,13 +1135,12 @@
         ),
     )
     tokens_own = tokens[0]
-    u12_far = to_xl(u12)
-    p1 = jnp.stack([u12[:4], u12_far[:4]])
-    p2 = jnp.stack([u12[4:], u12_far[4:]])
-    tokens_far = to_xh(tokens_own)
+    p1 = jnp.stack([u1, to_xl(u1)])
+    p2 = jnp.stack([u2, to_xl(after(u2, p1))])
+    tokens_far = to_xh(after(tokens_own, p1))
     share = [tokens_own, to_core(tokens_own), tokens_far, to_core(tokens_far)]
     s1 = three_inner(p1)
-    inner1 = after(inner_of(p1, s1), tokens_far)
+    inner1 = after(inner_of(p1, s1), p2, idc, tokens_far)
     pieces1 = [inner1] + three_outer(inner1)
     p2 = after(p2, *pieces1[1:])
     u3 = after(u3, inner1)
@@ -1126,39 +1148,41 @@
     p3 = after(p3, *pieces1[1:])
     inner3 = gather_along(p3, INNER)
     s2 = three_inner(p2)
-    qkv0, vec_rows, fins = assemble_first(table, pieces1, [p2, p3])
+    qkv0, vec_rows, fins = assemble_first(table, pieces1, pin(p2, p3))
     qkv0 = qkv0.reshape(3, width, UNIT)
     fwd0 = attn_fwd(True, 0, one, share, qkv0, vec_rows, idc)
     o_own, o_oth = fwd0[6:]
     o_got = to_core(o_oth)
     inner2 = inner_of(p2, [after(part, o_own) for part in s2])
-    pieces2 = [inner2] + three_outer(inner2)
+    pieces2 = [inner2] + [after(piece, o_got) for piece in three_outer(inner2)]
     others2 = [to_core(piece) for piece in pieces2]
     inner3 = after(after(inner3, o_own), *pieces2[1:])
     pieces3 = [inner3] + three_outer(inner3)
-    full0 = assemble_both(0, one, [table, table_o], pieces2, others2, [o_got, inner3])
+    full0 = assemble_both(0, one, [table, table_o], pieces2, others2, [o_got] + pin(inner3))
     m0, pack0, d0, x1, a1 = mlp_fwd(0, False, one, tokens_own, o_own, o_got, vec_rows, fins, full0)
     pack0_o = to_core(pack0)
     a1_far = to_xh(a1)
     share1 = [a1, to_core(a1), a1_far, to_core(a1_far)]
     pieces3 = [inner3] + [after(piece, x1) for piece in pieces3[1:]]
-    qkv1 = assemble(table_abs, pieces3, []).reshape(3, width, UNIT)
-    fwd1 = attn_fwd(False, 12, one, share1, qkv1, vec_rows, idc, [pack0_o])
+    qkv1, wide1, outs1 = assemble(
+        [(0, 3, False), (3, 5, False), (8, 4, True)], table_abs, pieces3, share1[1:]
+    )
+    full1 = [wide1, outs1, to_core(wide1), to_core(outs1)]
+    fwd1 = attn_fwd(False, 12, one, share1, qkv1, vec_rows, idc)
     o_own, o_oth = fwd1[6:]
     o_got = to_core(o_oth)
     others3 = [to_core(part) for part in pieces3]
-    full1 = assemble_both(3, one, [table_abs, table_abs_o], pieces3, others3, [o_got])
     m1, pack1, d1, block_output = mlp_fwd(12, True, one, x1, o_own, o_got, vec_rows, fins, full1)
     pack1_o = to_core(pack1)
 
     gmid1, own1, oth1, rows1, fing1 = mlp_bwd(
-        12, True, one, vec_rows, m1, d1, [cotangent[0]], full1, [block_output]
+        12, True, one, vec_rows, m1, d1, [cotangent[0]], full1, pin(block_output)
     )
     got1 = to_core(oth1)
     block_a = mlp_grad(table_sum, [pack1, pack1_o, own1, got1])
     sum_a = reduce_along(block_a, OUTER)
     gq, gk, gv, da, da_keep, da_send, sums1, _ = attn_bwd(
-        12, fwd1[1:6], [], own1, got1, idc, qkv1, [block_a]
+        12, fwd1[1:6], [], own1, got1, idc, qkv1, pin(block_a)
     )
     da_got = to_core(da_send)
     far_in = (da_keep + da_got[tok:].astype(F32)).astype(BF)
@@ -1166,7 +1190,7 @@
     block_e = qkv_grad_rest(table_out, fwd1[0], gq, gk, gv, [far_in])
 
     gmid0, own0, oth0, rows0, fing0 = mlp_bwd(
-        0, False, one, vec_rows, m0, d0, [x1, gmid1, da, da_got, far], full0, block_e
+        0, False, one, vec_rows, m0, d0, [x1, gmid1, da, da_got, far], full0, pin(block_e[0])
     )
     got0 = to_core(oth0)
     sum_a = after(sum_a, gmid0)
@@ -1175,7 +1199,7 @@
     block_b = mlp_grad(table_out, [pack0, pack0_o, own0, got0], block_e)
     sent_b = send_outer(block_b)
     gq, gk, gv, da, da_keep, da_send, sums0, norm0 = attn_bwd(
-        0, fwd0[1:6], share, own0, got0, idc, qkv0, [block_b[0], mid_a]
+        0, fwd0[1:6], share, own0, got0, idc, qkv0, pin(block_b[0], mid_a)
     )
     da_got = to_core(da_send)
     far = to_xh((da_keep + da_got[tok:].astype(F32)).astype(BF))
@@ -1184,13 +1208,13 @@
     block_c = qkv_grad(table_out, one, fwd0[0], gq, gk, gv, vecs, [])
     sent_c = send_outer(block_c)
     gx = last_norm(0, vec_rows, [tokens_own, gmid0, da, da_got, far])
-    mine_a, other_a = sum_inner(xl_one, [[sum_a]], [block_c[0]])
+    mine_a, other_a = sum_inner(xl_one, [[sum_a]], pin(block_c[0]))
     part_a = add_all(mine_a, to_xl(other_a))
     part_a = add_all(part_a, to_xh(part_a))
     part_a_o = to_core(part_a)
-    sum_bc = sum_outer(inner_at, [sent_b, sent_c], [far, other_a])
+    sum_bc = sum_outer(inner_at, [sent_b, sent_c], [far] + pin(other_a))
     sent_bc = [sum_bc[0]] + [to_inner(sum_bc[d], d) for d in (1, 2, 3)]
-    mine_bc, other_bc = sum_inner(xl_one, [sent_bc], [gx])
+    mine_bc, other_bc = sum_inner(xl_one, [sent_bc], pin(gx))
     part_bc = add_all(mine_bc, to_xl(other_bc))
     part_bc = add_all(part_bc, to_xh(part_bc))
     done = finish(one, [part_bc, to_core(part_bc), part_a, part_a_o])

time: 426 us -> 404 us (0.948)
  local copies, waits for them, and re-layouts: 25 us -> 12.6 us
  waiting for transfers between devices: 101 us -> 112 us
  Pallas kernels: 180 us -> 171 us
  starting transfers between devices: 86.1 us -> 78.8 us
  other arithmetic: 14.3 us -> 9.71 us
    pallas_call x2 -> x1, Pallas kernels: 24.8 us -> 12.6 us  [assemble_both(): pl.pallas_call(functools.partial(assemble_both_kernel, begin), out_shape=...]
    ppermute x56 -> x55, waiting for transfers between devices: 101 us -> 112 us  [shift(): return lax.ppermute(array, AXES, pairs)]
    unnamed x84 -> x56, local copies, waits for them, and re-layouts: 20.1 us -> 12 us
    ppermute x56 -> x55, starting transfers between devices: 85.3 us -> 78.1 us  [shift(): return lax.ppermute(array, AXES, pairs)]
  transfers between devices with their start and end apart: 59 -> 58, of which waited for: 22 -> 24; matrix products, arithmetic and copies ran while one was open for 5% -> 3% of each run, Pallas kernels for 33% -> 34%
where the time goes in v3:
time: 404 us; the launch traced here: 398 us
  Pallas kernels  171 us (42%)
  waiting for transfers between devices  112 us (28%)
  starting transfers between devices  78.8 us (20%)
  between operations  14.8 us (4%)
  local copies, waits for them, and re-layouts  12.6 us (3%)
  other arithmetic  9.71 us (2%)
    ppermute x55, waiting for transfers between devices, shift(): return lax.ppermute(array, AXES, pairs)  112 us
    ppermute x55, starting transfers between devices, shift(): return lax.ppermute(array, AXES, pairs)  78.1 us
    pallas_call x2, Pallas kernels, attn_bwd(): pl.pallas_call(functools.partial(attn_bwd_kernel, row, len(raw), len(deps...  33.8 us
    pallas_call x2, Pallas kernels, attn_fwd(): pl.pallas_call(functools.partial(attn_fwd_kernel, raw, row, len(deps)), o...  24.6 us
    pallas_call x2, Pallas kernels, mlp_bwd(): pl.pallas_call(functools.partial(mlp_bwd_kernel, row, first, len(weights)...  22.1 us
    pallas_call x2, Pallas kernels, mlp_fwd(): pl.pallas_call(functools.partial(mlp_fwd_kernel, row, last, len(weights))...  19.9 us
    pallas_call x2, Pallas kernels, mlp_grad(): pl.pallas_call(functools.partial(mlp_grad_kernel, more), out_shape=blocks...  18.8 us
    pallas_call x1, Pallas kernels, assemble_both(): pl.pallas_call(functools.partial(assemble_both_kernel, begin), out_shape=...  12.6 us
  transfers between devices with their start and end apart: 58, of which 24 were waited for; matrix products, arithmetic and copies ran while one was open for 3% of the time, Pallas kernels for 34%

profile of v3, /device:TPU:1, one launch (start us, length us, event | category | flops | bytes accessed | tf_op | source)
XLA Modules:
  0.0 398.5 jit_solution(16646564047351521127)
XLA Ops:
  28.6 5.7 %collective-permute-done.7 = bf16[9,24,384]{2,1,0:T(8,128)(2,1)S(1)} collective-permute-done((bf16[9,24,384]{2,1,0:T(8,128)(2,1)}, bf16[9,24,384]{2,1,0:T(8,128)(2,1)S(1)}, u32[]{:S(2)}, u32[]{:S(2)}) %collective-permute-start.7) | collective-permute-done | bytes 165920 | tf_op jit(solution)/shard_map/ppermute | solution.py:48
  43.4 10.2 %collective-permute-done.10.refs_3_ = bf16[4,2,4,24,384]{4,3,2,1,0:T(8,128)(2,1)S(1)} collective-permute-done((bf16[4,2,4,24,384]{4,3,2,1,0:T(8,128)(2,1)}, bf16[4,2,4,24,384]{4,3,2,1,0:T(8,128)(2,1)S(1)}, u32[]{:S(2)}, u32[]{:S(2)}) %collective-permute-start.10) | collective-permute-done | bytes 589856 | tf_op jit(solution)/shard_map/ppermute | solution.py:48
  68.9 12.8 %shard_map.279 = (bf16[1024,768]{1,0:T(8,128)(2,1)}, bf16[512,384]{1,0:T(8,128)(2,1)}, bf16[1024,384]{1,0:T(8,128)(2,1)}, bf16[1024,384]{1,0:T(8,128)(2,1)}, f32...) custom-call(s32[1]{0:T(128)} %bitcast.core, ...), custom_call_target="tpu_custom_call" | custom-call | flops 1000000 | bytes 100000 | tf_op jit(solution)/shard_map/pallas_call | solution.py:523
  91.9 10.6 %collective-permute-done.18.refs_0_ = bf16[4,2,9,24,384]{4,3,2,1,0:T(8,128)(2,1)} collective-permute-done((bf16[4,2,9,24,384]{4,3,2,1,0:T(8,128)(2,1)}, bf16[4,2,9,24,384]{4,3,2,1,0:T(8,128)(2,1)}, u32[]{:S(2)}, u32[]{:S(2)}) %collective-permute-start.18) | collective-permute-done | bytes 1327136 | tf_op jit(solution)/shard_map/ppermute | solution.py:48
  107.9 10.7 %collective-permute-done.16.refs_0_ = bf16[4,2,9,24,384]{4,3,2,1,0:T(8,128)(2,1)S(1)} collective-permute-done((bf16[4,2,9,24,384]{4,3,2,1,0:T(8,128)(2,1)}, bf16[4,2,9,24,384]{4,3,2,1,0:T(8,128)(2,1)S(1)}, u32[]{:S(2)}, u32[]{:S(2)}) %collective-permute-start.16) | collective-permute-done | bytes 1327136 | tf_op jit(solution)/shard_map/ppermute | solution.py:48
  125.4 12.6 %shard_map.288 = (bf16[2,5,32,24,384]{4,3,2,1,0:T(8,128)(2,1)}, bf16[2,32,4,24,384]{4,3,2,1,0:T(8,128)(2,1)}) custom-call(s32[1]{0:T(128)} %bitcast.core, s32[32]{0:T(128)S(1)} %select_n.188.table, s32[32]{0:T(128)S(1)} %select_n.203.table_o, bf16[4,2,9,24,384]{4,3,2,1,0:T(8,128)(2,1)} %pad_maximum_fusion.refs_0_, bf16[4,2,9,24,384]{4,3,2,1,0:T(8,128)(2,1)S(1)} %copy-done.3, ...), custom_call_target="tpu_custom_call" | custom-call | flops 1000000 | bytes 100000 | tf_op jit(solution)/shard_map/pallas_call | solution.py:259
  138.0 10.8 %shard_map.289 = (f32[256,768]{1,0:T(8,128)}, bf16[256,4608]{1,0:T(8,128)(2,1)}, f32[256,3072]{1,0:T(8,128)}, f32[256,768]{1,0:T(8,128)}, bf16[256,768]{1,0:T(8,128)(2,1)}) custom-call(s32[1]{0:T(128)} %bitcast.core, bf16[256,768]{1,0:T(8,128)(2,1)} %bitcast.1.x0.x.rest_0_, bf16[256,384]{1,0:T(8,128)(2,1)} %get-tuple-element.114.refs_1_.o_own, ...), custom_call_target="tpu_custom_call" | custom-call | flops 1000000 | bytes 100000 | tf_op jit(solution)/shard_map/pallas_call | solution.py:624
  152.2 8.0 %collective-permute-done.24.refs_5_.x2 = bf16[256,768]{1,0:T(8,128)(2,1)S(1)} collective-permute-done((bf16[256,768]{1,0:T(8,128)(2,1)}, bf16[256,768]{1,0:T(8,128)(2,1)S(1)}, u32[]{:S(2)}, u32[]{:S(2)}) %collective-permute-start.24) | collective-permute-done | bytes 393248 | tf_op jit(solution)/shard_map/ppermute | solution.py:48
  165.0 8.0 %shard_map.293 = (bf16[3,32,24,384]{3,2,1,0:T(8,128)(2,1)}, bf16[5,32,24,384]{3,2,1,0:T(8,128)(2,1)}, bf16[32,4,24,384]{3,2,1,0:T(8,128)(2,1)}) custom-call(s32[32]{0:T(128)S(1)} %select_n.205.table, bf16[4,2,12,24,384]{4,3,2,1,0:T(8,128)(2,1)S(1)} %copy-done, bf16[4,2,12,24,384]{4,3,2,1,0:T(8,128)(2,1)} %shard_map.290.refs_1_, ...), custom_call_target="tpu_custom_call" | custom-call | flops 1000000 | bytes 100000 | tf_op jit(solution)/shard_map/pallas_call | solution.py:180
  177.2 11.8 %shard_map.294 = (bf16[1024,768]{1,0:T(8,128)(2,1)}, bf16[512,384]{1,0:T(8,128)(2,1)}, bf16[1024,384]{1,0:T(8,128)(2,1)}, bf16[1024,384]{1,0:T(8,128)(2,1)}, f32...) custom-call(s32[1]{0:T(128)} %bitcast.core, ...), custom_call_target="tpu_custom_call" | custom-call | flops 1000000 | bytes 100000 | tf_op jit(solution)/shard_map/pallas_call | solution.py:523
  191.0 9.0 %shard_map.295 = (f32[256,768]{1,0:T(8,128)}, bf16[256,4608]{1,0:T(8,128)(2,1)}, f32[256,3072]{1,0:T(8,128)}, bf16[256,768]{1,0:T(8,128)(2,1)}) custom-call(s32[1]{0:T(128)} %bitcast.core, f32[256,768]{1,0:T(8,128)} %get-tuple-element.119.refs_1_.x.rest_0_, bf16[256,384]{1,0:T(8,128)(2,1)} %get-tuple-element.122.o_own, ...), custom_call_target="tpu_custom_call" | custom-call | flops 1000000 | bytes 100000 | tf_op jit(solution)/shard_map/pallas_call | solution.py:624
  200.5 9.9 %shard_map.296 = (f32[256,768]{1,0:T(8,128)}, bf16[256,2688]{1,0:T(8,128)(2,1)}, bf16[256,2688]{1,0:T(8,128)(2,1)}, f32[16,768]{1,0:T(8,128)}, f32[1,3072]{1,0:T(1,128)}) custom-call(s32[1]{0:T(128)} %bitcast.core, f32[32,768]{1,0:T(8,128)} %get-tuple-element.113.vec, f32[256,768]{1,0:T(8,128)} %get-tuple-element.129.m_ref, ...), custom_call_target="tpu_custom_call" | custom-call | flops 1000000 | bytes 100000 | tf_op jit(solution)/shard_map/pallas_call | solution.py:705
  213.8 9.2 %shard_map.297.rest_3_ = bf16[4,4,2,9,24,384]{5,4,3,2,1,0:T(8,128)(2,1)} custom-call(s32[32]{0:T(128)S(1)} %select_n.207.table, bf16[256,4608]{1,0:T(8,128)(2,1)} %get-tuple-element.139.f0, bf16[256,4608]{1,0:T(8,128)(2,1)} %collective-permute-done.33.f1, bf16[256,2688]{1,0:T(8,128)(2,1)} %get-tuple-element.137.b0.rest_0_, ...), custom_call_target="tpu_custom_call" | custom-call | flops 1000000 | bytes 100000 | tf_op jit(solution)/shard_map/pallas_call | solution.py:967
  223.5 16.5 %shard_map.298 = (bf16[512,384]{1,0:T(8,128)(2,1)}, bf16[1024,384]{1,0:T(8,128)(2,1)}, bf16[1024,384]{1,0:T(8,128)(2,1)}, f32[256,768]{1,0:T(8,128)}, f32[256,76...) custom-call(bf16[512,384]{1,0:T(8,128)(2,1)} %get-tuple-element.132.q_ref, ...), custom_call_target="tpu_custom_call" | custom-call | flops 1000000 | bytes 100000 | tf_op jit(solution)/shard_map/pallas_call | solution.py:848
  245.9 5.6 %shard_map.299 = (bf16[4,2,12,24,384]{4,3,2,1,0:T(8,128)(2,1)}, bf16[4,2,12,24,384]{4,3,2,1,0:T(8,128)(2,1)}, bf16[4,2,12,24,384]{4,3,2,1,0:T(8,128)(2,1)}, bf16[4,2,12,24,384]{4,3,2,1,0:T(8,128)(2,1)}) custom-call(s32[32]{0:T(128)S(1)} %select_n.210.table, bf16[1024,768]{1,0:T(8,128)(2,1)} %get-tuple-element.143.a_ref, ...), custom_call_target="tpu_custom_call" | custom-call | flops 1000000 | bytes 100000 | tf_op jit(solution)/shard_map/pallas_call | solution.py:1001
  256.1 12.2 %shard_map.300 = (f32[256,768]{1,0:T(8,128)}, bf16[256,2688]{1,0:T(8,128)(2,1)}, bf16[256,2688]{1,0:T(8,128)(2,1)}, f32[16,768]{1,0:T(8,128)}, f32[1,3072]{1,0:T(1,128)}) custom-call(s32[1]{0:T(128)} %bitcast.core, f32[32,768]{1,0:T(8,128)} %get-tuple-element.113.vec, f32[256,768]{1,0:T(8,128)} %get-tuple-element.127.m_ref, ...), custom_call_target="tpu_custom_call" | custom-call | flops 1000000 | bytes 100000 | tf_op jit(solution)/shard_map/pallas_call | solution.py:705
  272.3 9.6 %shard_map.301 = (bf16[4,2,12,24,384]{4,3,2,1,0:T(8,128)(2,1)}, bf16[4,2,12,24,384]{4,3,2,1,0:T(8,128)(2,1)}, bf16[4,2,12,24,384]{4,3,2,1,0:T(8,128)(2,1)}, bf16[4,2,12,24,384]{4,3,2,1,0:T(8,128)(2,1)}) custom-call(s32[32]{0:T(128)S(1)} %select_n.210.table, ...), custom_call_target="tpu_custom_call", output_to_operand_aliasing={{0}: (5, {}), {1}: (6, {}), {2}: (7, {}), {3}: (8, {})} | custom-call | flops 1000000 | bytes 100000 | tf_op jit(solution)/shard_map/pallas_call | solution.py:967
  284.7 17.4 %shard_map.303 = (bf16[512,384]{1,0:T(8,128)(2,1)}, bf16[1024,384]{1,0:T(8,128)(2,1)}, bf16[1024,384]{1,0:T(8,128)(2,1)}, f32[256,768]{1,0:T(8,128)}, f32[256,76...) custom-call(bf16[512,384]{1,0:T(8,128)(2,1)} %get-tuple-element.149.q_ref, ...), custom_call_target="tpu_custom_call" | custom-call | flops 1000000 | bytes 100000 | tf_op jit(solution)/shard_map/pallas_call | solution.py:848
  303.3 5.8 %shard_map.305 = (bf16[4,2,4,24,384]{4,3,2,1,0:T(8,128)(2,1)}, bf16[4,2,4,24,384]{4,3,2,1,0:T(8,128)(2,1)}, bf16[4,2,4,24,384]{4,3,2,1,0:T(8,128)(2,1)}, bf16[4,2,4,24,384]{4,3,2,1,0:T(8,128)(2,1)}) custom-call(s32[32]{0:T(128)S(1)} %select_n.210.table, s32[1]{0:T(128)} %bitcast.core, bf16[1024,768]{1,0:T(8,128)(2,1)} %get-tuple-element.167.a_ref, ...), custom_call_target="tpu_custom_call" | custom-call | flops 1000000 | bytes 100000 | tf_op jit(solution)/shard_map/pallas_call | solution.py:920
  309.4 15.5 %collective-permute-done.40.refs_1_ = bf16[4,2,12,24,384]{4,3,2,1,0:T(8,128)(2,1)S(1)} collective-permute-done((bf16[4,2,12,24,384]{4,3,2,1,0:T(8,128)(2,1)}, bf16[4,2,12,24,384]{4,3,2,1,0:T(8,128)(2,1)S(1)}, u32[]{:S(2)}, u32[]{:S(2)}) %collective-permute-start.40) | collective-permute-done | bytes 1769504 | tf_op jit(solution)/shard_map/ppermute | solution.py:48
  330.6 7.0 %collective-permute-done.43.refs_5_ = bf16[4,2,4,24,384]{4,3,2,1,0:T(8,128)(2,1)} collective-permute-done((bf16[4,2,4,24,384]{4,3,2,1,0:T(8,128)(2,1)}, bf16[4,2,4,24,384]{4,3,2,1,0:T(8,128)(2,1)}, u32[]{:S(2)}, u32[]{:S(2)}) %collective-permute-start.43) | collective-permute-done | bytes 589856 | tf_op jit(solution)/shard_map/ppermute | solution.py:48
  340.6 4.9 %shard_map.307 = (bf16[2,16,24,384]{3,2,1,0:T(8,128)(2,1)}, bf16[2,16,24,384]{3,2,1,0:T(8,128)(2,1)}, bf16[2,16,24,384]{3,2,1,0:T(8,128)(2,1)}, bf16[2,16,24,384]{3,2,1,0:T(8,128)(2,1)}) custom-call(s32[1]{0:T(128)} %bitcast.34.place_at, bf16[4,2,12,24,384]{4,3,2,1,0:T(8,128)(2,1)} %get-tuple-element.160.rest_7_.refs_0_, ...), custom_call_target="tpu_custom_call" | custom-call | flops 1000000 | bytes 100000 | tf_op jit(solution)/shard_map/pallas_call | solution.py:357
  355.9 6.4 %collective-permute-done.47.refs_2_ = bf16[2,16,24,384]{3,2,1,0:T(8,128)(2,1)S(1)} collective-permute-done((bf16[2,16,24,384]{3,2,1,0:T(8,128)(2,1)}, bf16[2,16,24,384]{3,2,1,0:T(8,128)(2,1)S(1)}, u32[]{:S(2)}, u32[]{:S(2)}) %collective-permute-start.47) | collective-permute-done | bytes 589856 | tf_op jit(solution)/shard_map/ppermute | solution.py:48
  381.8 5.7 %collective-permute-start.51 = (bf16[16,24,384]{2,1,0:T(8,128)(2,1)S(1)}, bf16[16,24,384]{2,1,0:T(8,128)(2,1)S(1)}, u32[]{:S(2)}, u32[]{:S(2)}) collective-permute-start(bf16[16,24,384]{2,1,0:T(8,128)(2,1)S(1)} %add_convert_fusion.2.own0), channel_id=1, source_target_pairs={{0,32},{1,33},{2,34},{3,35},{4,36},{5,37},{6,38},{7,39},{8,40},{9,... | collective-permute-start | bytes 884744 | tf_op jit(solution)/shard_map/ppermute | solution.py:48
  (221 shorter events, 147.8 us)
Async XLA Ops:
  7.2 115.1 %all-gather.2.cloned.1.call-start = ((), (), s32[]{:S(2)}) async-start(), calls=%async_computation.2 | async-start | bytes 2211840 | tf_op jit(solution)/shard_map/all_gather | solution.py:1024
  25.1 43.8 %collective-permute-start = (bf16[256,768]{1,0:T(8,128)(2,1)}, bf16[256,768]{1,0:T(8,128)(2,1)}, u32[]{:S(2)}, u32[]{:S(2)}) collective-permute-start(bf16[256,768]{1,0:T(8,128)(2,1)} %bitcast.1.x0.x.rest_0_), channel_id=1, source_target_pairs={{0,32},{1,33},{2,34},{3,35},{4,36},{5,37},{6,38},{7,39},{8,40},{9,... | collective-permute-start | bytes 1179656 | tf_op jit(solution)/shard_map/ppermute | solution.py:48
  35.8 17.8 %collective-permute-start.10 = (bf16[4,2,4,24,384]{4,3,2,1,0:T(8,128)(2,1)}, bf16[4,2,4,24,384]{4,3,2,1,0:T(8,128)(2,1)S(1)}, u32[]{:S(2)}, u32[]{:S(2)}) collective-permute-start(bf16[4,2,4,24,384]{4,3,2,1,0:T(8,128)(2,1)} %shard_map.274.refs_1_.refs_0_), channel_id=1, source_target_pairs={{0,24},{1,25},{2,26},{3,27},{4,28},{5,29},{6,30},{7,31},{8,0},{9,1... | collective-permute-start | bytes 1769480 | tf_op jit(solution)/shard_map/ppermute | solution.py:48
  42.1 17.5 %collective-permute-start.11 = (bf16[12,24,384]{2,1,0:T(8,128)(2,1)}, bf16[12,24,384]{2,1,0:T(8,128)(2,1)S(1)}, u32[]{:S(2)}, u32[]{:S(2)}) collective-permute-start(bf16[12,24,384]{2,1,0:T(8,128)(2,1)} %shard_map.276), channel_id=1, source_target_pairs={{0,4},{1,5},{2,6},{3,7},{4,0},{5,1},{6,2},{7,3},{8,12},{9,13},{10,... | collective-permute-start | bytes 663560 | tf_op jit(solution)/shard_map/ppermute | solution.py:48
  58.4 23.3 %collective-permute-start.13 = (bf16[2,9,24,384]{3,2,1,0:T(8,128)(2,1)}, bf16[2,9,24,384]{3,2,1,0:T(8,128)(2,1)}, u32[]{:S(2)}, u32[]{:S(2)}) collective-permute-start(bf16[2,9,24,384]{3,2,1,0:T(8,128)(2,1)} %shard_map.275.refs_4_), channel_id=1, source_target_pairs={{0,1},{1,2},{2,3},{3,0},{4,5},{5,6},{6,7},{7,4},{8,9},{9,10},{10,1... | collective-permute-start | bytes 995336 | tf_op jit(solution)/shard_map/ppermute | solution.py:48
  59.7 22.1 %collective-permute-start.14 = (bf16[2,9,24,384]{3,2,1,0:T(8,128)(2,1)}, bf16[2,9,24,384]{3,2,1,0:T(8,128)(2,1)}, u32[]{:S(2)}, u32[]{:S(2)}) collective-permute-start(bf16[2,9,24,384]{3,2,1,0:T(8,128)(2,1)} %shard_map.275.refs_4_), channel_id=1, source_target_pairs={{0,2},{1,3},{2,0},{3,1},{4,6},{5,7},{6,4},{7,5},{8,10},{9,11},{10,... | collective-permute-start | bytes 995336 | tf_op jit(solution)/shard_map/ppermute | solution.py:48
  59.7 22.1 %collective-permute-start.15 = (bf16[2,9,24,384]{3,2,1,0:T(8,128)(2,1)}, bf16[2,9,24,384]{3,2,1,0:T(8,128)(2,1)}, u32[]{:S(2)}, u32[]{:S(2)}) collective-permute-start(bf16[2,9,24,384]{3,2,1,0:T(8,128)(2,1)} %shard_map.275.refs_4_), channel_id=1, source_target_pairs={{0,3},{1,0},{2,1},{3,2},{4,7},{5,4},{6,5},{7,6},{8,11},{9,8},{10,9... | collective-permute-start | bytes 995336 | tf_op jit(solution)/shard_map/ppermute | solution.py:48
  63.1 206.2 %reduce-scatter.3.cloned.1.call-start = ((), (), s32[]{:S(2)}) async-start(), calls=%async_computation.3 | async-start | bytes 6635520 | tf_op jit(solution)/shard_map/reduce_scatter | solution.py:1018
  85.8 19.6 %collective-permute-start.17 = (bf16[4,2,9,24,384]{4,3,2,1,0:T(8,128)(2,1)}, bf16[4,2,9,24,384]{4,3,2,1,0:T(8,128)(2,1)S(1)}, u32[]{:S(2)}, u32[]{:S(2)}) collective-permute-start(bf16[4,2,9,24,384]{4,3,2,1,0:T(8,128)(2,1)} %pad_maximum_fusion.refs_0_), channel_id=1, source_target_pairs={{0,16},{1,17},{2,18},{3,19},{4,20},{5,21},{6,22},{7,23},{8,24},{9,... | collective-permute-start | bytes 3981320 | tf_op jit(solution)/shard_map/ppermute | solution.py:48
  86.1 32.5 %collective-permute-start.16 = (bf16[4,2,9,24,384]{4,3,2,1,0:T(8,128)(2,1)}, bf16[4,2,9,24,384]{4,3,2,1,0:T(8,128)(2,1)S(1)}, u32[]{:S(2)}, u32[]{:S(2)}) collective-permute-start(bf16[4,2,9,24,384]{4,3,2,1,0:T(8,128)(2,1)} %pad_maximum_fusion.refs_0_), channel_id=1, source_target_pairs={{0,8},{1,9},{2,10},{3,11},{4,12},{5,13},{6,14},{7,15},{8,16},{9,17... | collective-permute-start | bytes 3981320 | tf_op jit(solution)/shard_map/ppermute | solution.py:48
  90.3 32.1 %collective-permute-start.19 = (bf16[4,2,9,24,384]{4,3,2,1,0:T(8,128)(2,1)}, bf16[4,2,9,24,384]{4,3,2,1,0:T(8,128)(2,1)}, u32[]{:S(2)}, u32[]{:S(2)}) collective-permute-start(bf16[4,2,9,24,384]{4,3,2,1,0:T(8,128)(2,1)} %pad_maximum_fusion.refs_0_), channel_id=1, source_target_pairs={{0,32},{1,33},{2,34},{3,35},{4,36},{5,37},{6,38},{7,39},{8,40},{9,... | collective-permute-start | bytes 3981320 | tf_op jit(solution)/shard_map/ppermute | solution.py:48
  102.4 22.3 %collective-permute-start.22 = (bf16[4,2,9,24,384]{4,3,2,1,0:T(8,128)(2,1)}, bf16[4,2,9,24,384]{4,3,2,1,0:T(8,128)(2,1)}, u32[]{:S(2)}, u32[]{:S(2)}) collective-permute-start(bf16[4,2,9,24,384]{4,3,2,1,0:T(8,128)(2,1)} %shard_map.285.refs_3_), channel_id=1, source_target_pairs={{0,32},{1,33},{2,34},{3,35},{4,36},{5,37},{6,38},{7,39},{8,40},{9,... | collective-permute-start | bytes 3981320 | tf_op jit(solution)/shard_map/ppermute | solution.py:48
  106.4 18.5 %collective-permute-start.21 = (bf16[4,2,9,24,384]{4,3,2,1,0:T(8,128)(2,1)}, bf16[4,2,9,24,384]{4,3,2,1,0:T(8,128)(2,1)}, u32[]{:S(2)}, u32[]{:S(2)}) collective-permute-start(bf16[4,2,9,24,384]{4,3,2,1,0:T(8,128)(2,1)} %shard_map.284.refs_2_), channel_id=1, source_target_pairs={{0,32},{1,33},{2,34},{3,35},{4,36},{5,37},{6,38},{7,39},{8,40},{9,... | collective-permute-start | bytes 3981320 | tf_op jit(solution)/shard_map/ppermute | solution.py:48
  122.4 39.9 %collective-permute-start.28 = (bf16[4,2,12,24,384]{4,3,2,1,0:T(8,128)(2,1)}, bf16[4,2,12,24,384]{4,3,2,1,0:T(8,128)(2,1)}, u32[]{:S(2)}, u32[]{:S(2)}) collective-permute-start(bf16[4,2,12,24,384]{4,3,2,1,0:T(8,128)(2,1)} %shard_map.287.refs_9_.refs_0_), channel_id=1, source_target_pairs={{0,24},{1,25},{2,26},{3,27},{4,28},{5,29},{6,30},{7,31},{8,0},{9,1... | collective-permute-start | bytes 5308424 | tf_op jit(solution)/shard_map/ppermute | solution.py:48
  122.5 39.8 %collective-permute-start.27 = (bf16[4,2,12,24,384]{4,3,2,1,0:T(8,128)(2,1)}, bf16[4,2,12,24,384]{4,3,2,1,0:T(8,128)(2,1)}, u32[]{:S(2)}, u32[]{:S(2)}) collective-permute-start(bf16[4,2,12,24,384]{4,3,2,1,0:T(8,128)(2,1)} %shard_map.287.refs_9_.refs_0_), channel_id=1, source_target_pairs={{0,16},{1,17},{2,18},{3,19},{4,20},{5,21},{6,22},{7,23},{8,24},{9,... | collective-permute-start | bytes 5308424 | tf_op jit(solution)/shard_map/ppermute | solution.py:48
  124.7 40.3 %collective-permute-start.26 = (bf16[4,2,12,24,384]{4,3,2,1,0:T(8,128)(2,1)}, bf16[4,2,12,24,384]{4,3,2,1,0:T(8,128)(2,1)}, u32[]{:S(2)}, u32[]{:S(2)}) collective-permute-start(bf16[4,2,12,24,384]{4,3,2,1,0:T(8,128)(2,1)} %shard_map.287.refs_9_.refs_0_), channel_id=1, source_target_pairs={{0,8},{1,9},{2,10},{3,11},{4,12},{5,13},{6,14},{7,15},{8,16},{9,17... | collective-permute-start | bytes 5308424 | tf_op jit(solution)/shard_map/ppermute | solution.py:48
  173.0 18.0 %collective-permute-start.30 = (bf16[5,768,384]{2,1,0:T(8,128)(2,1)}, bf16[5,768,384]{2,1,0:T(8,128)(2,1)S(1)}, u32[]{:S(2)}, u32[]{:S(2)}) collective-permute-start(bf16[5,768,384]{2,1,0:T(8,128)(2,1)} %bitcast.50), channel_id=1, source_target_pairs={{0,32},{1,33},{2,34},{3,35},{4,36},{5,37},{6,38},{7,39},{8,40},{9,... | collective-permute-start | bytes 8847368 | tf_op jit(solution)/shard_map/ppermute | solution.py:48
  223.1 105.8 %reduce-scatter.5.cloned.1.call-start = ((), (), s32[]{:S(2)}) async-start(), calls=%async_computation.4 | async-start | bytes 1658880 | tf_op jit(solution)/shard_map/reduce_scatter | solution.py:1018
  240.2 29.1 %collective-permute-start.37 = (bf16[256,4608]{1,0:T(8,128)(2,1)}, bf16[256,4608]{1,0:T(8,128)(2,1)}, u32[]{:S(2)}, u32[]{:S(2)}) collective-permute-start(bf16[256,4608]{1,0:T(8,128)(2,1)} %get-tuple-element.156.f0), channel_id=1, source_target_pairs={{0,32},{1,33},{2,34},{3,35},{4,36},{5,37},{6,38},{7,39},{8,40},{9,... | collective-permute-start | bytes 7077896 | tf_op jit(solution)/shard_map/ppermute | solution.py:48
  281.9 43.1 %collective-permute-start.40 = (bf16[4,2,12,24,384]{4,3,2,1,0:T(8,128)(2,1)}, bf16[4,2,12,24,384]{4,3,2,1,0:T(8,128)(2,1)S(1)}, u32[]{:S(2)}, u32[]{:S(2)}) collective-permute-start(bf16[4,2,12,24,384]{4,3,2,1,0:T(8,128)(2,1)} %get-tuple-element.164), channel_id=1, source_target_pairs={{0,8},{1,9},{2,10},{3,11},{4,12},{5,13},{6,14},{7,15},{8,16},{9,17... | collective-permute-start | bytes 5308424 | tf_op jit(solution)/shard_map/ppermute | solution.py:48
  282.2 42.9 %collective-permute-start.41 = (bf16[4,2,12,24,384]{4,3,2,1,0:T(8,128)(2,1)}, bf16[4,2,12,24,384]{4,3,2,1,0:T(8,128)(2,1)S(1)}, u32[]{:S(2)}, u32[]{:S(2)}) collective-permute-start(bf16[4,2,12,24,384]{4,3,2,1,0:T(8,128)(2,1)} %get-tuple-element.165), channel_id=1, source_target_pairs={{0,16},{1,17},{2,18},{3,19},{4,20},{5,21},{6,22},{7,23},{8,24},{9,... | collective-permute-start | bytes 5308424 | tf_op jit(solution)/shard_map/ppermute | solution.py:48
  282.6 48.0 %collective-permute-start.42 = (bf16[4,2,12,24,384]{4,3,2,1,0:T(8,128)(2,1)}, bf16[4,2,12,24,384]{4,3,2,1,0:T(8,128)(2,1)}, u32[]{:S(2)}, u32[]{:S(2)}) collective-permute-start(bf16[4,2,12,24,384]{4,3,2,1,0:T(8,128)(2,1)} %get-tuple-element.166), channel_id=1, source_target_pairs={{0,24},{1,25},{2,26},{3,27},{4,28},{5,29},{6,30},{7,31},{8,0},{9,1... | collective-permute-start | bytes 5308424 | tf_op jit(solution)/shard_map/ppermute | solution.py:48
  302.1 22.9 %collective-permute-start.38 = (bf16[512,768]{1,0:T(8,128)(2,1)}, bf16[512,768]{1,0:T(8,128)(2,1)S(1)}, u32[]{:S(2)}, u32[]{:S(2)}) collective-permute-start(bf16[512,768]{1,0:T(8,128)(2,1)} %get-tuple-element.162), channel_id=1, source_target_pairs={{0,32},{1,33},{2,34},{3,35},{4,36},{5,37},{6,38},{7,39},{8,40},{9,... | collective-permute-start | bytes 2359304 | tf_op jit(solution)/shard_map/ppermute | solution.py:48
  309.1 28.5 %collective-permute-start.43 = (bf16[4,2,4,24,384]{4,3,2,1,0:T(8,128)(2,1)}, bf16[4,2,4,24,384]{4,3,2,1,0:T(8,128)(2,1)}, u32[]{:S(2)}, u32[]{:S(2)}) collective-permute-start(bf16[4,2,4,24,384]{4,3,2,1,0:T(8,128)(2,1)} %get-tuple-element.179), channel_id=1, source_target_pairs={{0,8},{1,9},{2,10},{3,11},{4,12},{5,13},{6,14},{7,15},{8,16},{9,17... | collective-permute-start | bytes 1769480 | tf_op jit(solution)/shard_map/ppermute | solution.py:48
  (61 other events, 494.1 us)
Sparse Core Ops, SparseCore 0:
  63.2 21.1 all-gather.1
  223.2 30.3 reduce-scatter.2
  269.5 16.9 reduce-scatter.4

commit v4 on v3

--- a/solution.py
+++ b/solution.py
@@ -439,6 +439,11 @@
     ]
 
 
+def lane_mask(hh):
+    lane = lax.broadcasted_iota(jnp.int32, (1, 128), 1)
+    return jnp.where((lane < 64) == (hh == 0), 1.0, 0.0).astype(BF)
+
+
 def three(column):
     hi = column.astype(BF).astype(F32)
     mid = (column - hi).astype(BF).astype(F32)
@@ -469,36 +474,42 @@
     ids = idc[...]
     lane_k = lanes(4 * tok)
     lane_q = lanes(tok)
+    masks = [lane_mask(hh) for hh in range(2)]
+    feats = [
+        place(lane_k, 64 * (1 - hh), [-1e30 * (1 - ids), -1e30 * ids]).astype(BF) for hh in range(2)
+    ]
+    own = ids[: 2 * tok, :]
+    lane_2 = lanes(2 * tok)
+    feats_q = [place(lane_2, 64 * (1 - hh), [own, 1 - own]).astype(BF) for hh in range(2)]
     lse_all = [jnp.zeros((tok, 128), F32) for _ in range(2)]
-    for t in range(3):
+    items = [(t, hh, b) for t in range(3) for hh in range(2) for b in range(2)]
+
+    def scores(item):
+        t, hh, b = item
         cols = slice(t * 128, (t + 1) * 128)
-        tiles = [[], []]
-        for hh in range(2):
-            base = 64 * (1 - hh)
-            sel_k = (lane_k < 64) == (hh == 0)
-            sel_q = (lane_q < 64) == (hh == 0)
-            kk = jnp.where(
-                sel_k, k_ref[:, cols].astype(F32), place(lane_k, base, [-1e30 * (1 - ids), -1e30 * ids])
-            ).astype(BF)
-            vv = jnp.where(sel_k, v_ref[:, cols].astype(F32), 1.0).astype(BF)
-            for b in range(2):
-                rows = slice(b * tok, (b + 1) * tok)
-                idq = ids[rows, :]
-                qq = jnp.where(
-                    sel_q,
-                    q_ref[rows, cols].astype(F32) * HD**-0.5,
-                    place(lane_q, base, [idq, 1 - idq]),
-                ).astype(BF)
-                s = fdot(qq, kk, 1, 1)
-                peak = jnp.max(s, -1, keepdims=True)
-                e = jnp.exp(s - peak).astype(BF)
-                o = fdot(e, vv)
-                total = o[:, base : base + 1]
-                lse = peak + jnp.log(total)
-                lse_all[b] = jnp.where(lane_q == 2 * t + hh, lse, lse_all[b])
-                tiles[b].append(o / total)
-        for b, out in enumerate((own_ref, oth_ref)):
-            o = jnp.where(lane_q < 64, tiles[b][0], tiles[b][1])
+        rows = slice(b * tok, (b + 1) * tok)
+        kk = k_ref[:, cols] * masks[hh] + feats[hh]
+        qq = q_ref[rows, cols] * (masks[hh] * BF(HD**-0.5)) + feats_q[hh][rows, :]
+        return fdot(qq, kk, 1, 1)
+
+    ahead = scores(items[0])
+    tiles = {}
+    for n, (t, hh, b) in enumerate(items):
+        cols = slice(t * 128, (t + 1) * 128)
+        s = ahead
+        if n + 1 < len(items):
+            ahead = scores(items[n + 1])
+        base = 64 * (1 - hh)
+        peak = jnp.max(s, -1, keepdims=True)
+        e = jnp.exp(s - peak).astype(BF)
+        o = fdot(e, v_ref[:, cols] * masks[hh] + masks[1 - hh])
+        total = o[:, base : base + 1]
+        lse = peak + jnp.log(total)
+        lse_all[b] = jnp.where(lane_q == 2 * t + hh, lse, lse_all[b])
+        tiles[hh, b] = o / total
+        if hh == 1:
+            out = oth_ref if b else own_ref
+            o = jnp.where(lane_q < 64, tiles[0, b], tiles[1, b])
             o32_ref[b * tok : (b + 1) * tok, cols] = o
             out[:, cols] = o.astype(BF)
     for b in range(2):
@@ -758,9 +769,31 @@
     ids = idc[...]
     near = 2 * tok
     lane_q = lanes(near)
-    lane_k = lanes(near)
+    masks = [lane_mask(hh) for hh in range(2)]
+    feats_q = [place(lane_q, 64 * (1 - hh), [ids[:near, :], 1 - ids[:near, :]]) for hh in range(2)]
+    feats_k = [
+        [
+            place(
+                lane_q,
+                64 * (1 - hh),
+                [
+                    -1e30 * (1 - ids[b * near : (b + 1) * near, :]),
+                    -1e30 * ids[b * near : (b + 1) * near, :],
+                    1.0,
+                    1.0,
+                    1.0,
+                ],
+            ).astype(BF)
+            for b in range(2)
+        ]
+        for hh in range(2)
+    ]
+    feats_v = [place(lane_q[:8], 64 * (1 - hh), [1.0] * 3)[0:1].astype(BF) for hh in range(2)]
     for t in range(3):
         cols = slice(t * 128, (t + 1) * 128)
+        k_turned = [
+            k_ref[b * near : (b + 1) * near, cols].astype(F32).T.astype(BF) for b in range(2)
+        ]
         gq_tile = []
         gk_tile = [[], []]
         gv_tile = [[], []]
@@ -771,34 +804,25 @@
             go32 = go_ref[:, cols].astype(F32)
             inner = jnp.sum(jnp.where(sel, go32 * o32_ref[:, cols], 0.0), -1, keepdims=True)
             lse = lse_ref[:, h : h + 1]
-            idq = ids[:near, :]
-            qq = jnp.where(
-                sel,
-                q_ref[:, cols].astype(F32) * HD**-0.5,
-                place(lane_q, base, [idq, 1 - idq] + three(-lse)),
-            ).astype(BF)
-            gg = jnp.where(sel, go32, place(lane_q, base, three(-inner))).astype(BF)
+            scaled = q_ref[:, cols] * (masks[hh] * BF(HD**-0.5))
+            lse3 = place(lane_q, base + 2, three(-lse)) + feats_q[hh]
+            qq = scaled + lse3.astype(BF)
+            gg = go_ref[:, cols] * masks[hh] + place(lane_q, base, three(-inner)).astype(BF)
             gq = None
             for b in range(2):
                 rows = slice(b * near, (b + 1) * near)
-                idk = ids[rows, :]
-                kk = jnp.where(
-                    sel,
-                    k_ref[rows, cols].astype(F32),
-                    place(lane_k, base, [-1e30 * (1 - idk), -1e30 * idk, 1.0, 1.0, 1.0]),
-                ).astype(BF)
-                vv = jnp.where(
-                    sel, v_ref[rows, cols].astype(F32), place(lane_k, base, [1.0, 1.0, 1.0])
-                ).astype(BF)
+                kk = k_ref[rows, cols] * masks[hh] + feats_k[hh][b]
+                vv = v_ref[rows, cols] * masks[hh] + feats_v[hh]
                 prob = jnp.exp(fdot(kk, qq, 1, 1))
                 gs = (prob * fdot(vv, gg, 1, 1)).astype(BF)
                 gv_tile[b].append(fdot(prob.astype(BF), go_ref[:, cols]))
                 gk_tile[b].append(fdot(gs, q_ref[:, cols]))
-                part = fdot(gs, k_ref[rows, cols], 0, 0)
+                part = fdot(k_turned[b], gs)
                 gq = part if gq is None else gq + part
             gq_tile.append(gq)
         left = lane_q < 64
-        gq_ref[:, cols] = (jnp.where(left, gq_tile[0], gq_tile[1]) * HD**-0.5).astype(BF)
+        turned = jnp.concatenate([gq_tile[0][:64], gq_tile[1][64:]], 0)
+        gq_ref[:, cols] = (turned.T * HD**-0.5).astype(BF)
         for b in range(2):
             rows = slice(b * near, (b + 1) * near)
             gk_ref[rows, cols] = (jnp.where(left, *gk_tile[b]) * HD**-0.5).astype(BF)

time: 404 us -> 399 us (0.988)
  Pallas kernels: 171 us -> 165 us
  transfers between devices with their start and end apart: 58 -> 58, of which waited for: 24 -> 23; matrix products, arithmetic and copies ran while one was open for 3% -> 3% of each run, Pallas kernels for 34% -> 33%
where the time goes in v4:
time: 399 us; the launch traced here: 394 us
  Pallas kernels  165 us (41%)
  waiting for transfers between devices  111 us (28%)
  starting transfers between devices  79.8 us (20%)
  between operations  14.8 us (4%)
  local copies, waits for them, and re-layouts  12.7 us (3%)
  other arithmetic  9.7 us (2%)
    ppermute x55, waiting for transfers between devices, shift(): return lax.ppermute(array, AXES, pairs)  111 us
    ppermute x55, starting transfers between devices, shift(): return lax.ppermute(array, AXES, pairs)  79.1 us
    pallas_call x2, Pallas kernels, attn_bwd(): pl.pallas_call(functools.partial(attn_bwd_kernel, row, len(raw), len(deps...  31.8 us
    pallas_call x2, Pallas kernels, mlp_bwd(): pl.pallas_call(functools.partial(mlp_bwd_kernel, row, first, len(weights)...  22.1 us
    pallas_call x2, Pallas kernels, attn_fwd(): pl.pallas_call(functools.partial(attn_fwd_kernel, raw, row, len(deps)), o...  21.3 us
    pallas_call x2, Pallas kernels, mlp_fwd(): pl.pallas_call(functools.partial(mlp_fwd_kernel, row, last, len(weights))...  19.9 us
    pallas_call x2, Pallas kernels, mlp_grad(): pl.pallas_call(functools.partial(mlp_grad_kernel, more), out_shape=blocks...  18.8 us
    pallas_call x1, Pallas kernels, assemble_both(): pl.pallas_call(functools.partial(assemble_both_kernel, begin), out_shape=...  12.6 us
  transfers between devices with their start and end apart: 58, of which 23 were waited for; matrix products, arithmetic and copies ran while one was open for 3% of the time, Pallas kernels for 33%

profile of v4, /device:TPU:1, one launch (start us, length us, event | category | flops | bytes accessed | tf_op | source)
XLA Modules:
  0.0 393.6 jit_solution(9511360238857893501)
XLA Ops:
  28.6 5.7 %collective-permute-done.7 = bf16[9,24,384]{2,1,0:T(8,128)(2,1)S(1)} collective-permute-done((bf16[9,24,384]{2,1,0:T(8,128)(2,1)}, bf16[9,24,384]{2,1,0:T(8,128)(2,1)S(1)}, u32[]{:S(2)}, u32[]{:S(2)}) %collective-permute-start.7) | collective-permute-done | bytes 165920 | tf_op jit(solution)/shard_map/ppermute | solution.py:48
  43.4 10.2 %collective-permute-done.10.refs_3_ = bf16[4,2,4,24,384]{4,3,2,1,0:T(8,128)(2,1)S(1)} collective-permute-done((bf16[4,2,4,24,384]{4,3,2,1,0:T(8,128)(2,1)}, bf16[4,2,4,24,384]{4,3,2,1,0:T(8,128)(2,1)S(1)}, u32[]{:S(2)}, u32[]{:S(2)}) %collective-permute-start.10) | collective-permute-done | bytes 589856 | tf_op jit(solution)/shard_map/ppermute | solution.py:48
  68.9 11.1 %shard_map.279 = (bf16[1024,768]{1,0:T(8,128)(2,1)}, bf16[512,384]{1,0:T(8,128)(2,1)}, bf16[1024,384]{1,0:T(8,128)(2,1)}, bf16[1024,384]{1,0:T(8,128)(2,1)}, f32...) custom-call(s32[1]{0:T(128)} %bitcast.core, ...), custom_call_target="tpu_custom_call" | custom-call | flops 1000000 | bytes 100000 | tf_op jit(solution)/shard_map/pallas_call | solution.py:534
  90.2 10.6 %collective-permute-done.18.refs_0_ = bf16[4,2,9,24,384]{4,3,2,1,0:T(8,128)(2,1)} collective-permute-done((bf16[4,2,9,24,384]{4,3,2,1,0:T(8,128)(2,1)}, bf16[4,2,9,24,384]{4,3,2,1,0:T(8,128)(2,1)}, u32[]{:S(2)}, u32[]{:S(2)}) %collective-permute-start.18) | collective-permute-done | bytes 1327136 | tf_op jit(solution)/shard_map/ppermute | solution.py:48
  106.3 10.7 %collective-permute-done.16.refs_0_ = bf16[4,2,9,24,384]{4,3,2,1,0:T(8,128)(2,1)S(1)} collective-permute-done((bf16[4,2,9,24,384]{4,3,2,1,0:T(8,128)(2,1)}, bf16[4,2,9,24,384]{4,3,2,1,0:T(8,128)(2,1)S(1)}, u32[]{:S(2)}, u32[]{:S(2)}) %collective-permute-start.16) | collective-permute-done | bytes 1327136 | tf_op jit(solution)/shard_map/ppermute | solution.py:48
  123.5 12.6 %shard_map.288 = (bf16[2,5,32,24,384]{4,3,2,1,0:T(8,128)(2,1)}, bf16[2,32,4,24,384]{4,3,2,1,0:T(8,128)(2,1)}) custom-call(s32[1]{0:T(128)} %bitcast.core, s32[32]{0:T(128)S(1)} %select_n.188.table, s32[32]{0:T(128)S(1)} %select_n.203.table_o, bf16[4,2,9,24,384]{4,3,2,1,0:T(8,128)(2,1)} %pad_maximum_fusion.refs_0_, bf16[4,2,9,24,384]{4,3,2,1,0:T(8,128)(2,1)S(1)} %copy-done.3, ...), custom_call_target="tpu_custom_call" | custom-call | flops 1000000 | bytes 100000 | tf_op jit(solution)/shard_map/pallas_call | solution.py:259
  136.1 10.8 %shard_map.289 = (f32[256,768]{1,0:T(8,128)}, bf16[256,4608]{1,0:T(8,128)(2,1)}, f32[256,3072]{1,0:T(8,128)}, f32[256,768]{1,0:T(8,128)}, bf16[256,768]{1,0:T(8,128)(2,1)}) custom-call(s32[1]{0:T(128)} %bitcast.core, bf16[256,768]{1,0:T(8,128)(2,1)} %bitcast.1.x0.x.rest_0_, bf16[256,384]{1,0:T(8,128)(2,1)} %get-tuple-element.114.refs_1_.o_own, ...), custom_call_target="tpu_custom_call" | custom-call | flops 1000000 | bytes 100000 | tf_op jit(solution)/shard_map/pallas_call | solution.py:635
  150.6 7.3 %collective-permute-done.24.refs_5_.x2 = bf16[256,768]{1,0:T(8,128)(2,1)S(1)} collective-permute-done((bf16[256,768]{1,0:T(8,128)(2,1)}, bf16[256,768]{1,0:T(8,128)(2,1)S(1)}, u32[]{:S(2)}, u32[]{:S(2)}) %collective-permute-start.24) | collective-permute-done | bytes 393248 | tf_op jit(solution)/shard_map/ppermute | solution.py:48
  163.1 8.0 %shard_map.293 = (bf16[3,32,24,384]{3,2,1,0:T(8,128)(2,1)}, bf16[5,32,24,384]{3,2,1,0:T(8,128)(2,1)}, bf16[32,4,24,384]{3,2,1,0:T(8,128)(2,1)}) custom-call(s32[32]{0:T(128)S(1)} %select_n.205.table, bf16[4,2,12,24,384]{4,3,2,1,0:T(8,128)(2,1)S(1)} %copy-done, bf16[4,2,12,24,384]{4,3,2,1,0:T(8,128)(2,1)} %shard_map.290.refs_1_, ...), custom_call_target="tpu_custom_call" | custom-call | flops 1000000 | bytes 100000 | tf_op jit(solution)/shard_map/pallas_call | solution.py:180
  174.9 10.2 %shard_map.294 = (bf16[1024,768]{1,0:T(8,128)(2,1)}, bf16[512,384]{1,0:T(8,128)(2,1)}, bf16[1024,384]{1,0:T(8,128)(2,1)}, bf16[1024,384]{1,0:T(8,128)(2,1)}, f32...) custom-call(s32[1]{0:T(128)} %bitcast.core, ...), custom_call_target="tpu_custom_call" | custom-call | flops 1000000 | bytes 100000 | tf_op jit(solution)/shard_map/pallas_call | solution.py:534
  186.9 9.0 %shard_map.295 = (f32[256,768]{1,0:T(8,128)}, bf16[256,4608]{1,0:T(8,128)(2,1)}, f32[256,3072]{1,0:T(8,128)}, bf16[256,768]{1,0:T(8,128)(2,1)}) custom-call(s32[1]{0:T(128)} %bitcast.core, f32[256,768]{1,0:T(8,128)} %get-tuple-element.119.refs_1_.x.rest_0_, bf16[256,384]{1,0:T(8,128)(2,1)} %get-tuple-element.122.o_own, ...), custom_call_target="tpu_custom_call" | custom-call | flops 1000000 | bytes 100000 | tf_op jit(solution)/shard_map/pallas_call | solution.py:635
  196.6 9.9 %shard_map.296 = (f32[256,768]{1,0:T(8,128)}, bf16[256,2688]{1,0:T(8,128)(2,1)}, bf16[256,2688]{1,0:T(8,128)(2,1)}, f32[16,768]{1,0:T(8,128)}, f32[1,3072]{1,0:T(1,128)}) custom-call(s32[1]{0:T(128)} %bitcast.core, f32[32,768]{1,0:T(8,128)} %get-tuple-element.113.vec, f32[256,768]{1,0:T(8,128)} %get-tuple-element.129.m_ref, ...), custom_call_target="tpu_custom_call" | custom-call | flops 1000000 | bytes 100000 | tf_op jit(solution)/shard_map/pallas_call | solution.py:716
  209.9 9.2 %shard_map.297.rest_3_ = bf16[4,4,2,9,24,384]{5,4,3,2,1,0:T(8,128)(2,1)} custom-call(s32[32]{0:T(128)S(1)} %select_n.207.table, bf16[256,4608]{1,0:T(8,128)(2,1)} %get-tuple-element.139.f0, bf16[256,4608]{1,0:T(8,128)(2,1)} %collective-permute-done.33.f1, bf16[256,2688]{1,0:T(8,128)(2,1)} %get-tuple-element.137.b0.rest_0_, ...), custom_call_target="tpu_custom_call" | custom-call | flops 1000000 | bytes 100000 | tf_op jit(solution)/shard_map/pallas_call | solution.py:991
  219.6 15.4 %shard_map.298 = (bf16[512,384]{1,0:T(8,128)(2,1)}, bf16[1024,384]{1,0:T(8,128)(2,1)}, bf16[1024,384]{1,0:T(8,128)(2,1)}, f32[256,768]{1,0:T(8,128)}, f32[256,76...) custom-call(bf16[512,384]{1,0:T(8,128)(2,1)} %get-tuple-element.132.q_ref, ...), custom_call_target="tpu_custom_call" | custom-call | flops 1000000 | bytes 100000 | tf_op jit(solution)/shard_map/pallas_call | solution.py:872
  241.1 5.6 %shard_map.299 = (bf16[4,2,12,24,384]{4,3,2,1,0:T(8,128)(2,1)}, bf16[4,2,12,24,384]{4,3,2,1,0:T(8,128)(2,1)}, bf16[4,2,12,24,384]{4,3,2,1,0:T(8,128)(2,1)}, bf16[4,2,12,24,384]{4,3,2,1,0:T(8,128)(2,1)}) custom-call(s32[32]{0:T(128)S(1)} %select_n.210.table, bf16[1024,768]{1,0:T(8,128)(2,1)} %get-tuple-element.143.a_ref, ...), custom_call_target="tpu_custom_call" | custom-call | flops 1000000 | bytes 100000 | tf_op jit(solution)/shard_map/pallas_call | solution.py:1025
  251.1 12.2 %shard_map.300 = (f32[256,768]{1,0:T(8,128)}, bf16[256,2688]{1,0:T(8,128)(2,1)}, bf16[256,2688]{1,0:T(8,128)(2,1)}, f32[16,768]{1,0:T(8,128)}, f32[1,3072]{1,0:T(1,128)}) custom-call(s32[1]{0:T(128)} %bitcast.core, f32[32,768]{1,0:T(8,128)} %get-tuple-element.113.vec, f32[256,768]{1,0:T(8,128)} %get-tuple-element.127.m_ref, ...), custom_call_target="tpu_custom_call" | custom-call | flops 1000000 | bytes 100000 | tf_op jit(solution)/shard_map/pallas_call | solution.py:716
  267.4 9.6 %shard_map.301 = (bf16[4,2,12,24,384]{4,3,2,1,0:T(8,128)(2,1)}, bf16[4,2,12,24,384]{4,3,2,1,0:T(8,128)(2,1)}, bf16[4,2,12,24,384]{4,3,2,1,0:T(8,128)(2,1)}, bf16[4,2,12,24,384]{4,3,2,1,0:T(8,128)(2,1)}) custom-call(s32[32]{0:T(128)S(1)} %select_n.210.table, ...), custom_call_target="tpu_custom_call", output_to_operand_aliasing={{0}: (5, {}), {1}: (6, {}), {2}: (7, {}), {3}: (8, {})} | custom-call | flops 1000000 | bytes 100000 | tf_op jit(solution)/shard_map/pallas_call | solution.py:991
  280.0 16.3 %shard_map.303 = (bf16[512,384]{1,0:T(8,128)(2,1)}, bf16[1024,384]{1,0:T(8,128)(2,1)}, bf16[1024,384]{1,0:T(8,128)(2,1)}, f32[256,768]{1,0:T(8,128)}, f32[256,76...) custom-call(bf16[512,384]{1,0:T(8,128)(2,1)} %get-tuple-element.149.q_ref, ...), custom_call_target="tpu_custom_call" | custom-call | flops 1000000 | bytes 100000 | tf_op jit(solution)/shard_map/pallas_call | solution.py:872
  297.5 5.8 %shard_map.305 = (bf16[4,2,4,24,384]{4,3,2,1,0:T(8,128)(2,1)}, bf16[4,2,4,24,384]{4,3,2,1,0:T(8,128)(2,1)}, bf16[4,2,4,24,384]{4,3,2,1,0:T(8,128)(2,1)}, bf16[4,2,4,24,384]{4,3,2,1,0:T(8,128)(2,1)}) custom-call(s32[32]{0:T(128)S(1)} %select_n.210.table, s32[1]{0:T(128)} %bitcast.core, bf16[1024,768]{1,0:T(8,128)(2,1)} %get-tuple-element.167.a_ref, ...), custom_call_target="tpu_custom_call" | custom-call | flops 1000000 | bytes 100000 | tf_op jit(solution)/shard_map/pallas_call | solution.py:944
  303.7 16.3 %collective-permute-done.40.refs_1_ = bf16[4,2,12,24,384]{4,3,2,1,0:T(8,128)(2,1)S(1)} collective-permute-done((bf16[4,2,12,24,384]{4,3,2,1,0:T(8,128)(2,1)}, bf16[4,2,12,24,384]{4,3,2,1,0:T(8,128)(2,1)S(1)}, u32[]{:S(2)}, u32[]{:S(2)}) %collective-permute-start.40) | collective-permute-done | bytes 1769504 | tf_op jit(solution)/shard_map/ppermute | solution.py:48
  325.7 7.0 %collective-permute-done.43.refs_5_ = bf16[4,2,4,24,384]{4,3,2,1,0:T(8,128)(2,1)} collective-permute-done((bf16[4,2,4,24,384]{4,3,2,1,0:T(8,128)(2,1)}, bf16[4,2,4,24,384]{4,3,2,1,0:T(8,128)(2,1)}, u32[]{:S(2)}, u32[]{:S(2)}) %collective-permute-start.43) | collective-permute-done | bytes 589856 | tf_op jit(solution)/shard_map/ppermute | solution.py:48
  335.7 4.9 %shard_map.307 = (bf16[2,16,24,384]{3,2,1,0:T(8,128)(2,1)}, bf16[2,16,24,384]{3,2,1,0:T(8,128)(2,1)}, bf16[2,16,24,384]{3,2,1,0:T(8,128)(2,1)}, bf16[2,16,24,384]{3,2,1,0:T(8,128)(2,1)}) custom-call(s32[1]{0:T(128)} %bitcast.34.place_at, bf16[4,2,12,24,384]{4,3,2,1,0:T(8,128)(2,1)} %get-tuple-element.160.rest_7_.refs_0_, ...), custom_call_target="tpu_custom_call" | custom-call | flops 1000000 | bytes 100000 | tf_op jit(solution)/shard_map/pallas_call | solution.py:357
  351.0 6.4 %collective-permute-done.47.refs_2_ = bf16[2,16,24,384]{3,2,1,0:T(8,128)(2,1)S(1)} collective-permute-done((bf16[2,16,24,384]{3,2,1,0:T(8,128)(2,1)}, bf16[2,16,24,384]{3,2,1,0:T(8,128)(2,1)S(1)}, u32[]{:S(2)}, u32[]{:S(2)}) %collective-permute-start.47) | collective-permute-done | bytes 589856 | tf_op jit(solution)/shard_map/ppermute | solution.py:48
  376.9 5.7 %collective-permute-start.51 = (bf16[16,24,384]{2,1,0:T(8,128)(2,1)S(1)}, bf16[16,24,384]{2,1,0:T(8,128)(2,1)S(1)}, u32[]{:S(2)}, u32[]{:S(2)}) collective-permute-start(bf16[16,24,384]{2,1,0:T(8,128)(2,1)S(1)} %add_convert_fusion.2.own0), channel_id=1, source_target_pairs={{0,32},{1,33},{2,34},{3,35},{4,36},{5,37},{6,38},{7,39},{8,40},{9,... | collective-permute-start | bytes 884744 | tf_op jit(solution)/shard_map/ppermute | solution.py:48
  (221 shorter events, 148.2 us)
Async XLA Ops:
  7.2 113.2 %all-gather.2.cloned.1.call-start = ((), (), s32[]{:S(2)}) async-start(), calls=%async_computation.2 | async-start | bytes 2211840 | tf_op jit(solution)/shard_map/all_gather | solution.py:1048
  25.1 43.8 %collective-permute-start = (bf16[256,768]{1,0:T(8,128)(2,1)}, bf16[256,768]{1,0:T(8,128)(2,1)}, u32[]{:S(2)}, u32[]{:S(2)}) collective-permute-start(bf16[256,768]{1,0:T(8,128)(2,1)} %bitcast.1.x0.x.rest_0_), channel_id=1, source_target_pairs={{0,32},{1,33},{2,34},{3,35},{4,36},{5,37},{6,38},{7,39},{8,40},{9,... | collective-permute-start | bytes 1179656 | tf_op jit(solution)/shard_map/ppermute | solution.py:48
  35.8 17.8 %collective-permute-start.10 = (bf16[4,2,4,24,384]{4,3,2,1,0:T(8,128)(2,1)}, bf16[4,2,4,24,384]{4,3,2,1,0:T(8,128)(2,1)S(1)}, u32[]{:S(2)}, u32[]{:S(2)}) collective-permute-start(bf16[4,2,4,24,384]{4,3,2,1,0:T(8,128)(2,1)} %shard_map.274.refs_1_.refs_0_), channel_id=1, source_target_pairs={{0,24},{1,25},{2,26},{3,27},{4,28},{5,29},{6,30},{7,31},{8,0},{9,1... | collective-permute-start | bytes 1769480 | tf_op jit(solution)/shard_map/ppermute | solution.py:48
  42.1 17.5 %collective-permute-start.11 = (bf16[12,24,384]{2,1,0:T(8,128)(2,1)}, bf16[12,24,384]{2,1,0:T(8,128)(2,1)S(1)}, u32[]{:S(2)}, u32[]{:S(2)}) collective-permute-start(bf16[12,24,384]{2,1,0:T(8,128)(2,1)} %shard_map.276), channel_id=1, source_target_pairs={{0,4},{1,5},{2,6},{3,7},{4,0},{5,1},{6,2},{7,3},{8,12},{9,13},{10,... | collective-permute-start | bytes 663560 | tf_op jit(solution)/shard_map/ppermute | solution.py:48
  58.4 21.7 %collective-permute-start.13 = (bf16[2,9,24,384]{3,2,1,0:T(8,128)(2,1)}, bf16[2,9,24,384]{3,2,1,0:T(8,128)(2,1)}, u32[]{:S(2)}, u32[]{:S(2)}) collective-permute-start(bf16[2,9,24,384]{3,2,1,0:T(8,128)(2,1)} %shard_map.275.refs_4_), channel_id=1, source_target_pairs={{0,1},{1,2},{2,3},{3,0},{4,5},{5,6},{6,7},{7,4},{8,9},{9,10},{10,1... | collective-permute-start | bytes 995336 | tf_op jit(solution)/shard_map/ppermute | solution.py:48
  59.7 20.4 %collective-permute-start.14 = (bf16[2,9,24,384]{3,2,1,0:T(8,128)(2,1)}, bf16[2,9,24,384]{3,2,1,0:T(8,128)(2,1)}, u32[]{:S(2)}, u32[]{:S(2)}) collective-permute-start(bf16[2,9,24,384]{3,2,1,0:T(8,128)(2,1)} %shard_map.275.refs_4_), channel_id=1, source_target_pairs={{0,2},{1,3},{2,0},{3,1},{4,6},{5,7},{6,4},{7,5},{8,10},{9,11},{10,... | collective-permute-start | bytes 995336 | tf_op jit(solution)/shard_map/ppermute | solution.py:48
  59.7 20.4 %collective-permute-start.15 = (bf16[2,9,24,384]{3,2,1,0:T(8,128)(2,1)}, bf16[2,9,24,384]{3,2,1,0:T(8,128)(2,1)}, u32[]{:S(2)}, u32[]{:S(2)}) collective-permute-start(bf16[2,9,24,384]{3,2,1,0:T(8,128)(2,1)} %shard_map.275.refs_4_), channel_id=1, source_target_pairs={{0,3},{1,0},{2,1},{3,2},{4,7},{5,4},{6,5},{7,6},{8,11},{9,8},{10,9... | collective-permute-start | bytes 995336 | tf_op jit(solution)/shard_map/ppermute | solution.py:48
  63.1 201.3 %reduce-scatter.3.cloned.1.call-start = ((), (), s32[]{:S(2)}) async-start(), calls=%async_computation.3 | async-start | bytes 6635520 | tf_op jit(solution)/shard_map/reduce_scatter | solution.py:1042
  83.5 17.2 %collective-permute-start.18 = (bf16[4,2,9,24,384]{4,3,2,1,0:T(8,128)(2,1)}, bf16[4,2,9,24,384]{4,3,2,1,0:T(8,128)(2,1)}, u32[]{:S(2)}, u32[]{:S(2)}) collective-permute-start(bf16[4,2,9,24,384]{4,3,2,1,0:T(8,128)(2,1)} %pad_maximum_fusion.refs_0_), channel_id=1, source_target_pairs={{0,24},{1,25},{2,26},{3,27},{4,28},{5,29},{6,30},{7,31},{8,0},{9,1... | collective-permute-start | bytes 3981320 | tf_op jit(solution)/shard_map/ppermute | solution.py:48
  84.1 19.6 %collective-permute-start.17 = (bf16[4,2,9,24,384]{4,3,2,1,0:T(8,128)(2,1)}, bf16[4,2,9,24,384]{4,3,2,1,0:T(8,128)(2,1)S(1)}, u32[]{:S(2)}, u32[]{:S(2)}) collective-permute-start(bf16[4,2,9,24,384]{4,3,2,1,0:T(8,128)(2,1)} %pad_maximum_fusion.refs_0_), channel_id=1, source_target_pairs={{0,16},{1,17},{2,18},{3,19},{4,20},{5,21},{6,22},{7,23},{8,24},{9,... | collective-permute-start | bytes 3981320 | tf_op jit(solution)/shard_map/ppermute | solution.py:48
  84.4 32.5 %collective-permute-start.16 = (bf16[4,2,9,24,384]{4,3,2,1,0:T(8,128)(2,1)}, bf16[4,2,9,24,384]{4,3,2,1,0:T(8,128)(2,1)S(1)}, u32[]{:S(2)}, u32[]{:S(2)}) collective-permute-start(bf16[4,2,9,24,384]{4,3,2,1,0:T(8,128)(2,1)} %pad_maximum_fusion.refs_0_), channel_id=1, source_target_pairs={{0,8},{1,9},{2,10},{3,11},{4,12},{5,13},{6,14},{7,15},{8,16},{9,17... | collective-permute-start | bytes 3981320 | tf_op jit(solution)/shard_map/ppermute | solution.py:48
  88.7 31.9 %collective-permute-start.19 = (bf16[4,2,9,24,384]{4,3,2,1,0:T(8,128)(2,1)}, bf16[4,2,9,24,384]{4,3,2,1,0:T(8,128)(2,1)}, u32[]{:S(2)}, u32[]{:S(2)}) collective-permute-start(bf16[4,2,9,24,384]{4,3,2,1,0:T(8,128)(2,1)} %pad_maximum_fusion.refs_0_), channel_id=1, source_target_pairs={{0,32},{1,33},{2,34},{3,35},{4,36},{5,37},{6,38},{7,39},{8,40},{9,... | collective-permute-start | bytes 3981320 | tf_op jit(solution)/shard_map/ppermute | solution.py:48
  100.8 22.0 %collective-permute-start.22 = (bf16[4,2,9,24,384]{4,3,2,1,0:T(8,128)(2,1)}, bf16[4,2,9,24,384]{4,3,2,1,0:T(8,128)(2,1)}, u32[]{:S(2)}, u32[]{:S(2)}) collective-permute-start(bf16[4,2,9,24,384]{4,3,2,1,0:T(8,128)(2,1)} %shard_map.285.refs_3_), channel_id=1, source_target_pairs={{0,32},{1,33},{2,34},{3,35},{4,36},{5,37},{6,38},{7,39},{8,40},{9,... | collective-permute-start | bytes 3981320 | tf_op jit(solution)/shard_map/ppermute | solution.py:48
  104.8 18.6 %collective-permute-start.21 = (bf16[4,2,9,24,384]{4,3,2,1,0:T(8,128)(2,1)}, bf16[4,2,9,24,384]{4,3,2,1,0:T(8,128)(2,1)}, u32[]{:S(2)}, u32[]{:S(2)}) collective-permute-start(bf16[4,2,9,24,384]{4,3,2,1,0:T(8,128)(2,1)} %shard_map.284.refs_2_), channel_id=1, source_target_pairs={{0,32},{1,33},{2,34},{3,35},{4,36},{5,37},{6,38},{7,39},{8,40},{9,... | collective-permute-start | bytes 3981320 | tf_op jit(solution)/shard_map/ppermute | solution.py:48
  120.5 39.9 %collective-permute-start.28 = (bf16[4,2,12,24,384]{4,3,2,1,0:T(8,128)(2,1)}, bf16[4,2,12,24,384]{4,3,2,1,0:T(8,128)(2,1)}, u32[]{:S(2)}, u32[]{:S(2)}) collective-permute-start(bf16[4,2,12,24,384]{4,3,2,1,0:T(8,128)(2,1)} %shard_map.287.refs_9_.refs_0_), channel_id=1, source_target_pairs={{0,24},{1,25},{2,26},{3,27},{4,28},{5,29},{6,30},{7,31},{8,0},{9,1... | collective-permute-start | bytes 5308424 | tf_op jit(solution)/shard_map/ppermute | solution.py:48
  120.6 39.8 %collective-permute-start.27 = (bf16[4,2,12,24,384]{4,3,2,1,0:T(8,128)(2,1)}, bf16[4,2,12,24,384]{4,3,2,1,0:T(8,128)(2,1)}, u32[]{:S(2)}, u32[]{:S(2)}) collective-permute-start(bf16[4,2,12,24,384]{4,3,2,1,0:T(8,128)(2,1)} %shard_map.287.refs_9_.refs_0_), channel_id=1, source_target_pairs={{0,16},{1,17},{2,18},{3,19},{4,20},{5,21},{6,22},{7,23},{8,24},{9,... | collective-permute-start | bytes 5308424 | tf_op jit(solution)/shard_map/ppermute | solution.py:48
  122.8 40.3 %collective-permute-start.26 = (bf16[4,2,12,24,384]{4,3,2,1,0:T(8,128)(2,1)}, bf16[4,2,12,24,384]{4,3,2,1,0:T(8,128)(2,1)}, u32[]{:S(2)}, u32[]{:S(2)}) collective-permute-start(bf16[4,2,12,24,384]{4,3,2,1,0:T(8,128)(2,1)} %shard_map.287.refs_9_.refs_0_), channel_id=1, source_target_pairs={{0,8},{1,9},{2,10},{3,11},{4,12},{5,13},{6,14},{7,15},{8,16},{9,17... | collective-permute-start | bytes 5308424 | tf_op jit(solution)/shard_map/ppermute | solution.py:48
  219.2 104.8 %reduce-scatter.5.cloned.1.call-start = ((), (), s32[]{:S(2)}) async-start(), calls=%async_computation.4 | async-start | bytes 1658880 | tf_op jit(solution)/shard_map/reduce_scatter | solution.py:1042
  235.3 29.1 %collective-permute-start.37 = (bf16[256,4608]{1,0:T(8,128)(2,1)}, bf16[256,4608]{1,0:T(8,128)(2,1)}, u32[]{:S(2)}, u32[]{:S(2)}) collective-permute-start(bf16[256,4608]{1,0:T(8,128)(2,1)} %get-tuple-element.156.f0), channel_id=1, source_target_pairs={{0,32},{1,33},{2,34},{3,35},{4,36},{5,37},{6,38},{7,39},{8,40},{9,... | collective-permute-start | bytes 7077896 | tf_op jit(solution)/shard_map/ppermute | solution.py:48
  276.9 43.1 %collective-permute-start.40 = (bf16[4,2,12,24,384]{4,3,2,1,0:T(8,128)(2,1)}, bf16[4,2,12,24,384]{4,3,2,1,0:T(8,128)(2,1)S(1)}, u32[]{:S(2)}, u32[]{:S(2)}) collective-permute-start(bf16[4,2,12,24,384]{4,3,2,1,0:T(8,128)(2,1)} %get-tuple-element.164), channel_id=1, source_target_pairs={{0,8},{1,9},{2,10},{3,11},{4,12},{5,13},{6,14},{7,15},{8,16},{9,17... | collective-permute-start | bytes 5308424 | tf_op jit(solution)/shard_map/ppermute | solution.py:48
  277.4 42.8 %collective-permute-start.41 = (bf16[4,2,12,24,384]{4,3,2,1,0:T(8,128)(2,1)}, bf16[4,2,12,24,384]{4,3,2,1,0:T(8,128)(2,1)S(1)}, u32[]{:S(2)}, u32[]{:S(2)}) collective-permute-start(bf16[4,2,12,24,384]{4,3,2,1,0:T(8,128)(2,1)} %get-tuple-element.165), channel_id=1, source_target_pairs={{0,16},{1,17},{2,18},{3,19},{4,20},{5,21},{6,22},{7,23},{8,24},{9,... | collective-permute-start | bytes 5308424 | tf_op jit(solution)/shard_map/ppermute | solution.py:48
  277.9 47.8 %collective-permute-start.42 = (bf16[4,2,12,24,384]{4,3,2,1,0:T(8,128)(2,1)}, bf16[4,2,12,24,384]{4,3,2,1,0:T(8,128)(2,1)}, u32[]{:S(2)}, u32[]{:S(2)}) collective-permute-start(bf16[4,2,12,24,384]{4,3,2,1,0:T(8,128)(2,1)} %get-tuple-element.166), channel_id=1, source_target_pairs={{0,24},{1,25},{2,26},{3,27},{4,28},{5,29},{6,30},{7,31},{8,0},{9,1... | collective-permute-start | bytes 5308424 | tf_op jit(solution)/shard_map/ppermute | solution.py:48
  296.4 23.7 %collective-permute-start.38 = (bf16[512,768]{1,0:T(8,128)(2,1)}, bf16[512,768]{1,0:T(8,128)(2,1)S(1)}, u32[]{:S(2)}, u32[]{:S(2)}) collective-permute-start(bf16[512,768]{1,0:T(8,128)(2,1)} %get-tuple-element.162), channel_id=1, source_target_pairs={{0,32},{1,33},{2,34},{3,35},{4,36},{5,37},{6,38},{7,39},{8,40},{9,... | collective-permute-start | bytes 2359304 | tf_op jit(solution)/shard_map/ppermute | solution.py:48
  303.4 29.3 %collective-permute-start.43 = (bf16[4,2,4,24,384]{4,3,2,1,0:T(8,128)(2,1)}, bf16[4,2,4,24,384]{4,3,2,1,0:T(8,128)(2,1)}, u32[]{:S(2)}, u32[]{:S(2)}) collective-permute-start(bf16[4,2,4,24,384]{4,3,2,1,0:T(8,128)(2,1)} %get-tuple-element.179), channel_id=1, source_target_pairs={{0,8},{1,9},{2,10},{3,11},{4,12},{5,13},{6,14},{7,15},{8,16},{9,17... | collective-permute-start | bytes 1769480 | tf_op jit(solution)/shard_map/ppermute | solution.py:48
  (61 other events, 491.3 us)
Sparse Core Ops, SparseCore 0:
  63.2 21.1 all-gather.1
  219.3 30.4 reduce-scatter.2
  264.6 17.0 reduce-scatter.4

commit v5 on v4

--- a/solution.py
+++ b/solution.py
@@ -1161,10 +1161,10 @@
     tokens_own = tokens[0]
     p1 = jnp.stack([u1, to_xl(u1)])
     p2 = jnp.stack([u2, to_xl(after(u2, p1))])
-    tokens_far = to_xh(after(tokens_own, p1))
+    tokens_far = to_xh(after(tokens_own, p2))
     share = [tokens_own, to_core(tokens_own), tokens_far, to_core(tokens_far)]
     s1 = three_inner(p1)
-    inner1 = after(inner_of(p1, s1), p2, idc, tokens_far)
+    inner1 = after(inner_of(p1, s1), p2, idc)
     pieces1 = [inner1] + three_outer(inner1)
     p2 = after(p2, *pieces1[1:])
     u3 = after(u3, inner1)
@@ -1172,7 +1172,7 @@
     p3 = after(p3, *pieces1[1:])
     inner3 = gather_along(p3, INNER)
     s2 = three_inner(p2)
-    qkv0, vec_rows, fins = assemble_first(table, pieces1, pin(p2, p3))
+    qkv0, vec_rows, fins = assemble_first(table, pieces1, pin(p2, p3) + [tokens_far])
     qkv0 = qkv0.reshape(3, width, UNIT)
     fwd0 = attn_fwd(True, 0, one, share, qkv0, vec_rows, idc)
     o_own, o_oth = fwd0[6:]

time: 399 us -> 394 us (0.987)
  waiting for transfers between devices: 111 us -> 98 us
  starting transfers between devices: 79.8 us -> 86.5 us
    ppermute x55, waiting for transfers between devices: 111 us -> 97.9 us  [shift(): return lax.ppermute(array, AXES, pairs)]
    ppermute x55, starting transfers between devices: 79.1 us -> 85.8 us  [shift(): return lax.ppermute(array, AXES, pairs)]
    unnamed x56 -> x52, local copies, waits for them, and re-layouts: 12 us -> 13.1 us
  transfers between devices with their start and end apart: 58 -> 58, of which waited for: 23 -> 24; matrix products, arithmetic and copies ran while one was open for 3% -> 3% of each run, Pallas kernels for 33% -> 33%
where the time goes in v5:
time: 394 us; the launch traced here: 388 us
  Pallas kernels  165 us (42%)
  waiting for transfers between devices  98 us (25%)
  starting transfers between devices  86.5 us (22%)
  between operations  14.7 us (4%)
  local copies, waits for them, and re-layouts  14.5 us (4%)
  other arithmetic  9.72 us (2%)
    ppermute x55, waiting for transfers between devices, shift(): return lax.ppermute(array, AXES, pairs)  97.9 us
    ppermute x55, starting transfers between devices, shift(): return lax.ppermute(array, AXES, pairs)  85.8 us
    pallas_call x2, Pallas kernels, attn_bwd(): pl.pallas_call(functools.partial(attn_bwd_kernel, row, len(raw), len(deps...  31.7 us
    pallas_call x2, Pallas kernels, mlp_bwd(): pl.pallas_call(functools.partial(mlp_bwd_kernel, row, first, len(weights)...  22.2 us
    pallas_call x2, Pallas kernels, attn_fwd(): pl.pallas_call(functools.partial(attn_fwd_kernel, raw, row, len(deps)), o...  21.3 us
    pallas_call x2, Pallas kernels, mlp_fwd(): pl.pallas_call(functools.partial(mlp_fwd_kernel, row, last, len(weights))...  19.9 us
    pallas_call x2, Pallas kernels, mlp_grad(): pl.pallas_call(functools.partial(mlp_grad_kernel, more), out_shape=blocks...  18.5 us
    unnamed x52, local copies, waits for them, and re-layouts  13.1 us
  transfers between devices with their start and end apart: 58, of which 24 were waited for; matrix products, arithmetic and copies ran while one was open for 3% of the time, Pallas kernels for 33%

profile of v5, /device:TPU:1, one launch (start us, length us, event | category | flops | bytes accessed | tf_op | source)
XLA Modules:
  0.0 388.3 jit_solution(16687934006474186728)
XLA Ops:
  38.0 5.6 %collective-permute-done.3.refs_6_.x2.rest_2_ = bf16[256,768]{1,0:T(8,128)(2,1)S(1)} collective-permute-done((bf16[256,768]{1,0:T(8,128)(2,1)}, bf16[256,768]{1,0:T(8,128)(2,1)S(1)}, u32[]{:S(2)}, u32[]{:S(2)}) %collective-permute-start.3) | collective-permute-done | bytes 393248 | tf_op jit(solution)/shard_map/ppermute | solution.py:48
  43.6 6.7 %collective-permute-start = (bf16[256,768]{1,0:T(8,128)(2,1)}, bf16[256,768]{1,0:T(8,128)(2,1)}, u32[]{:S(2)}, u32[]{:S(2)}) collective-permute-start(bf16[256,768]{1,0:T(8,128)(2,1)} %bitcast.1.x0.x.rest_0_), channel_id=1, source_target_pairs={{0,32},{1,33},{2,34},{3,35},{4,36},{5,37},{6,38},{7,39},{8,40},{9,... | collective-permute-start | bytes 1179656 | tf_op jit(solution)/shard_map/ppermute | solution.py:48
  62.4 11.1 %shard_map.279 = (bf16[1024,768]{1,0:T(8,128)(2,1)}, bf16[512,384]{1,0:T(8,128)(2,1)}, bf16[1024,384]{1,0:T(8,128)(2,1)}, bf16[1024,384]{1,0:T(8,128)(2,1)}, f32...) custom-call(s32[1]{0:T(128)} %bitcast.core, ...), custom_call_target="tpu_custom_call" | custom-call | flops 1000000 | bytes 100000 | tf_op jit(solution)/shard_map/pallas_call | solution.py:534
  84.3 11.0 %collective-permute-done.18.refs_0_ = bf16[4,2,9,24,384]{4,3,2,1,0:T(8,128)(2,1)} collective-permute-done((bf16[4,2,9,24,384]{4,3,2,1,0:T(8,128)(2,1)}, bf16[4,2,9,24,384]{4,3,2,1,0:T(8,128)(2,1)}, u32[]{:S(2)}, u32[]{:S(2)}) %collective-permute-start.18) | collective-permute-done | bytes 1327136 | tf_op jit(solution)/shard_map/ppermute | solution.py:48
  100.0 11.7 %collective-permute-done.16.refs_0_ = bf16[4,2,9,24,384]{4,3,2,1,0:T(8,128)(2,1)S(1)} collective-permute-done((bf16[4,2,9,24,384]{4,3,2,1,0:T(8,128)(2,1)}, bf16[4,2,9,24,384]{4,3,2,1,0:T(8,128)(2,1)S(1)}, u32[]{:S(2)}, u32[]{:S(2)}) %collective-permute-start.16) | collective-permute-done | bytes 1327136 | tf_op jit(solution)/shard_map/ppermute | solution.py:48
  118.2 12.6 %shard_map.288 = (bf16[2,5,32,24,384]{4,3,2,1,0:T(8,128)(2,1)}, bf16[2,32,4,24,384]{4,3,2,1,0:T(8,128)(2,1)}) custom-call(s32[1]{0:T(128)} %bitcast.core, s32[32]{0:T(128)S(1)} %select_n.188.table, s32[32]{0:T(128)S(1)} %select_n.203.table_o, bf16[4,2,9,24,384]{4,3,2,1,0:T(8,128)(2,1)} %pad_maximum_fusion.refs_0_, bf16[4,2,9,24,384]{4,3,2,1,0:T(8,128)(2,1)S(1)} %copy-done.3, ...), custom_call_target="tpu_custom_call" | custom-call | flops 1000000 | bytes 100000 | tf_op jit(solution)/shard_map/pallas_call | solution.py:259
  130.8 10.8 %shard_map.289 = (f32[256,768]{1,0:T(8,128)}, bf16[256,4608]{1,0:T(8,128)(2,1)}, f32[256,3072]{1,0:T(8,128)}, f32[256,768]{1,0:T(8,128)}, bf16[256,768]{1,0:T(8,128)(2,1)}) custom-call(s32[1]{0:T(128)} %bitcast.core, bf16[256,768]{1,0:T(8,128)(2,1)} %bitcast.1.x0.x.rest_0_, bf16[256,384]{1,0:T(8,128)(2,1)} %get-tuple-element.114.refs_1_.o_own, ...), custom_call_target="tpu_custom_call" | custom-call | flops 1000000 | bytes 100000 | tf_op jit(solution)/shard_map/pallas_call | solution.py:635
  145.6 7.7 %collective-permute-done.24.refs_5_.x2 = bf16[256,768]{1,0:T(8,128)(2,1)S(1)} collective-permute-done((bf16[256,768]{1,0:T(8,128)(2,1)}, bf16[256,768]{1,0:T(8,128)(2,1)S(1)}, u32[]{:S(2)}, u32[]{:S(2)}) %collective-permute-start.24) | collective-permute-done | bytes 393248 | tf_op jit(solution)/shard_map/ppermute | solution.py:48
  157.8 8.0 %shard_map.293 = (bf16[3,32,24,384]{3,2,1,0:T(8,128)(2,1)}, bf16[5,32,24,384]{3,2,1,0:T(8,128)(2,1)}, bf16[32,4,24,384]{3,2,1,0:T(8,128)(2,1)}) custom-call(s32[32]{0:T(128)S(1)} %select_n.205.table, bf16[4,2,12,24,384]{4,3,2,1,0:T(8,128)(2,1)S(1)} %copy-done, bf16[4,2,12,24,384]{4,3,2,1,0:T(8,128)(2,1)} %shard_map.290.refs_1_, ...), custom_call_target="tpu_custom_call" | custom-call | flops 1000000 | bytes 100000 | tf_op jit(solution)/shard_map/pallas_call | solution.py:180
  168.6 10.2 %shard_map.294 = (bf16[1024,768]{1,0:T(8,128)(2,1)}, bf16[512,384]{1,0:T(8,128)(2,1)}, bf16[1024,384]{1,0:T(8,128)(2,1)}, bf16[1024,384]{1,0:T(8,128)(2,1)}, f32...) custom-call(s32[1]{0:T(128)} %bitcast.core, ...), custom_call_target="tpu_custom_call" | custom-call | flops 1000000 | bytes 100000 | tf_op jit(solution)/shard_map/pallas_call | solution.py:534
  180.5 9.0 %shard_map.295 = (f32[256,768]{1,0:T(8,128)}, bf16[256,4608]{1,0:T(8,128)(2,1)}, f32[256,3072]{1,0:T(8,128)}, bf16[256,768]{1,0:T(8,128)(2,1)}) custom-call(s32[1]{0:T(128)} %bitcast.core, f32[256,768]{1,0:T(8,128)} %get-tuple-element.119.refs_1_.x.rest_0_, bf16[256,384]{1,0:T(8,128)(2,1)} %get-tuple-element.122.o_own, ...), custom_call_target="tpu_custom_call" | custom-call | flops 1000000 | bytes 100000 | tf_op jit(solution)/shard_map/pallas_call | solution.py:635
  190.2 9.9 %shard_map.296 = (f32[256,768]{1,0:T(8,128)}, bf16[256,2688]{1,0:T(8,128)(2,1)}, bf16[256,2688]{1,0:T(8,128)(2,1)}, f32[16,768]{1,0:T(8,128)}, f32[1,3072]{1,0:T(1,128)}) custom-call(s32[1]{0:T(128)} %bitcast.core, f32[32,768]{1,0:T(8,128)} %get-tuple-element.113.vec, f32[256,768]{1,0:T(8,128)} %get-tuple-element.129.m_ref, ...), custom_call_target="tpu_custom_call" | custom-call | flops 1000000 | bytes 100000 | tf_op jit(solution)/shard_map/pallas_call | solution.py:716
  203.6 9.2 %shard_map.297.rest_3_ = bf16[4,4,2,9,24,384]{5,4,3,2,1,0:T(8,128)(2,1)} custom-call(s32[32]{0:T(128)S(1)} %select_n.207.table, bf16[256,4608]{1,0:T(8,128)(2,1)} %get-tuple-element.139.f0, bf16[256,4608]{1,0:T(8,128)(2,1)} %collective-permute-done.33.f1, bf16[256,2688]{1,0:T(8,128)(2,1)} %get-tuple-element.137.b0.rest_0_, ...), custom_call_target="tpu_custom_call" | custom-call | flops 1000000 | bytes 100000 | tf_op jit(solution)/shard_map/pallas_call | solution.py:991
  213.3 15.4 %shard_map.298 = (bf16[512,384]{1,0:T(8,128)(2,1)}, bf16[1024,384]{1,0:T(8,128)(2,1)}, bf16[1024,384]{1,0:T(8,128)(2,1)}, f32[256,768]{1,0:T(8,128)}, f32[256,76...) custom-call(bf16[512,384]{1,0:T(8,128)(2,1)} %get-tuple-element.132.q_ref, ...), custom_call_target="tpu_custom_call" | custom-call | flops 1000000 | bytes 100000 | tf_op jit(solution)/shard_map/pallas_call | solution.py:872
  235.6 5.6 %shard_map.299 = (bf16[4,2,12,24,384]{4,3,2,1,0:T(8,128)(2,1)}, bf16[4,2,12,24,384]{4,3,2,1,0:T(8,128)(2,1)}, bf16[4,2,12,24,384]{4,3,2,1,0:T(8,128)(2,1)}, bf16[4,2,12,24,384]{4,3,2,1,0:T(8,128)(2,1)}) custom-call(s32[32]{0:T(128)S(1)} %select_n.210.table, bf16[1024,768]{1,0:T(8,128)(2,1)} %get-tuple-element.143.a_ref, ...), custom_call_target="tpu_custom_call" | custom-call | flops 1000000 | bytes 100000 | tf_op jit(solution)/shard_map/pallas_call | solution.py:1025
  244.8 12.3 %shard_map.300 = (f32[256,768]{1,0:T(8,128)}, bf16[256,2688]{1,0:T(8,128)(2,1)}, bf16[256,2688]{1,0:T(8,128)(2,1)}, f32[16,768]{1,0:T(8,128)}, f32[1,3072]{1,0:T(1,128)}) custom-call(s32[1]{0:T(128)} %bitcast.core, f32[32,768]{1,0:T(8,128)} %get-tuple-element.113.vec, f32[256,768]{1,0:T(8,128)} %get-tuple-element.127.m_ref, ...), custom_call_target="tpu_custom_call" | custom-call | flops 1000000 | bytes 100000 | tf_op jit(solution)/shard_map/pallas_call | solution.py:716
  261.1 9.3 %shard_map.301 = (bf16[4,2,12,24,384]{4,3,2,1,0:T(8,128)(2,1)}, bf16[4,2,12,24,384]{4,3,2,1,0:T(8,128)(2,1)}, bf16[4,2,12,24,384]{4,3,2,1,0:T(8,128)(2,1)}, bf16[4,2,12,24,384]{4,3,2,1,0:T(8,128)(2,1)}) custom-call(s32[32]{0:T(128)S(1)} %select_n.210.table, ...), custom_call_target="tpu_custom_call", output_to_operand_aliasing={{0}: (5, {}), {1}: (6, {}), {2}: (7, {}), {3}: (8, {})} | custom-call | flops 1000000 | bytes 100000 | tf_op jit(solution)/shard_map/pallas_call | solution.py:991
  275.2 16.3 %shard_map.303 = (bf16[512,384]{1,0:T(8,128)(2,1)}, bf16[1024,384]{1,0:T(8,128)(2,1)}, bf16[1024,384]{1,0:T(8,128)(2,1)}, f32[256,768]{1,0:T(8,128)}, f32[256,76...) custom-call(bf16[512,384]{1,0:T(8,128)(2,1)} %get-tuple-element.149.q_ref, ...), custom_call_target="tpu_custom_call" | custom-call | flops 1000000 | bytes 100000 | tf_op jit(solution)/shard_map/pallas_call | solution.py:872
  291.9 5.8 %shard_map.305 = (bf16[4,2,4,24,384]{4,3,2,1,0:T(8,128)(2,1)}, bf16[4,2,4,24,384]{4,3,2,1,0:T(8,128)(2,1)}, bf16[4,2,4,24,384]{4,3,2,1,0:T(8,128)(2,1)}, bf16[4,2,4,24,384]{4,3,2,1,0:T(8,128)(2,1)}) custom-call(s32[32]{0:T(128)S(1)} %select_n.210.table, s32[1]{0:T(128)} %bitcast.core, bf16[1024,768]{1,0:T(8,128)(2,1)} %get-tuple-element.167.a_ref, ...), custom_call_target="tpu_custom_call" | custom-call | flops 1000000 | bytes 100000 | tf_op jit(solution)/shard_map/pallas_call | solution.py:944
  301.5 12.9 %collective-permute-done.41.refs_2_ = bf16[4,2,12,24,384]{4,3,2,1,0:T(8,128)(2,1)S(1)} collective-permute-done((bf16[4,2,12,24,384]{4,3,2,1,0:T(8,128)(2,1)}, bf16[4,2,12,24,384]{4,3,2,1,0:T(8,128)(2,1)S(1)}, u32[]{:S(2)}, u32[]{:S(2)}) %collective-permute-start.41) | collective-permute-done | bytes 1769504 | tf_op jit(solution)/shard_map/ppermute | solution.py:48
  321.0 6.3 %collective-permute-done.44.refs_6_ = bf16[4,2,4,24,384]{4,3,2,1,0:T(8,128)(2,1)} collective-permute-done((bf16[4,2,4,24,384]{4,3,2,1,0:T(8,128)(2,1)}, bf16[4,2,4,24,384]{4,3,2,1,0:T(8,128)(2,1)}, u32[]{:S(2)}, u32[]{:S(2)}) %collective-permute-start.44) | collective-permute-done | bytes 589856 | tf_op jit(solution)/shard_map/ppermute | solution.py:48
  344.5 6.7 %collective-permute-done.47.refs_2_ = bf16[2,16,24,384]{3,2,1,0:T(8,128)(2,1)S(1)} collective-permute-done((bf16[2,16,24,384]{3,2,1,0:T(8,128)(2,1)}, bf16[2,16,24,384]{3,2,1,0:T(8,128)(2,1)S(1)}, u32[]{:S(2)}, u32[]{:S(2)}) %collective-permute-start.47) | collective-permute-done | bytes 589856 | tf_op jit(solution)/shard_map/ppermute | solution.py:48
  364.8 6.0 %collective-permute-done.50 = bf16[16,24,384]{2,1,0:T(8,128)(2,1)S(1)} collective-permute-done((bf16[16,24,384]{2,1,0:T(8,128)(2,1)S(1)}, bf16[16,24,384]{2,1,0:T(8,128)(2,1)S(1)}, u32[]{:S(2)}, u32[]{:S(2)}) %collective-permute-start.50) | collective-permute-done | bytes 294944 | tf_op jit(solution)/shard_map/ppermute | solution.py:48
  370.9 6.4 %collective-permute-start.51 = (bf16[16,24,384]{2,1,0:T(8,128)(2,1)S(1)}, bf16[16,24,384]{2,1,0:T(8,128)(2,1)S(1)}, u32[]{:S(2)}, u32[]{:S(2)}) collective-permute-start(bf16[16,24,384]{2,1,0:T(8,128)(2,1)S(1)} %add_convert_fusion.2.own0), channel_id=1, source_target_pairs={{0,32},{1,33},{2,34},{3,35},{4,36},{5,37},{6,38},{7,39},{8,40},{9,... | collective-permute-start | bytes 884744 | tf_op jit(solution)/shard_map/ppermute | solution.py:48
  (217 shorter events, 147.1 us)
Async XLA Ops:
  7.2 107.0 %all-gather.2.cloned.1.call-start = ((), (), s32[]{:S(2)}) async-start(), calls=%async_computation.2 | async-start | bytes 2211840 | tf_op jit(solution)/shard_map/all_gather | solution.py:1048
  27.1 23.1 %collective-permute-start.10 = (bf16[4,2,4,24,384]{4,3,2,1,0:T(8,128)(2,1)}, bf16[4,2,4,24,384]{4,3,2,1,0:T(8,128)(2,1)S(1)}, u32[]{:S(2)}, u32[]{:S(2)}) collective-permute-start(bf16[4,2,4,24,384]{4,3,2,1,0:T(8,128)(2,1)} %shard_map.274.refs_1_.refs_0_), channel_id=1, source_target_pairs={{0,24},{1,25},{2,26},{3,27},{4,28},{5,29},{6,30},{7,31},{8,0},{9,1... | collective-permute-start | bytes 1769480 | tf_op jit(solution)/shard_map/ppermute | solution.py:48
  31.1 19.3 %collective-permute-start.8 = (bf16[4,2,4,24,384]{4,3,2,1,0:T(8,128)(2,1)}, bf16[4,2,4,24,384]{4,3,2,1,0:T(8,128)(2,1)S(1)}, u32[]{:S(2)}, u32[]{:S(2)}) collective-permute-start(bf16[4,2,4,24,384]{4,3,2,1,0:T(8,128)(2,1)} %shard_map.274.refs_1_.refs_0_), channel_id=1, source_target_pairs={{0,8},{1,9},{2,10},{3,11},{4,12},{5,13},{6,14},{7,15},{8,16},{9,17... | collective-permute-start | bytes 1769480 | tf_op jit(solution)/shard_map/ppermute | solution.py:48
  31.2 19.2 %collective-permute-start.9 = (bf16[4,2,4,24,384]{4,3,2,1,0:T(8,128)(2,1)}, bf16[4,2,4,24,384]{4,3,2,1,0:T(8,128)(2,1)S(1)}, u32[]{:S(2)}, u32[]{:S(2)}) collective-permute-start(bf16[4,2,4,24,384]{4,3,2,1,0:T(8,128)(2,1)} %shard_map.274.refs_1_.refs_0_), channel_id=1, source_target_pairs={{0,16},{1,17},{2,18},{3,19},{4,20},{5,21},{6,22},{7,23},{8,24},{9,... | collective-permute-start | bytes 1769480 | tf_op jit(solution)/shard_map/ppermute | solution.py:48
  43.6 18.8 %collective-permute-start = (bf16[256,768]{1,0:T(8,128)(2,1)}, bf16[256,768]{1,0:T(8,128)(2,1)}, u32[]{:S(2)}, u32[]{:S(2)}) collective-permute-start(bf16[256,768]{1,0:T(8,128)(2,1)} %bitcast.1.x0.x.rest_0_), channel_id=1, source_target_pairs={{0,32},{1,33},{2,34},{3,35},{4,36},{5,37},{6,38},{7,39},{8,40},{9,... | collective-permute-start | bytes 1179656 | tf_op jit(solution)/shard_map/ppermute | solution.py:48
  52.1 22.2 %collective-permute-start.13 = (bf16[2,9,24,384]{3,2,1,0:T(8,128)(2,1)}, bf16[2,9,24,384]{3,2,1,0:T(8,128)(2,1)}, u32[]{:S(2)}, u32[]{:S(2)}) collective-permute-start(bf16[2,9,24,384]{3,2,1,0:T(8,128)(2,1)} %shard_map.275.refs_4_), channel_id=1, source_target_pairs={{0,1},{1,2},{2,3},{3,0},{4,5},{5,6},{6,7},{7,4},{8,9},{9,10},{10,1... | collective-permute-start | bytes 995336 | tf_op jit(solution)/shard_map/ppermute | solution.py:48
  53.2 21.1 %collective-permute-start.14 = (bf16[2,9,24,384]{3,2,1,0:T(8,128)(2,1)}, bf16[2,9,24,384]{3,2,1,0:T(8,128)(2,1)}, u32[]{:S(2)}, u32[]{:S(2)}) collective-permute-start(bf16[2,9,24,384]{3,2,1,0:T(8,128)(2,1)} %shard_map.275.refs_4_), channel_id=1, source_target_pairs={{0,2},{1,3},{2,0},{3,1},{4,6},{5,7},{6,4},{7,5},{8,10},{9,11},{10,... | collective-permute-start | bytes 995336 | tf_op jit(solution)/shard_map/ppermute | solution.py:48
  54.5 19.9 %collective-permute-start.15 = (bf16[2,9,24,384]{3,2,1,0:T(8,128)(2,1)}, bf16[2,9,24,384]{3,2,1,0:T(8,128)(2,1)}, u32[]{:S(2)}, u32[]{:S(2)}) collective-permute-start(bf16[2,9,24,384]{3,2,1,0:T(8,128)(2,1)} %shard_map.275.refs_4_), channel_id=1, source_target_pairs={{0,3},{1,0},{2,1},{3,2},{4,7},{5,4},{6,5},{7,6},{8,11},{9,8},{10,9... | collective-permute-start | bytes 995336 | tf_op jit(solution)/shard_map/ppermute | solution.py:48
  56.7 201.4 %reduce-scatter.3.cloned.1.call-start = ((), (), s32[]{:S(2)}) async-start(), calls=%async_computation.3 | async-start | bytes 6635520 | tf_op jit(solution)/shard_map/reduce_scatter | solution.py:1042
  81.3 30.4 %collective-permute-start.16 = (bf16[4,2,9,24,384]{4,3,2,1,0:T(8,128)(2,1)}, bf16[4,2,9,24,384]{4,3,2,1,0:T(8,128)(2,1)S(1)}, u32[]{:S(2)}, u32[]{:S(2)}) collective-permute-start(bf16[4,2,9,24,384]{4,3,2,1,0:T(8,128)(2,1)} %pad_maximum_fusion.refs_0_), channel_id=1, source_target_pairs={{0,8},{1,9},{2,10},{3,11},{4,12},{5,13},{6,14},{7,15},{8,16},{9,17... | collective-permute-start | bytes 3981320 | tf_op jit(solution)/shard_map/ppermute | solution.py:48
  82.8 32.5 %collective-permute-start.19 = (bf16[4,2,9,24,384]{4,3,2,1,0:T(8,128)(2,1)}, bf16[4,2,9,24,384]{4,3,2,1,0:T(8,128)(2,1)}, u32[]{:S(2)}, u32[]{:S(2)}) collective-permute-start(bf16[4,2,9,24,384]{4,3,2,1,0:T(8,128)(2,1)} %pad_maximum_fusion.refs_0_), channel_id=1, source_target_pairs={{0,32},{1,33},{2,34},{3,35},{4,36},{5,37},{6,38},{7,39},{8,40},{9,... | collective-permute-start | bytes 3981320 | tf_op jit(solution)/shard_map/ppermute | solution.py:48
  95.3 21.5 %collective-permute-start.22 = (bf16[4,2,9,24,384]{4,3,2,1,0:T(8,128)(2,1)}, bf16[4,2,9,24,384]{4,3,2,1,0:T(8,128)(2,1)}, u32[]{:S(2)}, u32[]{:S(2)}) collective-permute-start(bf16[4,2,9,24,384]{4,3,2,1,0:T(8,128)(2,1)} %shard_map.285.refs_3_), channel_id=1, source_target_pairs={{0,32},{1,33},{2,34},{3,35},{4,36},{5,37},{6,38},{7,39},{8,40},{9,... | collective-permute-start | bytes 3981320 | tf_op jit(solution)/shard_map/ppermute | solution.py:48
  98.6 19.5 %collective-permute-start.21 = (bf16[4,2,9,24,384]{4,3,2,1,0:T(8,128)(2,1)}, bf16[4,2,9,24,384]{4,3,2,1,0:T(8,128)(2,1)}, u32[]{:S(2)}, u32[]{:S(2)}) collective-permute-start(bf16[4,2,9,24,384]{4,3,2,1,0:T(8,128)(2,1)} %shard_map.284.refs_2_), channel_id=1, source_target_pairs={{0,32},{1,33},{2,34},{3,35},{4,36},{5,37},{6,38},{7,39},{8,40},{9,... | collective-permute-start | bytes 3981320 | tf_op jit(solution)/shard_map/ppermute | solution.py:48
  114.2 40.9 %collective-permute-start.28 = (bf16[4,2,12,24,384]{4,3,2,1,0:T(8,128)(2,1)}, bf16[4,2,12,24,384]{4,3,2,1,0:T(8,128)(2,1)}, u32[]{:S(2)}, u32[]{:S(2)}) collective-permute-start(bf16[4,2,12,24,384]{4,3,2,1,0:T(8,128)(2,1)} %shard_map.287.refs_9_.refs_0_), channel_id=1, source_target_pairs={{0,24},{1,25},{2,26},{3,27},{4,28},{5,29},{6,30},{7,31},{8,0},{9,1... | collective-permute-start | bytes 5308424 | tf_op jit(solution)/shard_map/ppermute | solution.py:48
  115.3 39.8 %collective-permute-start.27 = (bf16[4,2,12,24,384]{4,3,2,1,0:T(8,128)(2,1)}, bf16[4,2,12,24,384]{4,3,2,1,0:T(8,128)(2,1)}, u32[]{:S(2)}, u32[]{:S(2)}) collective-permute-start(bf16[4,2,12,24,384]{4,3,2,1,0:T(8,128)(2,1)} %shard_map.287.refs_9_.refs_0_), channel_id=1, source_target_pairs={{0,16},{1,17},{2,18},{3,19},{4,20},{5,21},{6,22},{7,23},{8,24},{9,... | collective-permute-start | bytes 5308424 | tf_op jit(solution)/shard_map/ppermute | solution.py:48
  116.8 41.0 %collective-permute-start.26 = (bf16[4,2,12,24,384]{4,3,2,1,0:T(8,128)(2,1)}, bf16[4,2,12,24,384]{4,3,2,1,0:T(8,128)(2,1)}, u32[]{:S(2)}, u32[]{:S(2)}) collective-permute-start(bf16[4,2,12,24,384]{4,3,2,1,0:T(8,128)(2,1)} %shard_map.287.refs_9_.refs_0_), channel_id=1, source_target_pairs={{0,8},{1,9},{2,10},{3,11},{4,12},{5,13},{6,14},{7,15},{8,16},{9,17... | collective-permute-start | bytes 5308424 | tf_op jit(solution)/shard_map/ppermute | solution.py:48
  212.8 105.5 %reduce-scatter.5.cloned.1.call-start = ((), (), s32[]{:S(2)}) async-start(), calls=%async_computation.4 | async-start | bytes 1658880 | tf_op jit(solution)/shard_map/reduce_scatter | solution.py:1042
  228.9 29.2 %collective-permute-start.37 = (bf16[256,4608]{1,0:T(8,128)(2,1)}, bf16[256,4608]{1,0:T(8,128)(2,1)}, u32[]{:S(2)}, u32[]{:S(2)}) collective-permute-start(bf16[256,4608]{1,0:T(8,128)(2,1)} %get-tuple-element.156.f0), channel_id=1, source_target_pairs={{0,32},{1,33},{2,34},{3,35},{4,36},{5,37},{6,38},{7,39},{8,40},{9,... | collective-permute-start | bytes 7077896 | tf_op jit(solution)/shard_map/ppermute | solution.py:48
  270.4 27.3 %collective-permute-start.40 = (bf16[4,2,12,24,384]{4,3,2,1,0:T(8,128)(2,1)}, bf16[4,2,12,24,384]{4,3,2,1,0:T(8,128)(2,1)S(1)}, u32[]{:S(2)}, u32[]{:S(2)}) collective-permute-start(bf16[4,2,12,24,384]{4,3,2,1,0:T(8,128)(2,1)} %get-tuple-element.164), channel_id=1, source_target_pairs={{0,8},{1,9},{2,10},{3,11},{4,12},{5,13},{6,14},{7,15},{8,16},{9,17... | collective-permute-start | bytes 5308424 | tf_op jit(solution)/shard_map/ppermute | solution.py:48
  271.0 43.4 %collective-permute-start.41 = (bf16[4,2,12,24,384]{4,3,2,1,0:T(8,128)(2,1)}, bf16[4,2,12,24,384]{4,3,2,1,0:T(8,128)(2,1)S(1)}, u32[]{:S(2)}, u32[]{:S(2)}) collective-permute-start(bf16[4,2,12,24,384]{4,3,2,1,0:T(8,128)(2,1)} %get-tuple-element.165), channel_id=1, source_target_pairs={{0,16},{1,17},{2,18},{3,19},{4,20},{5,21},{6,22},{7,23},{8,24},{9,... | collective-permute-start | bytes 5308424 | tf_op jit(solution)/shard_map/ppermute | solution.py:48
  273.1 47.0 %collective-permute-start.42 = (bf16[4,2,12,24,384]{4,3,2,1,0:T(8,128)(2,1)}, bf16[4,2,12,24,384]{4,3,2,1,0:T(8,128)(2,1)}, u32[]{:S(2)}, u32[]{:S(2)}) collective-permute-start(bf16[4,2,12,24,384]{4,3,2,1,0:T(8,128)(2,1)} %get-tuple-element.166), channel_id=1, source_target_pairs={{0,24},{1,25},{2,26},{3,27},{4,28},{5,29},{6,30},{7,31},{8,0},{9,1... | collective-permute-start | bytes 5308424 | tf_op jit(solution)/shard_map/ppermute | solution.py:48
  297.7 23.3 %collective-permute-start.43 = (bf16[4,2,4,24,384]{4,3,2,1,0:T(8,128)(2,1)}, bf16[4,2,4,24,384]{4,3,2,1,0:T(8,128)(2,1)}, u32[]{:S(2)}, u32[]{:S(2)}) collective-permute-start(bf16[4,2,4,24,384]{4,3,2,1,0:T(8,128)(2,1)} %get-tuple-element.179), channel_id=1, source_target_pairs={{0,8},{1,9},{2,10},{3,11},{4,12},{5,13},{6,14},{7,15},{8,16},{9,17... | collective-permute-start | bytes 1769480 | tf_op jit(solution)/shard_map/ppermute | solution.py:48
  297.7 29.6 %collective-permute-start.44 = (bf16[4,2,4,24,384]{4,3,2,1,0:T(8,128)(2,1)}, bf16[4,2,4,24,384]{4,3,2,1,0:T(8,128)(2,1)}, u32[]{:S(2)}, u32[]{:S(2)}) collective-permute-start(bf16[4,2,4,24,384]{4,3,2,1,0:T(8,128)(2,1)} %get-tuple-element.180), channel_id=1, source_target_pairs={{0,16},{1,17},{2,18},{3,19},{4,20},{5,21},{6,22},{7,23},{8,24},{9,... | collective-permute-start | bytes 1769480 | tf_op jit(solution)/shard_map/ppermute | solution.py:48
  300.0 27.7 %collective-permute-start.45 = (bf16[4,2,4,24,384]{4,3,2,1,0:T(8,128)(2,1)}, bf16[4,2,4,24,384]{4,3,2,1,0:T(8,128)(2,1)}, u32[]{:S(2)}, u32[]{:S(2)}) collective-permute-start(bf16[4,2,4,24,384]{4,3,2,1,0:T(8,128)(2,1)} %get-tuple-element.181), channel_id=1, source_target_pairs={{0,24},{1,25},{2,26},{3,27},{4,28},{5,29},{6,30},{7,31},{8,0},{9,1... | collective-permute-start | bytes 1769480 | tf_op jit(solution)/shard_map/ppermute | solution.py:48
  (59 other events, 433.5 us)
Sparse Core Ops, SparseCore 0:
  56.8 22.4 all-gather.1
  212.9 33.4 reduce-scatter.2
  258.3 21.6 reduce-scatter.4
